TPU v7x, 128 devices: a whole 4x4x4 slice. The times are simulated.
128 devices in a mesh: lon: 16 (over y_hi, z, core), lat: 8 (over y_lo, x).
Axes of the slice: x: 4, y: 4 (y_hi: 2, y_lo: 2; y = y_hi * 2 + y_lo), z: 4, core: 2. Of those that a mesh axis runs over, the one named last changes fastest.
Arguments:
- tracers: float32 [2, 10, 512, 2048], P(None, None, 'lat', 'lon'), may hold values from -6 to 6
- velocity: float32 [2, 10, 512, 2048], P(None, None, 'lat', 'lon'), may hold values from -6 to 6
- active_levels: int32 [512, 2048], P('lat', 'lon'), may hold values from 0 to 10, as said below
- diffusivity: float32 [512, 2048], P('lat', 'lon'), may hold values from 0.02 to 0.2
- viscosity: float32 [512, 2048], P('lat', 'lon'), may hold values from 0.002 to 0.012
- ocean_depth: float32 [512, 2048], P('lat', 'lon'), may hold values from 0.5 to 1.5
- wind_forcing: float32 [2, 512, 2048], P(None, 'lat', 'lon'), may hold values from -5 to 5
Outputs:
- tracers_out: float32 [2, 10, 512, 2048], P(None, None, 'lat', 'lon')
- velocity_out: float32 [2, 10, 512, 2048], P(None, None, 'lat', 'lon')
- surface: float32 [512, 2048], P('lat', 'lon')
Inputs may be any that keep to these rules, and one draw needn't show every extreme that they name: `active_levels`: 0 marks land, which covers whole aligned blocks of 8 x 8 cells; every other cell has 1 to 10 wet levels.
All inputs are finite; a program needn't handle non-finite values.
Results may differ from a plain program's by a relative error of at most 0.0003.
Values sent between devices are 32-bit elements; how exact they have to be, the bound alone decides.
No kernel may reach another device: no remote copies, remote signals or barrier semaphores. Data moves between devices by JAX's collectives and lax.ppermute only.
A program may use at most 128 MiB of HBM per device.

v0:
```python
import math

import jax
import jax.numpy as jnp
from jax import lax
from jax.sharding import PartitionSpec as P

SUBCYCLES = 8
SOLVE_ITERS = 4


edge_offsets = ((0, 1), (0, -1), (1, 0), (-1, 0))
corner_offsets = ((1, 1), (1, -1), (-1, 1), (-1, -1))
flow_step = 0.3
slope_step = 0.3
floor_diag = 0.05


def extended(block, sides, width):
    for axis, dim in sides:
        count = lax.axis_size(axis)
        forward = [(i, i + 1) for i in range(count - 1)]
        forward.append((count - 1, 0))
        backward = [(target, source) for source, target in forward]
        low = lax.ppermute(
            lax.slice_in_dim(block, block.shape[dim] - width, None, axis=dim), axis, forward
        )
        high = lax.ppermute(lax.slice_in_dim(block, 0, width, axis=dim), axis, backward)
        block = jnp.concatenate([low, block, high], axis=dim)
    return block


def from_partner(array, axis, apart):
    return lax.ppermute(array, axis, [(i, i ^ 1 << apart) for i in range(lax.axis_size(axis))])


def parity_of(values):
    return jnp.array(values, jnp.float32).reshape(-1, 1, 1)


def window(field, row_off, col_off):
    row_count = field.shape[-2] - 2
    col_count = field.shape[-1] - 2
    inner = lax.slice_in_dim(field, 1 + row_off, 1 + row_off + row_count, axis=field.ndim - 2)
    return lax.slice_in_dim(inner, 1 + col_off, 1 + col_off + col_count, axis=field.ndim - 1)


def masked_laplacian(field, coefficient, wet_mask):
    centre = window(field, 0, 0)
    mask_centre = window(wet_mask, 0, 0)
    summed = None
    for row_off, col_off in edge_offsets:
        face_weight = mask_centre * window(wet_mask, row_off, col_off)
        if coefficient is not None:
            face_weight = (
                0.5
                * (window(coefficient, 0, 0) + window(coefficient, row_off, col_off))
                * face_weight
            )
        flux_term = face_weight * (window(field, row_off, col_off) - centre)
        summed = flux_term if summed is None else summed + flux_term
    return summed


def clinic_extend(stacked, margin, parity):
    padded = extended(stacked, (("lon", 2), ("lat", 1)), margin)
    rim_rows = padded[:, -2 * margin : -margin, :]
    partner = rim_rows
    for bit_index in range(lax.axis_size("lon").bit_length() - 1):
        partner = from_partner(partner, "lon", bit_index)
    folded = jnp.flip(partner, (1, 2)) * parity
    lat_index = lax.axis_index("lat")
    south_rows = jnp.where(lat_index == 0, jnp.zeros_like(padded[:, :margin]), padded[:, :margin])
    north_rows = jnp.where(lat_index == lax.axis_size("lat") - 1, folded, padded[:, -margin:])
    return jnp.concatenate([south_rows, padded[:, margin:-margin], north_rows], axis=1)


def extend(stacked, margin, parity):
    return clinic_extend(stacked, margin, parity)


def squares(residual):
    return lax.psum(jnp.sum(residual * residual), ("lon", "lat"))


def nine_weights(statics):
    depth_pad = statics[0]
    ocean_pad = statics[1]
    depth_centre = window(depth_pad, 0, 0)
    ocean_centre = window(ocean_pad, 0, 0)
    weights = []
    for offsets, scale in ((edge_offsets, 1.0), (corner_offsets, 0.5)):
        for row_off, col_off in offsets:
            weights.append(
                scale
                * 0.5
                * (depth_centre + window(depth_pad, row_off, col_off))
                * ocean_centre
                * window(ocean_pad, row_off, col_off)
            )
    diagonal = floor_diag * ocean_centre + (1.0 - ocean_centre)
    return (weights, diagonal)


def operate_nine(direction_pad, weights, diagonal):
    centre = window(direction_pad, 0, 0)
    summed = diagonal * centre
    for offset, weight in zip(edge_offsets + corner_offsets, weights):
        summed = summed + weight * (centre - window(direction_pad, offset[0], offset[1]))
    return summed


def barotropic(fields):
    start_east, start_north, ocean_depth, ocean_mask = (fields[0], fields[1], fields[2], fields[3])
    height = jnp.zeros_like(start_east)
    east_flow, north_flow = (start_east, start_north)
    statics = extend(jnp.stack([ocean_depth, ocean_mask]), 1, parity_of([1.0, 1.0]))
    depth_pad = statics[0]
    for cycle_index in range(SUBCYCLES):
        moved = extend(jnp.stack([east_flow, north_flow]), 1, parity_of([-1.0, -1.0]))
        flux_east = depth_pad * moved[0]
        flux_north = depth_pad * moved[1]
        divergence = 0.5 * (
            window(flux_east, 0, 1)
            - window(flux_east, 0, -1)
            + (window(flux_north, 1, 0) - window(flux_north, -1, 0))
        )
        height = height - flow_step * ocean_mask * divergence
        height_pad = extend(height[None], 1, parity_of([1.0]))[0]
        east_flow = east_flow - slope_step * ocean_mask * (
            0.5 * (window(height_pad, 0, 1) - window(height_pad, 0, -1))
        )
        north_flow = north_flow - slope_step * ocean_mask * (
            0.5 * (window(height_pad, 1, 0) - window(height_pad, -1, 0))
        )
    weights, diagonal = nine_weights(statics)
    surface = jnp.zeros_like(height)
    residual = height
    direction = height
    old_norm = squares(residual)
    for iteration in range(SOLVE_ITERS):
        direction_pad = extend(direction[None], 1, parity_of([1.0]))[0]
        image = operate_nine(direction_pad, weights, diagonal)
        step_size = old_norm / lax.psum(jnp.sum(direction * image), ("lon", "lat"))
        surface = surface + step_size * direction
        residual = residual - step_size * image
        new_norm = squares(residual)
        direction = residual + new_norm / old_norm * direction
        old_norm = new_norm
    surface_pad = extend(surface[None], 1, parity_of([1.0]))[0]
    east_final = east_flow - slope_step * ocean_mask * (
        0.5 * (window(surface_pad, 0, 1) - window(surface_pad, 0, -1))
    )
    north_final = north_flow - slope_step * ocean_mask * (
        0.5 * (window(surface_pad, 1, 0) - window(surface_pad, -1, 0))
    )
    return jnp.stack([east_final, north_final, surface])


def per_device(tracers, velocity, active_levels, diffusivity, viscosity, ocean_depth, wind_forcing):
    level_total = tracers.shape[1]
    row_count = tracers.shape[2]
    col_count = tracers.shape[3]
    levels_float = active_levels.astype(jnp.float32)
    stacked = jnp.concatenate(
        [
            tracers.reshape(2 * level_total, row_count, col_count),
            velocity.reshape(2 * level_total, row_count, col_count),
            jnp.stack([diffusivity, viscosity, levels_float]),
        ],
        axis=0,
    )
    parity = jnp.concatenate(
        [
            jnp.ones((2 * level_total,), jnp.float32),
            -jnp.ones((2 * level_total,), jnp.float32),
            jnp.ones((3,), jnp.float32),
        ]
    ).reshape(-1, 1, 1)
    padded = clinic_extend(stacked, 2, parity)
    pad_rows = row_count + 4
    pad_cols = col_count + 4
    tracer_pad = padded[: 2 * level_total].reshape(2, level_total, pad_rows, pad_cols)
    velocity_pad = padded[2 * level_total : 4 * level_total].reshape(
        2, level_total, pad_rows, pad_cols
    )
    diffusion_pad = padded[4 * level_total]
    viscous_pad = padded[4 * level_total + 1]
    levels_pad = padded[4 * level_total + 2]
    level_ids = jnp.arange(level_total, dtype=jnp.float32)[:, None, None]
    wet_pad = (level_ids < levels_pad).astype(jnp.float32)
    tracer_lap = window(masked_laplacian(tracer_pad, diffusion_pad, wet_pad), 0, 0)
    tracers_out = tracers + tracer_lap
    first_pass = masked_laplacian(velocity_pad, None, wet_pad)
    second_pass = masked_laplacian(first_pass, window(viscous_pad, 0, 0), window(wet_pad, 0, 0))
    wet = wet_pad[:, 2:-2, 2:-2]
    row_ids = (lax.axis_index("lat") * row_count + jnp.arange(row_count, dtype=jnp.int32)).astype(
        jnp.float32
    )[:, None]
    coriolis = 0.25 * jnp.sin(
        math.pi * ((row_ids + 0.5) / (row_count * lax.axis_size("lat")) - 0.5)
    )
    rotated = jnp.stack([velocity[1], -velocity[0]])
    star = wet * (velocity - second_pass + coriolis * rotated)
    column_mean = jnp.sum(star, axis=1) / jnp.maximum(levels_float, 1.0)
    ocean_mask = (active_levels > 0).astype(jnp.float32)
    start = column_mean + wind_forcing * ocean_mask
    fields = jnp.stack([start[0], start[1], ocean_depth, ocean_mask])
    result = barotropic(fields)
    velocity_out = star + wet * (result[:2] - column_mean)[:, None]
    return (tracers_out, velocity_out, result[2])


def solution(mesh):
    placed = (
        P(None, None, "lat", "lon"),
        P(None, None, "lat", "lon"),
        P("lat", "lon"),
        P("lat", "lon"),
        P("lat", "lon"),
        P("lat", "lon"),
        P(None, "lat", "lon"),
    )
    return jax.shard_map(
        per_device,
        mesh=mesh,
        in_specs=placed,
        out_specs=(P(None, None, "lat", "lon"), P(None, None, "lat", "lon"), P("lat", "lon")),
        check_vma=False,
    )
```

profile of v0, /device:TPU:1, one launch (start us, length us, event | category | flops | bytes accessed | tf_op | source)
XLA Modules:
  0.0 1058.0 jit_solution(17641183671994034047)
XLA Ops:
  12.1 4.6 collective-permute-start.1
  25.2 6.3 collective-permute-start.3
  89.9 5.8 collective-permute-start.24
  105.0 5.3 collective-permute-start.28
  156.1 5.5 collective-permute-start.44
  207.4 5.3 collective-permute-start.60
  258.4 5.3 collective-permute-start.76
  309.9 5.3 collective-permute-start.92
  361.0 5.3 collective-permute-start.108
  412.3 5.3 collective-permute-start.124
  455.8 4.7 collective-permute-start.138
  467.2 5.0 collective-permute-start.140
  480.3 65.6 %all-reduce = (f32[]{:T(128)}, f32[]{:T(128)}) all-reduce(f32[]{:T(128)} %get-tuple-element.7, f32[]{:T(128)} %get-tuple-element.6), channel_id=1, replica_groups=mesh['lon'=16,'lat'=8] {'lon','lat'}, use_global_device_ids=true, to_apply=%region_2.3 | all-reduce | flops 2 | bytes 16 | tf_op jit(solution)/shard_map/psum | solution.py:83
  547.8 63.2 %psum.58 = f32[]{:T(128)} all-reduce(f32[]{:T(128)} %multiply_reduce_fusion.4), channel_id=1, replica_groups=mesh['lon'=16,'lat'=8] {'lon','lat'}, use_global_device_ids=true, to_apply=%region_6.7 | all-reduce | flops 1 | bytes 8 | tf_op jit(solution)/shard_map/psum | solution.py:83
  624.6 5.4 collective-permute-start.148
  638.4 65.6 %psum.59 = f32[]{:T(128)} all-reduce(f32[]{:T(128)} %get-tuple-element.14), channel_id=1, replica_groups=mesh['lon'=16,'lat'=8] {'lon','lat'}, use_global_device_ids=true, to_apply=%region_8.9 | all-reduce | flops 1 | bytes 8 | tf_op jit(solution)/shard_map/psum | solution.py:144
  707.3 62.6 %psum.60 = f32[]{:T(128)} all-reduce(f32[]{:T(128)} %get-tuple-element.12), channel_id=1, replica_groups=mesh['lon'=16,'lat'=8] {'lon','lat'}, use_global_device_ids=true, to_apply=%region_10.11 | all-reduce | flops 1 | bytes 8 | tf_op jit(solution)/shard_map/psum | solution.py:83
  784.2 5.0 collective-permute-start.156
  797.7 66.3 %psum.61 = f32[]{:T(128)} all-reduce(f32[]{:T(128)} %get-tuple-element.10), channel_id=1, replica_groups=mesh['lon'=16,'lat'=8] {'lon','lat'}, use_global_device_ids=true, to_apply=%region_12.13 | all-reduce | flops 1 | bytes 8 | tf_op jit(solution)/shard_map/psum | solution.py:144
  866.7 64.0 %psum.62 = f32[]{:T(128)} all-reduce(f32[]{:T(128)} %multiply_reduce_fusion), channel_id=1, replica_groups=mesh['lon'=16,'lat'=8] {'lon','lat'}, use_global_device_ids=true, to_apply=%region_14.15 | all-reduce | flops 1 | bytes 8 | tf_op jit(solution)/shard_map/psum | solution.py:83
  936.4 4.7 collective-permute-start.162
  945.5 4.8 collective-permute-start.164
  958.2 65.6 %psum.63 = f32[]{:T(128)} all-reduce(f32[]{:T(128)} %fusion.111), channel_id=1, replica_groups=mesh['lon'=16,'lat'=8] {'lon','lat'}, use_global_device_ids=true, to_apply=%region_16.17 | all-reduce | flops 1 | bytes 8 | tf_op jit(solution)/shard_map/psum | solution.py:144
  1029.2 5.4 collective-permute-start.170
  (668 shorter events, 504.7 us)
Async XLA Ops:
  3.7 29.2 %collective-permute-start.8 = (f32[2,64,1]{2,1,0:T(8,128)}, f32[2,64,1]{2,1,0:T(8,128)S(1)}, u32[]{:S(2)}, u32[]{:S(2)}) collective-permute-start(f32[2,64,1]{2,1,0:T(8,128)} %get-tuple-element.177), channel_id=1, source_target_pairs={{0,8},{8,16},{16,24},{24,32},{32,40},{40,48},{48,56},{56,64},{64,7... | collective-permute-start | bytes 1544 | tf_op jit(solution)/shard_map/ppermute | solution.py:25
  6.7 26.2 %collective-permute-start.9 = (f32[2,64,1]{2,1,0:T(8,128)}, f32[2,64,1]{2,1,0:T(8,128)}, u32[]{:S(2)}, u32[]{:S(2)}) collective-permute-start(f32[2,64,1]{2,1,0:T(8,128)} %get-tuple-element.178), channel_id=1, source_target_pairs={{8,0},{16,8},{24,16},{32,24},{40,32},{48,40},{56,48},{64,56},{72,6... | collective-permute-start | bytes 1544 | tf_op jit(solution)/shard_map/ppermute | solution.py:28
  37.6 25.5 %collective-permute-start.12 = (f32[2,1,130]{2,1,0:T(1,128)}, f32[2,1,130]{2,1,0:T(1,128)}, u32[]{:S(2)}, u32[]{:S(2)}) collective-permute-start(f32[2,1,130]{2,1,0:T(1,128)} %collective-permute-done.11), channel_id=1, source_target_pairs={{0,16},{8,24},{16,0},{24,8},{32,48},{40,56},{48,32},{56,40},{64,80... | collective-permute-start | bytes 3128 | tf_op jit(solution)/shard_map/ppermute | solution.py:34
  101.5 11.3 %collective-permute-start.31 = (f32[1,1,130]{2,1,0:T(1,128)S(1)}, f32[1,1,130]{2,1,0:T(1,128)S(1)}, u32[]{:S(2)}, u32[]{:S(2)}) collective-permute-start(f32[1,1,130]{2,1,0:T(1,128)S(1)} %get-tuple-element.176), channel_id=1, source_target_pairs={{0,1},{1,2},{2,3},{3,4},{4,5},{5,6},{6,7},{7,0},{8,9},{9,10},{10,1... | collective-permute-start | bytes 1568 | tf_op jit(solution)/shard_map/ppermute | solution.py:25
  101.5 13.9 %collective-permute-start.30 = (f32[1,1,130]{2,1,0:T(1,128)S(1)}, f32[1,1,130]{2,1,0:T(1,128)S(1)}, u32[]{:S(2)}, u32[]{:S(2)}) collective-permute-start(f32[1,1,130]{2,1,0:T(1,128)S(1)} %get-tuple-element.175), channel_id=1, source_target_pairs={{1,0},{2,1},{3,2},{4,3},{5,4},{6,5},{7,6},{0,7},{9,8},{10,9},{11,1... | collective-permute-start | bytes 1568 | tf_op jit(solution)/shard_map/ppermute | solution.py:28
  152.5 11.5 %collective-permute-start.47 = (f32[1,1,130]{2,1,0:T(1,128)S(1)}, f32[1,1,130]{2,1,0:T(1,128)S(1)}, u32[]{:S(2)}, u32[]{:S(2)}) collective-permute-start(f32[1,1,130]{2,1,0:T(1,128)S(1)} %get-tuple-element.172), channel_id=1, source_target_pairs={{0,1},{1,2},{2,3},{3,4},{4,5},{5,6},{6,7},{7,0},{8,9},{9,10},{10,1... | collective-permute-start | bytes 1568 | tf_op jit(solution)/shard_map/ppermute | solution.py:25
  152.5 14.1 %collective-permute-start.46 = (f32[1,1,130]{2,1,0:T(1,128)S(1)}, f32[1,1,130]{2,1,0:T(1,128)S(1)}, u32[]{:S(2)}, u32[]{:S(2)}) collective-permute-start(f32[1,1,130]{2,1,0:T(1,128)S(1)} %get-tuple-element.171), channel_id=1, source_target_pairs={{1,0},{2,1},{3,2},{4,3},{5,4},{6,5},{7,6},{0,7},{9,8},{10,9},{11,1... | collective-permute-start | bytes 1568 | tf_op jit(solution)/shard_map/ppermute | solution.py:28
  203.8 11.3 %collective-permute-start.63 = (f32[1,1,130]{2,1,0:T(1,128)S(1)}, f32[1,1,130]{2,1,0:T(1,128)S(1)}, u32[]{:S(2)}, u32[]{:S(2)}) collective-permute-start(f32[1,1,130]{2,1,0:T(1,128)S(1)} %get-tuple-element.168), channel_id=1, source_target_pairs={{0,1},{1,2},{2,3},{3,4},{4,5},{5,6},{6,7},{7,0},{8,9},{9,10},{10,1... | collective-permute-start | bytes 1568 | tf_op jit(solution)/shard_map/ppermute | solution.py:25
  203.8 13.9 %collective-permute-start.62 = (f32[1,1,130]{2,1,0:T(1,128)S(1)}, f32[1,1,130]{2,1,0:T(1,128)S(1)}, u32[]{:S(2)}, u32[]{:S(2)}) collective-permute-start(f32[1,1,130]{2,1,0:T(1,128)S(1)} %get-tuple-element.167), channel_id=1, source_target_pairs={{1,0},{2,1},{3,2},{4,3},{5,4},{6,5},{7,6},{0,7},{9,8},{10,9},{11,1... | collective-permute-start | bytes 1568 | tf_op jit(solution)/shard_map/ppermute | solution.py:28
  254.9 11.7 %collective-permute-start.79 = (f32[1,1,130]{2,1,0:T(1,128)S(1)}, f32[1,1,130]{2,1,0:T(1,128)S(1)}, u32[]{:S(2)}, u32[]{:S(2)}) collective-permute-start(f32[1,1,130]{2,1,0:T(1,128)S(1)} %get-tuple-element.164), channel_id=1, source_target_pairs={{0,1},{1,2},{2,3},{3,4},{4,5},{5,6},{6,7},{7,0},{8,9},{9,10},{10,1... | collective-permute-start | bytes 1568 | tf_op jit(solution)/shard_map/ppermute | solution.py:25
  254.9 14.3 %collective-permute-start.78 = (f32[1,1,130]{2,1,0:T(1,128)S(1)}, f32[1,1,130]{2,1,0:T(1,128)S(1)}, u32[]{:S(2)}, u32[]{:S(2)}) collective-permute-start(f32[1,1,130]{2,1,0:T(1,128)S(1)} %get-tuple-element.163), channel_id=1, source_target_pairs={{1,0},{2,1},{3,2},{4,3},{5,4},{6,5},{7,6},{0,7},{9,8},{10,9},{11,1... | collective-permute-start | bytes 1568 | tf_op jit(solution)/shard_map/ppermute | solution.py:28
  306.3 11.3 %collective-permute-start.95 = (f32[1,1,130]{2,1,0:T(1,128)S(1)}, f32[1,1,130]{2,1,0:T(1,128)S(1)}, u32[]{:S(2)}, u32[]{:S(2)}) collective-permute-start(f32[1,1,130]{2,1,0:T(1,128)S(1)} %get-tuple-element.160), channel_id=1, source_target_pairs={{0,1},{1,2},{2,3},{3,4},{4,5},{5,6},{6,7},{7,0},{8,9},{9,10},{10,1... | collective-permute-start | bytes 1568 | tf_op jit(solution)/shard_map/ppermute | solution.py:25
  306.4 13.9 %collective-permute-start.94 = (f32[1,1,130]{2,1,0:T(1,128)S(1)}, f32[1,1,130]{2,1,0:T(1,128)S(1)}, u32[]{:S(2)}, u32[]{:S(2)}) collective-permute-start(f32[1,1,130]{2,1,0:T(1,128)S(1)} %get-tuple-element.159), channel_id=1, source_target_pairs={{1,0},{2,1},{3,2},{4,3},{5,4},{6,5},{7,6},{0,7},{9,8},{10,9},{11,1... | collective-permute-start | bytes 1568 | tf_op jit(solution)/shard_map/ppermute | solution.py:28
  357.4 11.3 %collective-permute-start.111 = (f32[1,1,130]{2,1,0:T(1,128)S(1)}, f32[1,1,130]{2,1,0:T(1,128)S(1)}, u32[]{:S(2)}, u32[]{:S(2)}) collective-permute-start(f32[1,1,130]{2,1,0:T(1,128)S(1)} %get-tuple-element.156), channel_id=1, source_target_pairs={{0,1},{1,2},{2,3},{3,4},{4,5},{5,6},{6,7},{7,0},{8,9},{9,10},{10,1... | collective-permute-start | bytes 1568 | tf_op jit(solution)/shard_map/ppermute | solution.py:25
  357.4 13.9 %collective-permute-start.110 = (f32[1,1,130]{2,1,0:T(1,128)S(1)}, f32[1,1,130]{2,1,0:T(1,128)S(1)}, u32[]{:S(2)}, u32[]{:S(2)}) collective-permute-start(f32[1,1,130]{2,1,0:T(1,128)S(1)} %get-tuple-element.155), channel_id=1, source_target_pairs={{1,0},{2,1},{3,2},{4,3},{5,4},{6,5},{7,6},{0,7},{9,8},{10,9},{11,1... | collective-permute-start | bytes 1568 | tf_op jit(solution)/shard_map/ppermute | solution.py:28
  408.7 11.3 %collective-permute-start.127 = (f32[1,1,130]{2,1,0:T(1,128)S(1)}, f32[1,1,130]{2,1,0:T(1,128)S(1)}, u32[]{:S(2)}, u32[]{:S(2)}) collective-permute-start(f32[1,1,130]{2,1,0:T(1,128)S(1)} %get-tuple-element.152), channel_id=1, source_target_pairs={{0,1},{1,2},{2,3},{3,4},{4,5},{5,6},{6,7},{7,0},{8,9},{9,10},{10,1... | collective-permute-start | bytes 1568 | tf_op jit(solution)/shard_map/ppermute | solution.py:25
  408.7 13.9 %collective-permute-start.126 = (f32[1,1,130]{2,1,0:T(1,128)S(1)}, f32[1,1,130]{2,1,0:T(1,128)S(1)}, u32[]{:S(2)}, u32[]{:S(2)}) collective-permute-start(f32[1,1,130]{2,1,0:T(1,128)S(1)} %get-tuple-element.151), channel_id=1, source_target_pairs={{1,0},{2,1},{3,2},{4,3},{5,4},{6,5},{7,6},{0,7},{9,8},{10,9},{11,1... | collective-permute-start | bytes 1568 | tf_op jit(solution)/shard_map/ppermute | solution.py:28
  435.0 12.0 %collective-permute-start.130 = (f32[2,1,130]{2,1,0:T(1,128)S(1)}, f32[2,1,130]{2,1,0:T(1,128)S(1)}, u32[]{:S(2)}, u32[]{:S(2)}) collective-permute-start(f32[2,1,130]{2,1,0:T(1,128)S(1)} %get-tuple-element.83), channel_id=1, source_target_pairs={{0,1},{1,2},{2,3},{3,4},{4,5},{5,6},{6,7},{7,0},{8,9},{9,10},{10,1... | collective-permute-start | bytes 3128 | tf_op jit(solution)/shard_map/ppermute | solution.py:25
  463.6 13.8 %collective-permute-start.142 = (f32[1,1,130]{2,1,0:T(1,128)S(1)}, f32[1,1,130]{2,1,0:T(1,128)S(1)}, u32[]{:S(2)}, u32[]{:S(2)}) collective-permute-start(f32[1,1,130]{2,1,0:T(1,128)S(1)} %get-tuple-element.147), channel_id=1, source_target_pairs={{1,0},{2,1},{3,2},{4,3},{5,4},{6,5},{7,6},{0,7},{9,8},{10,9},{11,1... | collective-permute-start | bytes 1568 | tf_op jit(solution)/shard_map/ppermute | solution.py:28
  621.3 13.8 %collective-permute-start.150 = (f32[1,1,130]{2,1,0:T(1,128)S(1)}, f32[1,1,130]{2,1,0:T(1,128)S(1)}, u32[]{:S(2)}, u32[]{:S(2)}) collective-permute-start(f32[1,1,130]{2,1,0:T(1,128)S(1)} %get-tuple-element.145), channel_id=1, source_target_pairs={{1,0},{2,1},{3,2},{4,3},{5,4},{6,5},{7,6},{0,7},{9,8},{10,9},{11,1... | collective-permute-start | bytes 1568 | tf_op jit(solution)/shard_map/ppermute | solution.py:28
  781.8 12.5 %collective-permute-start.158 = (f32[1,1,130]{2,1,0:T(1,128)S(1)}, f32[1,1,130]{2,1,0:T(1,128)S(1)}, u32[]{:S(2)}, u32[]{:S(2)}) collective-permute-start(f32[1,1,130]{2,1,0:T(1,128)S(1)} %get-tuple-element.143), channel_id=1, source_target_pairs={{1,0},{2,1},{3,2},{4,3},{5,4},{6,5},{7,6},{0,7},{9,8},{10,9},{11,1... | collective-permute-start | bytes 1568 | tf_op jit(solution)/shard_map/ppermute | solution.py:28
  942.0 13.5 %collective-permute-start.166 = (f32[1,1,130]{2,1,0:T(1,128)S(1)}, f32[1,1,130]{2,1,0:T(1,128)S(1)}, u32[]{:S(2)}, u32[]{:S(2)}) collective-permute-start(f32[1,1,130]{2,1,0:T(1,128)S(1)} %get-tuple-element.141), channel_id=1, source_target_pairs={{1,0},{2,1},{3,2},{4,3},{5,4},{6,5},{7,6},{0,7},{9,8},{10,9},{11,1... | collective-permute-start | bytes 1568 | tf_op jit(solution)/shard_map/ppermute | solution.py:28
  1029.2 12.2 %collective-permute-start.170 = (f32[1,1,130]{2,1,0:T(1,128)S(1)}, f32[1,1,130]{2,1,0:T(1,128)S(1)}, u32[]{:S(2)}, u32[]{:S(2)}) collective-permute-start(f32[1,1,130]{2,1,0:T(1,128)S(1)} %get-tuple-element.140), channel_id=1, source_target_pairs={{0,8},{8,0},{16,24},{24,16},{32,40},{40,32},{48,56},{56,48},{64,72... | collective-permute-start | bytes 1568 | tf_op jit(solution)/shard_map/ppermute | solution.py:34
  1043.7 12.7 %collective-permute-start.174 = (f32[1,1,130]{2,1,0:T(1,128)S(1)}, f32[1,1,130]{2,1,0:T(1,128)S(1)}, u32[]{:S(2)}, u32[]{:S(2)}) collective-permute-start(f32[1,1,130]{2,1,0:T(1,128)S(1)} %get-tuple-element.139), channel_id=1, source_target_pairs={{1,0},{2,1},{3,2},{4,3},{5,4},{6,5},{7,6},{0,7},{9,8},{10,9},{11,1... | collective-permute-start | bytes 1568 | tf_op jit(solution)/shard_map/ppermute | solution.py:28
  (204 other events, 3717.4 us)
where the time goes:
time: 1070 us; the launch traced here: 1060 us
  blocking collectives  453 us (42%)
  starting transfers between devices  352 us (33%)
  waiting for transfers between devices  156 us (15%)
  other arithmetic  58.2 us (5%)
  local copies, waits for them, and re-layouts  27 us (3%)
  between operations  11.5 us (1%)
    psum x4, blocking collectives, squares(): return lax.psum(jnp.sum(residual * residual), ('lon', 'lat'))  255 us
    ppermute x88, starting transfers between devices, from_partner(): lax.ppermute(array, axis, [(i, i ^ 1 << apart) for i in range(lax.axis_si...  202 us
    psum x3, blocking collectives, barotropic(): step_size = old_norm / lax.psum(jnp.sum(direction * image), ('lon', 'lat'))  198 us
    ppermute x88, waiting for transfers between devices, from_partner(): lax.ppermute(array, axis, [(i, i ^ 1 << apart) for i in range(lax.axis_si...  96.8 us
    ppermute x44, starting transfers between devices, extended(): lax.ppermute(lax.slice_in_dim(block, 0, width, axis=dim), axis, backward)  85.5 us
    ppermute x44, starting transfers between devices, extended(): lax.ppermute(lax.slice_in_dim(block, block.shape[dim] - width, None, axis...  64.1 us
    ppermute x44, waiting for transfers between devices, extended(): lax.ppermute(lax.slice_in_dim(block, 0, width, axis=dim), axis, backward)  43.9 us
  transfers between devices with their start and end apart: 176, of which 98 were waited for; matrix products, arithmetic and copies ran while one was open for 5% of the time, Pallas kernels for 0%

commit v1 on v0

v1 whole, which is shorter than its diff:
```python
import functools
import math

import jax
import jax.numpy as jnp
from jax import lax
from jax.experimental import pallas as pl
from jax.experimental.pallas import tpu as pltpu
from jax.sharding import PartitionSpec as P

SUBCYCLES = 8
SOLVE_ITERS = 4
LEVELS = 10
PLANES = 2 * LEVELS
ROWS = 64
LANES = 128
MARGIN = 24
TALL = ROWS + 2 * MARGIN
RIM = 32
SLOPE = 0.15
CENTRE = 9.0
RADIUS = 9.1
F32 = jnp.float32
BOTH = ("lon", "lat")


def lane_ids(rows):
    return lax.broadcasted_iota(jnp.int32, (rows, LANES), 1)


def row_ids(rows):
    return lax.broadcasted_iota(jnp.int32, (rows, LANES), 0)


def turn(x, shift):
    return pltpu.roll(x, shift, 1)


def flip_lanes(x):
    lanes = lane_ids(x.shape[0])
    for bit in range(7):
        step = 1 << bit
        x = jnp.where((lanes & step) != 0, turn(x, step), turn(x, LANES - step))
    return x


def flip_rows(x):
    rows = x.shape[0]
    ids = row_ids(rows)
    for bit in range(3):
        step = 1 << bit
        x = jnp.where((ids & step) != 0, pltpu.roll(x, step, 0), pltpu.roll(x, rows - step, 0))
    return jnp.concatenate([x[r : r + 8] for r in range(rows - 8, -8, -8)], axis=0)


def odd(axis):
    return lax.rem(lax.axis_index(axis), 2) == 1


def at_fold():
    return lax.axis_index("lat") == lax.axis_size("lat") - 1


def pack_kernel(vel, tra, lev, visc, diff, cols, send_a, send_b, north, south):
    lanes = lane_ids(ROWS)

    def velocity_plane(p, acc):
        x = vel[pl.ds(pl.multiple_of(p * ROWS, ROWS), ROWS), :]
        return jnp.where((lanes >> 2) == p, turn(x, 4 * p + 2), acc)

    def tracer_plane(p, acc):
        x = tra[pl.ds(pl.multiple_of(p * ROWS, ROWS), ROWS), :]
        return jnp.where((lanes >> 1) == 40 + p, turn(x, 2 * p + 81), acc)

    acc = lax.fori_loop(0, PLANES, velocity_plane, jnp.zeros((ROWS, LANES), F32))
    acc = lax.fori_loop(0, PLANES, tracer_plane, acc)
    levels = lev[...].astype(F32)
    acc = jnp.where((lanes >> 2) == 30, turn(levels, 122), acc)
    acc = jnp.where((lanes >> 1) == 62, turn(visc[...], 125), acc)
    acc = jnp.where((lanes >> 1) == 63, turn(diff[...], 127), acc)
    cols[...] = acc
    for edge, step, out in ((ROWS - 1, -1, north), (0, 1, south)):
        out[pl.ds(0, PLANES, stride=2), :] = vel[pl.ds(edge, PLANES, stride=ROWS), :]
        out[pl.ds(1, PLANES, stride=2), :] = vel[pl.ds(edge + step, PLANES, stride=ROWS), :]
        out[pl.ds(40, PLANES), :] = tra[pl.ds(edge, PLANES, stride=ROWS), :]
        out[60:61, :] = levels[edge : edge + 1]
        out[61:62, :] = levels[edge + step : edge + step + 1]
        out[62:63, :] = visc[edge : edge + 1, :]
        out[63:64, :] = diff[edge : edge + 1, :]
    up = north[...]
    down = south[...]
    is_odd = odd("lat")
    send_a[...] = jnp.where(is_odd, down, up)
    send_b[...] = jnp.where(is_odd, up, down)

    @pl.when(at_fold())
    def _():
        turned = flip_lanes(up)
        send_b[...] = jnp.where(row_ids(ROWS) < 2 * PLANES, -turned, turned)


def corner_kernel(cols, recv_a, recv_b, out, rim_north, rim_south, spread):
    is_odd = odd("lat")
    got_a = recv_a[...]
    got_b = recv_b[...]
    rim_north[...] = jnp.where(is_odd, got_b, got_a)
    rim_south[...] = jnp.where(is_odd, got_a, got_b)
    out[0:ROWS, :] = cols[...]
    out[ROWS : ROWS + 8, :] = jnp.zeros((8, LANES), F32)
    phase = lane_ids(1) & 3
    for rim, row in ((rim_south, ROWS), (rim_north, ROWS + 1)):
        spread[...] = jnp.zeros((LANES, LANES), F32)
        spread[pl.ds(0, PLANES, stride=4), :] = rim[pl.ds(0, PLANES, stride=2), :]
        spread[120:121, :] = rim[60:61, :]
        flat = spread[...].T
        total = jnp.zeros((1, LANES), F32)
        for c, col in enumerate((126, 127, 0, 1)):
            total = jnp.where(phase == c, turn(flat[col : col + 1], c), total)
        out[row : row + 1, :] = total


def rim_lanes(own, east, west):
    phase = lane_ids(own.shape[0]) & 3
    return jnp.where(phase < 2, own, east), jnp.where(phase < 2, west, own)


def spread_levels(strip):
    lanes = lane_ids(strip.shape[0])
    x = jnp.where((lanes >> 2) == 30, strip, 0.0)
    for step in (4, 8, 16, 32, 64):
        x = x + turn(x, step)
    return x


def star_kernel(
    vel, lev, visc, depth, wind, rim_north, rim_south, own_cols, recv_a, recv_b,
    star, mean, fields, send_a, send_b,
    own_pad, east_pad, west_pad, level_pad, level_east, level_west, faces, plane_pad, lap_pad, swap, swap_lap, sums,
):
    is_odd = odd("lon")
    inner = pl.ds(8, ROWS)
    for src, dst in ((own_cols[...], own_pad), (jnp.where(is_odd, recv_b[...], recv_a[...]), east_pad),
                     (jnp.where(is_odd, recv_a[...], recv_b[...]), west_pad)):
        dst[8 : 8 + ROWS, :] = src[0:ROWS]
        dst[7:8, :] = src[ROWS : ROWS + 1]
        dst[8 + ROWS : 9 + ROWS, :] = src[ROWS + 1 : ROWS + 2]
    lanes = lane_ids(ROWS)
    group = (lanes >> 2).astype(F32)
    level_of_lane = jnp.where(group >= LEVELS, group - LEVELS, group)

    def strips(rows):
        return rim_lanes(own_pad[rows, :], east_pad[rows, :], west_pad[rows, :])

    laps = []
    for which in range(2):
        centre, north, south = (strips(pl.ds(r, ROWS))[which] for r in (8, 9, 7))

        def wet_of(strip):
            return (level_of_lane < spread_levels(strip)).astype(F32)

        wet = wet_of(centre)
        total = wet_of(north) * (north - centre) + wet_of(south) * (south - centre)
        for shift in (1, LANES - 1):
            total += turn(wet, shift) * (turn(centre, shift) - centre)
        laps.append(wet * total)
    phase = lanes & 3

    def swapped(east, west):
        return jnp.where(phase == 1, turn(east, LANES - 1), turn(west, 1))

    for tall in range(0, 72, 8):
        rows = pl.ds(7 + tall, 8)
        e, w = strips(rows)
        swap[pl.ds(tall, 8), :] = jnp.where((lane_ids(8) & 3) == 1, turn(e, LANES - 1), turn(w, 1))
    swap_lap[...] = swapped(laps[0], laps[1])
    level_pad[inner, :] = lev[...].astype(F32)
    level_pad[7:8, :] = rim_south[60:61, :]
    level_pad[6:7, :] = rim_south[61:62, :]
    level_pad[72:73, :] = rim_north[60:61, :]
    level_pad[73:74, :] = rim_north[61:62, :]
    tall_lanes = lane_ids(72)
    first_lane = tall_lanes == 0
    last_lane = tall_lanes == LANES - 1

    def east_west(x, halo):
        rows = x.shape[0]
        return (
            jnp.where(last_lane[0:rows], halo, turn(x, LANES - 1)),
            jnp.where(first_lane[0:rows], halo, turn(x, 1)),
        )

    level_centre = level_pad[pl.ds(7, 72), :]
    level_east[...], level_west[...] = east_west(level_centre, turn(swap[...], 6))
    v = visc[...]
    halo = turn(jnp.where((lanes & 1) == 0, turn(east_pad[inner, :], LANES - 1), turn(west_pad[inner, :], 1)), 3)
    v_east, v_west = east_west(v, halo)
    ids = row_ids(ROWS)
    v_north = jnp.where(ids == ROWS - 1, rim_north[62:63, :], pltpu.roll(v, ROWS - 1, 0))
    v_south = jnp.where(ids == 0, rim_south[62:63, :], pltpu.roll(v, 1, 0))
    for n, other in enumerate((v_east, v_west, v_north, v_south)):
        faces[n] = 0.5 * (v + other)
    row = (lax.axis_index("lat") * ROWS).astype(F32) + ids.astype(F32)
    turning = 0.25 * jnp.sin(math.pi * ((row + 0.5) / (ROWS * lax.axis_size("lat")) - 0.5))
    sums[...] = jnp.zeros((2, ROWS, LANES), F32)

    def level_step(k, carry):
        level = k.astype(F32)
        wet = (level < level_pad[pl.ds(7, 72), :]).astype(F32)
        wet_n = (level < level_pad[pl.ds(8, 72), :]).astype(F32)
        wet_s = (level < level_pad[pl.ds(6, 72), :]).astype(F32)
        wet_e = (level < level_east[...]).astype(F32)
        wet_w = (level < level_west[...]).astype(F32)
        wet_in = (level < level_pad[inner, :]).astype(F32)
        values = []
        for comp in range(2):
            p = comp * LEVELS + k
            x = vel[pl.ds(pl.multiple_of(p * ROWS, ROWS), ROWS), :]
            values.append(x)
            plane_pad[comp, inner, :] = x
            plane_pad[comp, 7:8, :] = rim_south[pl.ds(2 * p, 1), :]
            plane_pad[comp, 6:7, :] = rim_south[pl.ds(2 * p + 1, 1), :]
            plane_pad[comp, 72:73, :] = rim_north[pl.ds(2 * p, 1), :]
            plane_pad[comp, 73:74, :] = rim_north[pl.ds(2 * p + 1, 1), :]
            centre = plane_pad[comp, pl.ds(7, 72), :]
            east, west = east_west(centre, turn(swap[...], 126 - 4 * p))
            total = wet_e * (east - centre) + wet_w * (west - centre)
            total += wet_n * (plane_pad[comp, pl.ds(8, 72), :] - centre)
            total += wet_s * (plane_pad[comp, pl.ds(6, 72), :] - centre)
            lap_pad[comp, pl.ds(7, 72), :] = wet * total
        for comp in range(2):
            p = comp * LEVELS + k
            centre = lap_pad[comp, inner, :]
            east, west = east_west(centre, turn(swap_lap[...], 126 - 4 * p))
            total = faces[0] * wet_e[1:65] * (east - centre) + faces[1] * wet_w[1:65] * (west - centre)
            total += faces[2] * wet_n[1:65] * (lap_pad[comp, pl.ds(9, ROWS), :] - centre)
            total += faces[3] * wet_s[1:65] * (lap_pad[comp, pl.ds(7, ROWS), :] - centre)
            rotated = values[1] if comp == 0 else -values[0]
            out = wet_in * (values[comp] - total + turning * rotated)
            star[pl.ds(pl.multiple_of(p * ROWS, ROWS), ROWS), :] = out
            sums[comp] += out
        return carry

    lax.fori_loop(0, LEVELS, level_step, 0)
    levels = level_pad[inner, :]
    ocean = levels > 0.0
    for comp in range(2):
        column_mean = sums[comp] / jnp.maximum(levels, 1.0)
        mean[pl.ds(comp * ROWS, ROWS), :] = column_mean
        fields[pl.ds(comp * ROWS, ROWS), :] = column_mean + jnp.where(ocean, wind[pl.ds(comp * ROWS, ROWS), :], 0.0)
    fields[pl.ds(2 * ROWS, ROWS), :] = jnp.where(ocean, depth[...], 0.0)
    lat_odd = odd("lat")
    for f in range(3):
        up = fields[pl.ds(f * ROWS + ROWS - MARGIN, MARGIN), :]
        down = fields[pl.ds(f * ROWS, MARGIN), :]
        here = pl.ds(f * MARGIN, MARGIN)
        send_a[here, :] = jnp.where(lat_odd, down, up)
        send_b[here, :] = jnp.where(lat_odd, up, down)

    @pl.when(at_fold())
    def _():
        for f in range(3):
            up = fields[pl.ds(f * ROWS + ROWS - MARGIN, MARGIN), :]
            turned = flip_rows(flip_lanes(up))
            send_b[pl.ds(f * MARGIN, MARGIN), :] = turned if f == 2 else -turned


def tracer_kernel(tra, lev, diff, rim_north, rim_south, recv_a, recv_b, out, swap, faces, level_sides):
    is_odd = odd("lon")
    lanes = lane_ids(ROWS)
    ids = row_ids(ROWS)
    got_a = recv_a[0:ROWS, :]
    got_b = recv_b[0:ROWS, :]
    east_cols = jnp.where(is_odd, got_b, got_a)
    west_cols = jnp.where(is_odd, got_a, got_b)
    swap[...] = jnp.where((lanes & 1) == 0, turn(east_cols, LANES - 1), turn(west_cols, 1))

    def sides(x, halo, north_row, south_row):
        return (
            jnp.where(lanes == LANES - 1, halo, turn(x, LANES - 1)),
            jnp.where(lanes == 0, halo, turn(x, 1)),
            jnp.where(ids == ROWS - 1, north_row, pltpu.roll(x, ROWS - 1, 0)),
            jnp.where(ids == 0, south_row, pltpu.roll(x, 1, 0)),
        )

    level = lev[...].astype(F32)
    level_halo = jnp.where(lanes == LANES - 1, turn(east_cols, 5), turn(west_cols, 7))
    d = diff[...]
    for n, other in enumerate(sides(level, level_halo, rim_north[60:61, :], rim_south[60:61, :])):
        level_sides[n] = jnp.minimum(level, other)
    for n, other in enumerate(sides(d, turn(swap[...], 1), rim_north[63:64, :], rim_south[63:64, :])):
        faces[n] = 0.5 * (d + other)

    def level_step(k, carry):
        weights = [jnp.where(k.astype(F32) < level_sides[n], faces[n], 0.0) for n in range(4)]
        for comp in range(2):
            p = comp * LEVELS + k
            here = pl.ds(pl.multiple_of(p * ROWS, ROWS), ROWS)
            x = tra[here, :]
            around = sides(x, turn(swap[...], 47 - 2 * p), rim_north[pl.ds(40 + p, 1), :], rim_south[pl.ds(40 + p, 1), :])
            total = weights[0] * (around[0] - x)
            for n in range(1, 4):
                total += weights[n] * (around[n] - x)
            out[here, :] = x + total
        return carry

    lax.fori_loop(0, LEVELS, level_step, 0)


def widen_kernel(fields, recv_a, recv_b, tall, send):
    is_odd = odd("lat")
    group = lane_ids(TALL) >> 5
    east = jnp.zeros((TALL, LANES), F32)
    west = jnp.zeros((TALL, LANES), F32)
    for f in range(3):
        here = pl.ds(f * MARGIN, MARGIN)
        got_a = recv_a[here, :]
        got_b = recv_b[here, :]
        tall[pl.ds(f * TALL, MARGIN), :] = jnp.where(is_odd, got_a, got_b)
        tall[pl.ds(f * TALL + MARGIN, ROWS), :] = fields[pl.ds(f * ROWS, ROWS), :]
        tall[pl.ds(f * TALL + MARGIN + ROWS, MARGIN), :] = jnp.where(is_odd, got_b, got_a)
        x = tall[pl.ds(f * TALL, TALL), :]
        east = jnp.where(group == f, turn(x, 32 * (f + 1)), east)
        west = jnp.where(group == f, turn(x, 32 * f), west)
    send[0:TALL, :] = east
    send[TALL : 2 * TALL, :] = west


def gram_pairs():
    return [(i, j) for i in range(SOLVE_ITERS) for j in range(i, SOLVE_ITERS + 1)]


def surface_kernel(tall, recv_a, recv_b, basis_out, flow, partial, state, height, flux, slope, basis, weights, diagonal):
    is_odd = odd("lon")
    rows = pl.ds(8, TALL)
    lanes = lane_ids(TALL)
    got_a = recv_a[...]
    got_b = recv_b[...]
    from_east = jnp.where(is_odd, got_b, got_a)
    from_west = jnp.where(is_odd, got_a, got_b)
    for f in range(3):
        state[f, 0, rows, :] = tall[pl.ds(f * TALL, TALL), :]
        state[f, 1, rows, :] = jnp.where(
            lanes < 64, turn(from_east, (LANES - 32 * f) % LANES), turn(from_west, 96 - 32 * f)
        )
    last = lanes == LANES - 1
    first = lanes == 0

    def lane_sides(a, b):
        n = a.shape[0]
        ea, eb, wa, wb = turn(a, LANES - 1), turn(b, LANES - 1), turn(a, 1), turn(b, 1)
        return (
            (jnp.where(last[0:n], eb, ea), jnp.where(last[0:n], ea, eb)),
            (jnp.where(first[0:n], wb, wa), jnp.where(first[0:n], wa, wb)),
        )

    for half in range(2):
        slope[half, rows, :] = jnp.where(state[2, half, rows, :] > 0.0, SLOPE, 0.0)
        height[half, rows, :] = jnp.zeros((TALL, LANES), F32)

    def subcycle(step, carry):
        for half in range(2):
            flux[half, rows, :] = state[2, half, rows, :] * state[1, half, rows, :]
        east, west = lane_sides(*(state[2, half, rows, :] * state[0, half, rows, :] for half in range(2)))
        for half in range(2):
            divergence = (east[half] - west[half]) + (flux[half, pl.ds(9, TALL), :] - flux[half, pl.ds(7, TALL), :])
            height[half, rows, :] = height[half, rows, :] - slope[half, rows, :] * divergence
        east, west = lane_sides(height[0, rows, :], height[1, rows, :])
        for half in range(2):
            state[0, half, rows, :] = state[0, half, rows, :] - slope[half, rows, :] * (east[half] - west[half])
            state[1, half, rows, :] = state[1, half, rows, :] - slope[half, rows, :] * (
                height[half, pl.ds(9, TALL), :] - height[half, pl.ds(7, TALL), :]
            )
        return carry

    lax.fori_loop(0, SUBCYCLES, subcycle, 0)
    for comp in range(2):
        flow[pl.ds(comp * ROWS, ROWS), :] = state[comp, 0, pl.ds(8 + MARGIN, ROWS), :]
    scale = 2.0 / RADIUS
    short = ROWS + 16
    base = MARGIN

    def nine(read):
        out = [[], []]
        for off in (0, 1, -1):
            a, b = read(0, pl.ds(base + off, short)), read(1, pl.ds(base + off, short))
            east, west = lane_sides(a, b)
            for half, centre in enumerate((a, b)):
                out[half] += [centre, east[half], west[half]]
        return out

    around = nine(lambda half, where: state[2, half, where, :])
    for half in range(2):
        d = around[half][0]
        wet = d > 0.0
        total = jnp.where(wet, 0.05, 1.0)
        for n in range(1, 9):
            factor = 0.5 if n in (1, 2, 3, 6) else 0.25
            w = jnp.where(wet & (around[half][n] > 0.0), factor * (d + around[half][n]), 0.0)
            weights[n - 1, half] = scale * w
            total += w
        diagonal[half] = scale * (total - CENTRE)
        basis[0, half, pl.ds(base, short), :] = height[half, pl.ds(base, short), :]

    def applied(source):
        around = nine(lambda half, where: basis[source, half, where, :])
        out = []
        for half in range(2):
            total = diagonal[half] * around[half][0]
            for n in range(1, 9):
                total -= weights[n - 1, half] * around[half][n]
            out.append(total)
        return out

    for half, x in enumerate(applied(0)):
        basis[1, half, pl.ds(base, short), :] = 0.5 * x

    def next_basis(k, carry):
        for half, x in enumerate(applied(k)):
            basis[k + 1, half, pl.ds(base, short), :] = x - basis[k - 1, half, pl.ds(base, short), :]
        return carry

    lax.fori_loop(1, SOLVE_ITERS, next_basis, 0)
    lane = lane_ids(1)
    row = jnp.zeros((1, LANES), F32)
    mine = pl.ds(8 + MARGIN, ROWS)
    for n, (i, j) in enumerate(gram_pairs()):
        product = basis[i, 0, mine, :] * basis[j, 0, mine, :]
        row = jnp.where(lane == n, jnp.sum(jnp.sum(product, axis=0, keepdims=True), axis=1, keepdims=True), row)
    partial[...] = jnp.broadcast_to(row, partial.shape)
    for i in range(SOLVE_ITERS):
        for half in range(2):
            basis_out[i, half] = basis[i, half, pl.ds(base, short), :]


def solve_coefficients(gram):
    half = 0.5 * RADIUS

    def image_of(d):
        out = [None] * (len(d) + 1)

        def add(n, term):
            out[n] = term if out[n] is None else out[n] + term

        for j, value in enumerate(d):
            add(j, CENTRE * value)
            if j == 0:
                add(1, RADIUS * value)
            else:
                add(j + 1, half * value)
                add(j - 1, half * value)
        return out

    def inner(a, b):
        total = None
        for i, x in enumerate(a):
            for j, y in enumerate(b):
                term = x * y * gram[(min(i, j), max(i, j))]
                total = term if total is None else total + term
        return total

    one = jnp.ones((8, LANES), F32)
    residual, direction, surface = [one], [one], [0.0 * one]
    norm = gram[(0, 0)]
    for iteration in range(SOLVE_ITERS):
        image = image_of(direction)
        step = norm / inner(direction, image)
        surface = [a + step * b for a, b in zip(surface, direction)] + [0.0 * one]
        if iteration == SOLVE_ITERS - 1:
            break
        residual = [(residual[n] if n < len(residual) else 0.0) - step * x for n, x in enumerate(image)]
        fresh = inner(residual, residual)
        ratio = fresh / norm
        direction = [x + (ratio * direction[n] if n < len(direction) else 0.0) for n, x in enumerate(residual)]
        norm = fresh
    return surface[:SOLVE_ITERS]


def final_kernel(gathered, basis, flow, mean, star, lev, velocity_out, surface_out, pad, change):
    sums = jnp.sum(gathered[...], axis=0, keepdims=True)
    lane = lane_ids(1)
    gram = {}
    for n, pair in enumerate(gram_pairs()):
        value = jnp.sum(jnp.where(lane == n, sums, 0.0), axis=1, keepdims=True)
        gram[pair] = jnp.broadcast_to(value, (8, LANES))
    coefficients = [c[0:1] for c in solve_coefficients(gram)]
    for half in range(2):
        total = coefficients[0] * basis[0, half]
        for i in range(1, SOLVE_ITERS):
            total += coefficients[i] * basis[i, half]
        pad[half] = total
    mine = pl.ds(8, ROWS)
    centre = pad[0, mine, :]
    ghost = pad[1, mine, :]
    surface_out[...] = centre
    lanes = lane_ids(ROWS)
    east = jnp.where(lanes == LANES - 1, turn(ghost, LANES - 1), turn(centre, LANES - 1))
    west = jnp.where(lanes == 0, turn(ghost, 1), turn(centre, 1))
    levels = lev[...]
    slope = jnp.where(levels > 0, SLOPE, 0.0)
    slopes = (east - west, pad[0, pl.ds(9, ROWS), :] - pad[0, pl.ds(7, ROWS), :])
    for comp in range(2):
        here = pl.ds(comp * ROWS, ROWS)
        change[comp] = flow[here, :] - slope * slopes[comp] - mean[here, :]

    def level_step(k, carry):
        wet = k < levels
        for comp in range(2):
            here = pl.ds(pl.multiple_of((comp * LEVELS + k) * ROWS, ROWS), ROWS)
            velocity_out[here, :] = star[here, :] + jnp.where(wet, change[comp], 0.0)
        return carry

    lax.fori_loop(0, LEVELS, level_step, 0)


def call(kernel, shapes, scratch, flops, *args):
    out = tuple(jax.ShapeDtypeStruct(s, F32) for s in shapes)
    moved = sum(4 * math.prod(a.shape) for a in args) + sum(4 * math.prod(s) for s in shapes)
    return pl.pallas_call(
        kernel,
        out_shape=out,
        scratch_shapes=[pltpu.VMEM(s, F32) for s in scratch],
        compiler_params=pltpu.CompilerParams(vmem_limit_bytes=32 * 1024 * 1024),
        cost_estimate=pl.CostEstimate(flops=flops, bytes_accessed=moved, transcendentals=0),
    )(*args)


def pair_tables(lon, lat):
    def index(i, j):
        return j * lat + i

    lat_a, lat_b, lon_a, lon_b = [], [], [], []
    for j in range(lon):
        for i in range(lat):
            lat_a.append((index(i, j), index(i ^ 1, j)))
            if i == lat - 1:
                lat_b.append((index(i, j), index(i, lon - 1 - j)))
            elif i > 0:
                lat_b.append((index(i, j), index(i + 1 if i % 2 else i - 1, j)))
            lon_a.append((index(i, j), index(i, j ^ 1)))
            lon_b.append((index(i, j), index(i, (j + 1 if j % 2 else j - 1) % lon)))
    return lat_a, lat_b, lon_a, lon_b


def per_device(lon, lat, tracers, velocity, active_levels, diffusivity, viscosity, ocean_depth, wind_forcing):
    lat_a, lat_b, lon_a, lon_b = pair_tables(lon, lat)

    def swap(x, pairs):
        return lax.ppermute(x, BOTH, pairs)

    block = (ROWS, LANES)
    tra = tracers.reshape(PLANES * ROWS, LANES)
    vel = velocity.reshape(PLANES * ROWS, LANES)
    wind = wind_forcing.reshape(2 * ROWS, LANES)
    cols, send_a, send_b, _, _ = call(
        pack_kernel, [block] * 5, [], 10**6, vel, tra, active_levels, viscosity, diffusivity
    )
    got_b = swap(send_b, lat_b)
    got_a = swap(send_a, lat_a)
    cols, rim_north, rim_south = call(
        corner_kernel, [(ROWS + 8, LANES), block, block], [(LANES, LANES)], 10**5, cols, got_a, got_b
    )
    got_b = swap(cols, lon_b)
    got_a = swap(cols, lon_a)
    tall_pad = (ROWS + 24, LANES)
    star, mean, fields, send_a, send_b = call(
        star_kernel,
        [(PLANES * ROWS, LANES), (2 * ROWS, LANES), (3 * ROWS, LANES), (3 * MARGIN, LANES), (3 * MARGIN, LANES)],
        [tall_pad, tall_pad, tall_pad, tall_pad, (72, LANES), (72, LANES), (4,) + block, (2,) + tall_pad, (2,) + tall_pad,
         (72, LANES), block, (2,) + block],
        10**7,
        vel, active_levels, viscosity, ocean_depth, wind, rim_north, rim_south, cols, got_a, got_b,
    )
    (tracers_out,) = call(
        tracer_kernel, [(PLANES * ROWS, LANES)], [block, (4,) + block, (4,) + block], 10**6,
        tra, active_levels, diffusivity, rim_north, rim_south, got_a, got_b,
    )
    got_b = swap(send_b, lat_b)
    got_a = swap(send_a, lat_a)
    tall, send = call(widen_kernel, [(3 * TALL, LANES), (2 * TALL, LANES)], [], 10**5, fields, got_a, got_b)
    is_odd = lax.axis_index("lon") % 2 == 1
    east, west = send[:TALL], send[TALL:]
    got_b = swap(jnp.where(is_odd, east, west), lon_b)
    got_a = swap(jnp.where(is_odd, west, east), lon_a)
    padded = (2, TALL + 16, LANES)
    short = (2, ROWS + 16, LANES)
    basis, flow, partial = call(
        surface_kernel,
        [(SOLVE_ITERS,) + short, (2 * ROWS, LANES), (lon * lat, LANES)],
        [(3,) + padded, padded, padded, padded, (SOLVE_ITERS + 1,) + padded, (8,) + short, short],
        10**7,
        tall, got_a, got_b,
    )
    gathered = lax.all_to_all(partial, BOTH, 0, 0, tiled=True)
    velocity_out, surface = call(
        final_kernel, [(PLANES * ROWS, LANES), block], [short, (2,) + block], 10**6,
        gathered, basis, flow, mean, star, active_levels,
    )
    return tracers_out.reshape(tracers.shape), velocity_out.reshape(velocity.shape), surface


def solution(mesh):
    placed = (
        P(None, None, "lat", "lon"),
        P(None, None, "lat", "lon"),
        P("lat", "lon"),
        P("lat", "lon"),
        P("lat", "lon"),
        P("lat", "lon"),
        P(None, "lat", "lon"),
    )
    return jax.shard_map(
        functools.partial(per_device, mesh.shape["lon"], mesh.shape["lat"]),
        mesh=mesh,
        in_specs=placed,
        out_specs=(P(None, None, "lat", "lon"), P(None, None, "lat", "lon"), P("lat", "lon")),
        check_vma=False,
    )
```

time: 1070 us -> 72.8 us (0.07); the launches traced: 1060 us -> 72.2 us
  blocking collectives: 453 us -> 0 us
  starting transfers between devices: 352 us -> 38.4 us
  waiting for transfers between devices: 156 us -> 13.8 us
  other arithmetic: 58.2 us -> 0.01 us
  local copies, waits for them, and re-layouts: 27 us -> 4.46 us
  Pallas kernels: 0 us -> 14.8 us
  between operations: 11.5 us -> 0.75 us
    psum x7 -> x0, blocking collectives: 453 us -> none  [the longest x4 255 us: squares(): return lax.psum(jnp.sum(residual * residual), ('lon', 'lat'))]
    ppermute x176 -> x8, starting transfers between devices: 352 us -> 17 us  [swap(): return lax.ppermute(x, BOTH, pairs)]
    ppermute x176 -> x8, waiting for transfers between devices: 156 us -> 6.61 us  [swap(): return lax.ppermute(x, BOTH, pairs)]
    all_to_all x0 -> x1, starting transfers between devices: none -> 21.3 us  [per_device(): gathered = lax.all_to_all(partial, BOTH, 0, 0, tiled=True)]
    slice x40 -> x0, other arithmetic: 16.3 us -> none  [the longest x27 10.2 us: window(): lax.slice_in_dim(field, 1 + row_off, 1 + row_off + row_count, axis=field....]
    pallas_call x0 -> x7, Pallas kernels: none -> 14.8 us  [call(): pl.pallas_call(kernel, out_shape=out, scratch_shapes=[pltpu.VMEM(s, F32)...]
    slice x35 -> x0, local copies, waits for them, and re-layouts: 14.6 us -> none  [the longest x5 6.78 us: window(): lax.slice_in_dim(inner, 1 + col_off, 1 + col_off + col_count, axis=field....]
    reduce_sum x8 -> x0, other arithmetic: 14 us -> none  [the longest x4 8.38 us: barotropic(): step_size = old_norm / lax.psum(jnp.sum(direction * image), ('lon', 'lat'))]
  transfers between devices with their start and end apart: 176 -> 9, of which waited for: 98 -> 6; matrix products, arithmetic and copies ran while one was open for 5% -> 0% of each run, Pallas kernels for 0% -> 3%
where the time goes in v1:
time: 72.8 us; the launch traced here: 72.2 us
  starting transfers between devices  38.4 us (53%)
  Pallas kernels  14.8 us (20%)
  waiting for transfers between devices  13.8 us (19%)
  local copies, waits for them, and re-layouts  4.46 us (6%)
  between operations  0.75 us (1%)
    all_to_all x1, starting transfers between devices, per_device(): gathered = lax.all_to_all(partial, BOTH, 0, 0, tiled=True)  21.3 us
    ppermute x8, starting transfers between devices, swap(): return lax.ppermute(x, BOTH, pairs)  17 us
    pallas_call x7, Pallas kernels, call(): pl.pallas_call(kernel, out_shape=out, scratch_shapes=[pltpu.VMEM(s, F32)...  14.8 us
    all_to_all x1, waiting for transfers between devices, per_device(): gathered = lax.all_to_all(partial, BOTH, 0, 0, tiled=True)  7.22 us
    ppermute x8, waiting for transfers between devices, swap(): return lax.ppermute(x, BOTH, pairs)  6.61 us
    unnamed x22, local copies, waits for them, and re-layouts  4.46 us
  transfers between devices with their start and end apart: 9, of which 6 were waited for; matrix products, arithmetic and copies ran while one was open for 0% of the time, Pallas kernels for 3%

profile of v1, /device:TPU:1, one launch (start us, length us, event | category | flops | bytes accessed | tf_op | source)
XLA Modules:
  0.0 72.2 jit_solution(13468043254957556575)
XLA Ops:
  0.6 1.1 %copy-done = f32[2,10,64,128]{3,2,1,0:T(8,128)S(1)} copy-done((f32[2,10,64,128]{3,2,1,0:T(8,128)S(1)}, f32[2,10,64,128]{3,2,1,0:T(8,128)}, u32[]{:S(2)}) %copy-start) | copy-done | bytes 655384
  1.7 1.1 %copy-done.2 = f32[2,10,64,128]{3,2,1,0:T(8,128)S(1)} copy-done((f32[2,10,64,128]{3,2,1,0:T(8,128)S(1)}, f32[2,10,64,128]{3,2,1,0:T(8,128)}, u32[]{:S(2)}) %copy-start.2) | copy-done | bytes 655384
  2.8 0.8 %copy-done.4 = s32[64,128]{1,0:T(8,128)S(1)} copy-done((s32[64,128]{1,0:T(8,128)S(1)}, s32[64,128]{1,0:T(8,128)}, u32[]{:S(2)}) %copy-start.4) | copy-done | bytes 32792
  3.6 0.8 %copy-done.6 = f32[64,128]{1,0:T(8,128)S(1)} copy-done((f32[64,128]{1,0:T(8,128)S(1)}, f32[64,128]{1,0:T(8,128)}, u32[]{:S(2)}) %copy-start.6) | copy-done | bytes 32792
  4.3 0.8 %copy-done.7 = f32[64,128]{1,0:T(8,128)S(1)} copy-done((f32[64,128]{1,0:T(8,128)S(1)}, f32[64,128]{1,0:T(8,128)}, u32[]{:S(2)}) %copy-start.7) | copy-done | bytes 32792
  5.1 3.8 %shard_map.94 = (f32[64,128]{1,0:T(8,128)S(1)}, f32[64,128]{1,0:T(8,128)S(1)}, f32[64,128]{1,0:T(8,128)S(1)}, f32[64,128]{1,0:T(8,128)}, f32[64,128]{1,0:T(8,128)}) custom-call(f32[1280,128]{1,0:T(8,128)S(1)} %bitcast.9, f32[1280,128]{1,0:T(8,128)S(1)} %bitcast.11, s32[64,128]{1,0:T(8,128)S(1)} %copy-done.4, f32[64,128]{1,0:T(8,128)S(1)} %copy-done.6, ...), custom_call_target="tpu_custom_call" | custom-call | flops 1000000 | bytes 1572864 | tf_op jit(solution)/shard_map/pallas_call | solution.py:518
  8.9 2.0 %collective-permute-start = (f32[64,128]{1,0:T(8,128)S(1)}, f32[64,128]{1,0:T(8,128)S(1)}, u32[]{:S(2)}, u32[]{:S(2)}) collective-permute-start(f32[64,128]{1,0:T(8,128)S(1)} %get-tuple-element.22), channel_id=1, source_target_pairs={{0,1},{1,0},{2,3},{3,2},{4,5},{5,4},{6,7},{7,6},{8,9},{9,8},{10,11... | collective-permute-start | bytes 98312 | tf_op jit(solution)/shard_map/ppermute | solution.py:548
  10.9 0.7 collective-permute-start.1
  11.6 0.6 collective-permute-done.recv_a
  12.4 2.1 %collective-permute-start.2 = (f32[72,128]{1,0:T(8,128)S(1)}, f32[72,128]{1,0:T(8,128)S(1)}, u32[]{:S(2)}, u32[]{:S(2)}) collective-permute-start(f32[72,128]{1,0:T(8,128)S(1)} %get-tuple-element.26.own_cols), channel_id=1, source_target_pairs={{0,8},{1,9},{2,10},{3,11},{4,12},{5,13},{6,14},{7,15},{8,0},{9,1},... | collective-permute-start | bytes 110600 | tf_op jit(solution)/shard_map/ppermute | solution.py:548
  14.4 1.7 %collective-permute-start.3 = (f32[72,128]{1,0:T(8,128)S(1)}, f32[72,128]{1,0:T(8,128)S(1)}, u32[]{:S(2)}, u32[]{:S(2)}) collective-permute-start(f32[72,128]{1,0:T(8,128)S(1)} %get-tuple-element.26.own_cols), channel_id=1, source_target_pairs={{0,120},{1,121},{2,122},{3,123},{4,124},{5,125},{6,126},{7,127},{8... | collective-permute-start | bytes 110600 | tf_op jit(solution)/shard_map/ppermute | solution.py:548
  16.1 1.7 %collective-permute-done.3.recv_b = f32[72,128]{1,0:T(8,128)S(1)} collective-permute-done((f32[72,128]{1,0:T(8,128)S(1)}, f32[72,128]{1,0:T(8,128)S(1)}, u32[]{:S(2)}, u32[]{:S(2)}) %collective-permute-start.3) | collective-permute-done | bytes 36896 | tf_op jit(solution)/shard_map/ppermute | solution.py:548
  17.8 3.1 %shard_map.97 = (f32[1280,128]{1,0:T(8,128)S(1)}, f32[128,128]{1,0:T(8,128)S(1)}, f32[192,128]{1,0:T(8,128)S(1)}, f32[72,128]{1,0:T(8,128)S(1)}, f32[72,128]{1,0:T(8,128)S(1)}) custom-call(f32[1280,128]{1,0:T(8,128)S(1)} %bitcast.10, s32[64,128]{1,0:T(8,128)S(1)} %copy-done.4, f32[64,128]{1,0:T(8,128)S(1)} %copy-done.6, f32[64,128]{1,0:T(8,128)S(1)} %copy-done.10, ...), custom_call_target="tpu_custom_call" | custom-call | flops 10000000 | bytes 1888256 | tf_op jit(solution)/shard_map/pallas_call | solution.py:518
  20.9 3.9 %collective-permute-start.4 = (f32[72,128]{1,0:T(8,128)S(1)}, f32[72,128]{1,0:T(8,128)S(1)}, u32[]{:S(2)}, u32[]{:S(2)}) collective-permute-start(f32[72,128]{1,0:T(8,128)S(1)} %get-tuple-element.28), channel_id=1, source_target_pairs={{0,1},{1,0},{2,3},{3,2},{4,5},{5,4},{6,7},{7,6},{8,9},{9,8},{10,11... | collective-permute-start | bytes 110600 | tf_op jit(solution)/shard_map/ppermute | solution.py:548
  24.8 0.7 collective-permute-start.5
  25.5 0.7 collective-permute-done.4.recv_a
  26.4 6.0 %collective-permute-start.6 = (f32[112,128]{1,0:T(8,128)S(1)}, f32[112,128]{1,0:T(8,128)S(1)}, u32[]{:S(2)}, u32[]{:S(2)}) collective-permute-start(f32[112,128]{1,0:T(8,128)S(1)} %get-tuple-element.40), channel_id=1, source_target_pairs={{0,8},{1,9},{2,10},{3,11},{4,12},{5,13},{6,14},{7,15},{8,0},{9,1},... | collective-permute-start | bytes 172040 | tf_op jit(solution)/shard_map/ppermute | solution.py:548
  32.4 0.9 %collective-permute-done.6.recv_a = f32[112,128]{1,0:T(8,128)S(1)} collective-permute-done((f32[112,128]{1,0:T(8,128)S(1)}, f32[112,128]{1,0:T(8,128)S(1)}, u32[]{:S(2)}, u32[]{:S(2)}) %collective-permute-start.6) | collective-permute-done | bytes 57376 | tf_op jit(solution)/shard_map/ppermute | solution.py:548
  33.2 2.7 %collective-permute-done.7.recv_b = f32[112,128]{1,0:T(8,128)S(1)} collective-permute-done((f32[112,128]{1,0:T(8,128)S(1)}, f32[112,128]{1,0:T(8,128)S(1)}, u32[]{:S(2)}, u32[]{:S(2)}) %collective-permute-start.7) | collective-permute-done | bytes 57376 | tf_op jit(solution)/shard_map/ppermute | solution.py:548
  36.0 4.1 %shard_map.99 = (f32[4,2,80,128]{3,2,1,0:T(8,128)S(1)}, f32[128,128]{1,0:T(8,128)S(1)}, f32[128,128]{1,0:T(8,128)}) custom-call(f32[336,128]{1,0:T(8,128)S(1)} %get-tuple-element.30.tall, f32[112,128]{1,0:T(8,128)S(1)} %collective-permute-done.6.recv_a, f32[112,128]{1,0:T(8,128)S(1)} %collective-permute-done.7.recv_b), custom_call_target="tpu_custom_call" | custom-call | flops 10000000 | bytes 745472 | tf_op jit(solution)/shard_map/pallas_call | solution.py:518
  40.1 21.3 %all-to-all-start = ((f32[128,1,128]{2,1,0:T(1,128)}), f32[128,1,128]{2,1,0:T(1,128)S(1)}, u32[]{:S(2)}, u32[]{:S(2)}) async-start(f32[128,1,128]{2,1,0:T(1,128)} %bitcast.5), calls=%async_computation | async-start | bytes 131072 | tf_op jit(solution)/shard_map/all_to_all | solution.py:593
  61.4 2.3 %shard_map.96 = f32[1280,128]{1,0:T(8,128)} custom-call(f32[1280,128]{1,0:T(8,128)S(1)} %bitcast.12, s32[64,128]{1,0:T(8,128)S(1)} %copy-done.5, f32[64,128]{1,0:T(8,128)S(1)} %copy-done.8, f32[64,128]{1,0:T(8,128)S(1)} %get-tuple-element.24.rim_north, f32[64,128]{1,0:T(8,128)S(1)} %get-tuple-element.25.rim_south, ...), custom_call_target="tpu_custom_call" | custom-call | flops 1000000 | bytes 1515520 | tf_op jit(solution)/shard_map/pallas_call | solution.py:518
  63.7 7.2 %all-to-all-done = f32[128,1,128]{2,1,0:T(1,128)S(1)} async-done(((f32[128,1,128]{2,1,0:T(1,128)}), f32[128,1,128]{2,1,0:T(1,128)S(1)}, u32[]{:S(2)}, u32[]{:S(2)}) %all-to-all-start) | async-done | bytes 65568 | tf_op jit(solution)/shard_map/all_to_all | solution.py:593
  70.9 1.3 %shard_map.100 = (f32[1280,128]{1,0:T(8,128)}, f32[64,128]{1,0:T(8,128)}) custom-call(f32[128,128]{1,0:T(8,128)S(1)} %bitcast.13, f32[4,2,80,128]{3,2,1,0:T(8,128)S(1)} %get-tuple-element.33.basis, f32[128,128]{1,0:T(8,128)S(1)} %get-tuple-element.34.flow, f32[128,128]{1,0:T(8,128)S(1)} %get-tuple-element.35.mean, f32[1280,128]{1,0:T(8,128)S(1)} %get-tuple-element.36.star, ...), custom_call_target="tpu_custom_call" | custom-call | flops 1000000 | bytes 1900544 | tf_op jit(solution)/shard_map/pallas_call | solution.py:518
  (24 shorter events, 0.4 us)
Async XLA Ops:
  0.6 1.1 %copy-start = (f32[2,10,64,128]{3,2,1,0:T(8,128)S(1)}, f32[2,10,64,128]{3,2,1,0:T(8,128)}, u32[]{:S(2)}) copy-start(f32[2,10,64,128]{3,2,1,0:T(8,128)} %param.8) | copy-start | bytes 1966084
  1.7 1.1 %copy-start.2 = (f32[2,10,64,128]{3,2,1,0:T(8,128)S(1)}, f32[2,10,64,128]{3,2,1,0:T(8,128)}, u32[]{:S(2)}) copy-start(f32[2,10,64,128]{3,2,1,0:T(8,128)} %param.7) | copy-start | bytes 1966084
  2.8 0.8 %copy-start.4 = (s32[64,128]{1,0:T(8,128)S(1)}, s32[64,128]{1,0:T(8,128)}, u32[]{:S(2)}) copy-start(s32[64,128]{1,0:T(8,128)} %lev.7) | copy-start | bytes 98308
  3.6 0.8 %copy-start.6 = (f32[64,128]{1,0:T(8,128)S(1)}, f32[64,128]{1,0:T(8,128)}, u32[]{:S(2)}) copy-start(f32[64,128]{1,0:T(8,128)} %visc.3) | copy-start | bytes 98308
  4.3 0.8 %copy-start.7 = (f32[64,128]{1,0:T(8,128)S(1)}, f32[64,128]{1,0:T(8,128)}, u32[]{:S(2)}) copy-start(f32[64,128]{1,0:T(8,128)} %diff.3) | copy-start | bytes 98308
  5.1 12.7 %copy-start.1 = (f32[2,10,64,128]{3,2,1,0:T(8,128)S(1)}, f32[2,10,64,128]{3,2,1,0:T(8,128)}, u32[]{:S(2)}) copy-start(f32[2,10,64,128]{3,2,1,0:T(8,128)} %param.8) | copy-start | bytes 1966084
  8.9 9.0 %copy-start.9 = (f32[2,64,128]{2,1,0:T(8,128)S(1)}, f32[2,64,128]{2,1,0:T(8,128)}, u32[]{:S(2)}) copy-start(f32[2,64,128]{2,1,0:T(8,128)} %param.13) | copy-start | bytes 196612
  8.9 3.3 %collective-permute-start = (f32[64,128]{1,0:T(8,128)S(1)}, f32[64,128]{1,0:T(8,128)S(1)}, u32[]{:S(2)}, u32[]{:S(2)}) collective-permute-start(f32[64,128]{1,0:T(8,128)S(1)} %get-tuple-element.22), channel_id=1, source_target_pairs={{0,1},{1,0},{2,3},{3,2},{4,5},{5,4},{6,7},{7,6},{8,9},{9,8},{10,11... | collective-permute-start | bytes 98312 | tf_op jit(solution)/shard_map/ppermute | solution.py:548
  10.9 1.3 %collective-permute-start.1 = (f32[64,128]{1,0:T(8,128)S(1)}, f32[64,128]{1,0:T(8,128)S(1)}, u32[]{:S(2)}, u32[]{:S(2)}) collective-permute-start(f32[64,128]{1,0:T(8,128)S(1)} %get-tuple-element.23), channel_id=1, source_target_pairs={{1,2},{2,1},{3,4},{4,3},{5,6},{6,5},{7,127},{9,10},{10,9},{11,12},... | collective-permute-start | bytes 98312 | tf_op jit(solution)/shard_map/ppermute | solution.py:548
  12.2 5.6 %copy-start.10 = (f32[64,128]{1,0:T(8,128)S(1)}, f32[64,128]{1,0:T(8,128)}, u32[]{:S(2)}) copy-start(f32[64,128]{1,0:T(8,128)} %depth.1) | copy-start | bytes 98308
  12.4 3.8 %collective-permute-start.2 = (f32[72,128]{1,0:T(8,128)S(1)}, f32[72,128]{1,0:T(8,128)S(1)}, u32[]{:S(2)}, u32[]{:S(2)}) collective-permute-start(f32[72,128]{1,0:T(8,128)S(1)} %get-tuple-element.26.own_cols), channel_id=1, source_target_pairs={{0,8},{1,9},{2,10},{3,11},{4,12},{5,13},{6,14},{7,15},{8,0},{9,1},... | collective-permute-start | bytes 110600 | tf_op jit(solution)/shard_map/ppermute | solution.py:548
  14.4 3.4 %collective-permute-start.3 = (f32[72,128]{1,0:T(8,128)S(1)}, f32[72,128]{1,0:T(8,128)S(1)}, u32[]{:S(2)}, u32[]{:S(2)}) collective-permute-start(f32[72,128]{1,0:T(8,128)S(1)} %get-tuple-element.26.own_cols), channel_id=1, source_target_pairs={{0,120},{1,121},{2,122},{3,123},{4,124},{5,125},{6,126},{7,127},{8... | collective-permute-start | bytes 110600 | tf_op jit(solution)/shard_map/ppermute | solution.py:548
  20.9 40.5 %copy-start.3 = (f32[2,10,64,128]{3,2,1,0:T(8,128)S(1)}, f32[2,10,64,128]{3,2,1,0:T(8,128)}, u32[]{:S(2)}) copy-start(f32[2,10,64,128]{3,2,1,0:T(8,128)} %param.7) | copy-start | bytes 1966084
  20.9 5.3 %collective-permute-start.4 = (f32[72,128]{1,0:T(8,128)S(1)}, f32[72,128]{1,0:T(8,128)S(1)}, u32[]{:S(2)}, u32[]{:S(2)}) collective-permute-start(f32[72,128]{1,0:T(8,128)S(1)} %get-tuple-element.28), channel_id=1, source_target_pairs={{0,1},{1,0},{2,3},{3,2},{4,5},{5,4},{6,7},{7,6},{8,9},{9,8},{10,11... | collective-permute-start | bytes 110600 | tf_op jit(solution)/shard_map/ppermute | solution.py:548
  24.8 1.4 %collective-permute-start.5 = (f32[72,128]{1,0:T(8,128)S(1)}, f32[72,128]{1,0:T(8,128)S(1)}, u32[]{:S(2)}, u32[]{:S(2)}) collective-permute-start(f32[72,128]{1,0:T(8,128)S(1)} %get-tuple-element.29), channel_id=1, source_target_pairs={{1,2},{2,1},{3,4},{4,3},{5,6},{6,5},{7,127},{9,10},{10,9},{11,12},... | collective-permute-start | bytes 110600 | tf_op jit(solution)/shard_map/ppermute | solution.py:548
  26.4 6.9 %collective-permute-start.6 = (f32[112,128]{1,0:T(8,128)S(1)}, f32[112,128]{1,0:T(8,128)S(1)}, u32[]{:S(2)}, u32[]{:S(2)}) collective-permute-start(f32[112,128]{1,0:T(8,128)S(1)} %get-tuple-element.40), channel_id=1, source_target_pairs={{0,8},{1,9},{2,10},{3,11},{4,12},{5,13},{6,14},{7,15},{8,0},{9,1},... | collective-permute-start | bytes 172040 | tf_op jit(solution)/shard_map/ppermute | solution.py:548
  32.4 3.6 %collective-permute-start.7 = (f32[112,128]{1,0:T(8,128)S(1)}, f32[112,128]{1,0:T(8,128)S(1)}, u32[]{:S(2)}, u32[]{:S(2)}) collective-permute-start(f32[112,128]{1,0:T(8,128)S(1)} %get-tuple-element.39), channel_id=1, source_target_pairs={{0,120},{1,121},{2,122},{3,123},{4,124},{5,125},{6,126},{7,127},{8... | collective-permute-start | bytes 172040 | tf_op jit(solution)/shard_map/ppermute | solution.py:548
  40.1 21.4 %copy-start.5 = (s32[64,128]{1,0:T(8,128)S(1)}, s32[64,128]{1,0:T(8,128)}, u32[]{:S(2)}) copy-start(s32[64,128]{1,0:T(8,128)} %lev.7) | copy-start | bytes 98308
  40.1 21.4 %copy-start.8 = (f32[64,128]{1,0:T(8,128)S(1)}, f32[64,128]{1,0:T(8,128)}, u32[]{:S(2)}) copy-start(f32[64,128]{1,0:T(8,128)} %diff.3) | copy-start | bytes 98308
  40.1 30.9 %all-to-all-start = ((f32[128,1,128]{2,1,0:T(1,128)}), f32[128,1,128]{2,1,0:T(1,128)S(1)}, u32[]{:S(2)}, u32[]{:S(2)}) async-start(f32[128,1,128]{2,1,0:T(1,128)} %bitcast.5), calls=%async_computation | async-start | bytes 131072 | tf_op jit(solution)/shard_map/all_to_all | solution.py:593

commit v2 on v1

v2 whole, which is shorter than its diff:
```python
import functools
import math

import jax
import jax.numpy as jnp
from jax import lax
from jax.experimental import pallas as pl
from jax.experimental.pallas import tpu as pltpu
from jax.sharding import PartitionSpec as P

SUBCYCLES = 8
SOLVE_ITERS = 4
LEVELS = 10
PLANES = 2 * LEVELS
ROWS = 64
LANES = 128
MARGIN = 24
TALL = ROWS + 2 * MARGIN
RIM = 32
SLOPE = 0.15
CENTRE = 9.0
RADIUS = 9.1
F32 = jnp.float32
BOTH = ("lon", "lat")

STRIP = 24
RIMS = 3 * STRIP
LAT_SEND = 3 * MARGIN + RIMS + MARGIN
LON_SEND = 2 * TALL + 2 * STRIP


def lane_ids(rows):
    return lax.broadcasted_iota(jnp.int32, (rows, LANES), 1)


def row_ids(rows):
    return lax.broadcasted_iota(jnp.int32, (rows, LANES), 0)


def turn(x, shift):
    return pltpu.roll(x, shift, 1)


def flip_lanes(x, bits=7):
    lanes = lane_ids(x.shape[0])
    for bit in range(bits):
        step = 1 << bit
        x = jnp.where((lanes & step) != 0, turn(x, step), turn(x, LANES - step))
    return x


def flip_rows(x):
    rows = x.shape[0]
    ids = row_ids(rows)
    for bit in range(3):
        step = 1 << bit
        x = jnp.where((ids & step) != 0, pltpu.roll(x, step, 0), pltpu.roll(x, rows - step, 0))
    return jnp.concatenate([x[r : r + 8] for r in range(rows - 8, -8, -8)], axis=0)


def odd(axis):
    return lax.rem(lax.axis_index(axis), 2) == 1


def at_fold():
    return lax.axis_index("lat") == lax.axis_size("lat") - 1


def shifted(x):
    rows = x.shape[0]
    return (turn(x, LANES - 1), turn(x, 1), pltpu.roll(x, rows - 1, 0), pltpu.roll(x, 1, 0))


def block_kernel(
    vel, tra, lev, visc, diff, depth, wind,
    star, mean, fields, cols, north, south, send_a, send_b,
    faces, face_levels, sums, turning,
):
    lanes = lane_ids(ROWS)
    ids = row_ids(ROWS)
    levels = lev[...].astype(F32)
    v = visc[...]
    inside = (lanes < LANES - 1, lanes > 0, ids < ROWS - 1, ids > 0)
    for n, (v_n, level_n) in enumerate(zip(shifted(v), shifted(levels))):
        faces[n] = 0.5 * (v + v_n)
        face_levels[n] = jnp.where(inside[n], jnp.minimum(levels, level_n), 0.0)
    row = (lax.axis_index("lat") * ROWS).astype(F32) + ids.astype(F32)
    turning[...] = 0.25 * jnp.sin(math.pi * ((row + 0.5) / (ROWS * lax.axis_size("lat")) - 0.5))
    sums[...] = jnp.zeros((2, ROWS, LANES), F32)
    acc = jnp.where((lanes >> 2) == 20, turn(levels, 82), 0.0)
    cols[...] = jnp.where((lanes >> 2) == 21, turn(v, 86), acc)

    def level_step(k, carry):
        level = k.astype(F32)
        open_faces = [level < face_levels[n] for n in range(4)]
        wet = level < lev[...].astype(F32)
        weights = [jnp.where(o, faces[n], 0.0) for n, o in enumerate(open_faces)]
        values = [
            vel[pl.ds(pl.multiple_of((comp * LEVELS + k) * ROWS, ROWS), ROWS), :] for comp in range(2)
        ]
        packed = cols[...]
        for comp, x in enumerate(values):
            p = comp * LEVELS + k
            lap = jnp.zeros((ROWS, LANES), F32)
            for n, x_n in enumerate(shifted(x)):
                lap += jnp.where(open_faces[n], x_n - x, 0.0)
            second = jnp.zeros((ROWS, LANES), F32)
            for n, lap_n in enumerate(shifted(lap)):
                second += weights[n] * (lap_n - lap)
            rotated = values[1] if comp == 0 else -values[0]
            out = jnp.where(wet, x - second + turning[...] * rotated, 0.0)
            star[pl.ds(pl.multiple_of(p * ROWS, ROWS), ROWS), :] = out
            sums[comp] += out
            packed = jnp.where((lanes >> 2) == p, turn(x, 4 * p + 2), packed)
            t = tra[pl.ds(pl.multiple_of(p * ROWS, ROWS), ROWS), :]
            packed = jnp.where((lanes >> 1) == 44 + p, turn(t, lax.rem(89 + 2 * p, LANES)), packed)
        cols[...] = packed
        return carry

    lax.fori_loop(0, LEVELS, level_step, 0)
    ocean = levels > 0.0
    for comp in range(2):
        here = pl.ds(comp * ROWS, ROWS)
        column_mean = sums[comp] / jnp.maximum(levels, 1.0)
        mean[here, :] = column_mean
        fields[here, :] = column_mean + jnp.where(ocean, wind[here, :], 0.0)
    fields[pl.ds(2 * ROWS, ROWS), :] = jnp.where(ocean, depth[...], 0.0)
    for edge, step, out in ((ROWS - 1, -1, north), (0, 1, south)):
        out[...] = jnp.zeros((RIMS, LANES), F32)
        for d in range(2):
            r = edge + d * step
            out[pl.ds(d * STRIP, PLANES), :] = vel[pl.ds(r, PLANES, stride=ROWS), :]
            out[pl.ds(d * STRIP + 20, 1), :] = levels[r : r + 1]
            out[pl.ds(d * STRIP + 21, 1), :] = visc[pl.ds(r, 1), :]
        out[pl.ds(2 * STRIP, PLANES), :] = tra[pl.ds(edge, PLANES, stride=ROWS), :]
        out[pl.ds(2 * STRIP + 20, 1), :] = diff[pl.ds(edge, 1), :]
    lat_odd = odd("lat")

    def put(start, up, down):
        here = pl.ds(start, up.shape[0])
        send_a[here, :] = jnp.where(lat_odd, down, up)
        send_b[here, :] = jnp.where(lat_odd, up, down)

    for f in range(3):
        put(f * MARGIN, fields[pl.ds((f + 1) * ROWS - MARGIN, MARGIN), :], fields[pl.ds(f * ROWS, MARGIN), :])
    put(3 * MARGIN, north[...], south[...])
    put(3 * MARGIN + RIMS, cols[ROWS - MARGIN : ROWS, :], cols[0:MARGIN, :])

    @pl.when(at_fold())
    def _():
        for f in range(3):
            turned = flip_rows(flip_lanes(fields[pl.ds((f + 1) * ROWS - MARGIN, MARGIN), :]))
            send_b[pl.ds(f * MARGIN, MARGIN), :] = turned if f == 2 else -turned
        turned = flip_lanes(north[...])
        r = row_ids(RIMS)
        is_velocity = (r < PLANES) | ((r >= STRIP) & (r < STRIP + PLANES))
        send_b[pl.ds(3 * MARGIN, RIMS), :] = jnp.where(is_velocity, -turned, turned)
        turned = flip_rows(flip_lanes(cols[ROWS - MARGIN : ROWS, :], 2))
        send_b[pl.ds(3 * MARGIN + RIMS, MARGIN), :] = jnp.where(lane_ids(MARGIN) < 4 * PLANES, -turned, turned)


def widen_kernel(fields, cols, diff, north, south, recv_a, recv_b, tall, strips, tracer_rows, send_a, send_b, east, west):
    lat_odd = odd("lat")
    lon_odd = odd("lon")
    group = lane_ids(TALL) >> 5

    def received(start, count):
        here = pl.ds(start, count)
        got_a = recv_a[here, :]
        got_b = recv_b[here, :]
        return jnp.where(lat_odd, got_b, got_a), jnp.where(lat_odd, got_a, got_b)

    acc_east = jnp.zeros((TALL, LANES), F32)
    acc_west = jnp.zeros((TALL, LANES), F32)
    for f in range(4):
        from_north, from_south = received(f * MARGIN if f < 3 else 3 * MARGIN + RIMS, MARGIN)
        tall[pl.ds(f * TALL, MARGIN), :] = from_south
        tall[pl.ds(f * TALL + MARGIN, ROWS), :] = fields[pl.ds(f * ROWS, ROWS), :] if f < 3 else cols[...]
        tall[pl.ds(f * TALL + MARGIN + ROWS, MARGIN), :] = from_north
        if f < 3:
            x = tall[pl.ds(f * TALL, TALL), :]
            acc_east = jnp.where(group == f, turn(x, 32 * (f + 1)), acc_east)
            acc_west = jnp.where(group == f, turn(x, 32 * f), acc_west)
    for out, acc, shift in ((east, acc_east, 97), (west, acc_west, 96)):
        out[pl.ds(0, TALL), :] = acc
        out[pl.ds(MARGIN, ROWS), :] = jnp.where(lane_ids(ROWS) == 96, turn(diff[...], shift), acc[MARGIN : MARGIN + ROWS])
    rims = received(3 * MARGIN, RIMS)
    for s, (own, rim) in enumerate(((north, rims[0]), (south, rims[1]))):
        pieces = (rim[STRIP : 2 * STRIP], rim[0:STRIP], own[0:STRIP, :], own[STRIP : 2 * STRIP, :])
        acc_east = jnp.zeros((STRIP, LANES), F32)
        acc_west = jnp.zeros((STRIP, LANES), F32)
        for r, x in enumerate(pieces):
            strips[pl.ds((4 * s + r) * STRIP, STRIP), :] = x
            acc_east = jnp.where(group[0:STRIP] == r, turn(x, (32 * (r + 1)) % LANES), acc_east)
            acc_west = jnp.where(group[0:STRIP] == r, turn(x, 32 * r), acc_west)
        east[pl.ds(TALL + s * STRIP, STRIP), :] = acc_east
        west[pl.ds(TALL + s * STRIP, STRIP), :] = acc_west
        tracer_rows[pl.ds(2 * s * STRIP, STRIP), :] = rim[2 * STRIP : 3 * STRIP]
        tracer_rows[pl.ds((2 * s + 1) * STRIP, STRIP), :] = rim[0:STRIP]
    k = tall[pl.ds(3 * TALL, TALL), :]
    send_a[pl.ds(0, TALL), :] = k
    send_b[pl.ds(0, TALL), :] = k
    rest = pl.ds(TALL, TALL + 2 * STRIP)
    e, w = east[...], west[...]
    send_a[rest, :] = jnp.where(lon_odd, w, e)
    send_b[rest, :] = jnp.where(lon_odd, e, w)


def tracer_kernel(tra, lev, diff, tracer_rows, recv_a, recv_b, out, swap, faces, face_levels):
    is_odd = odd("lon")
    lanes = lane_ids(ROWS)
    ids = row_ids(ROWS)

    def received(start):
        here = pl.ds(start + MARGIN, ROWS)
        got_a = recv_a[here, :]
        got_b = recv_b[here, :]
        return jnp.where(is_odd, got_b, got_a), jnp.where(is_odd, got_a, got_b)

    east_cols, west_cols = received(0)
    east_rest, west_rest = received(TALL)
    swap[...] = jnp.where((lanes & 1) == 0, turn(east_cols, LANES - 1), turn(west_cols, 1))

    def sides(x, halo, row):
        east, west, north, south = shifted(x)
        return (
            jnp.where(lanes == LANES - 1, halo, east),
            jnp.where(lanes == 0, halo, west),
            jnp.where(ids == ROWS - 1, tracer_rows[pl.ds(row, 1), :], north),
            jnp.where(ids == 0, tracer_rows[pl.ds(row + 2 * STRIP, 1), :], south),
        )

    level = lev[...].astype(F32)
    level_halo = jnp.where(lanes == LANES - 1, turn(east_cols, 45), turn(west_cols, 47))
    d = diff[...]
    d_halo = jnp.where(lanes == LANES - 1, turn(east_rest, 31), turn(west_rest, 32))
    for n, other in enumerate(sides(level, level_halo, STRIP + 20)):
        face_levels[n] = jnp.minimum(level, other)
    for n, other in enumerate(sides(d, d_halo, 20)):
        faces[n] = 0.5 * (d + other)

    def level_step(k, carry):
        weights = [jnp.where(k.astype(F32) < face_levels[n], faces[n], 0.0) for n in range(4)]
        for comp in range(2):
            p = comp * LEVELS + k
            here = pl.ds(pl.multiple_of(p * ROWS, ROWS), ROWS)
            x = tra[here, :]
            around = sides(x, turn(swap[...], 39 - 2 * p), p)
            total = weights[0] * (around[0] - x)
            for n in range(1, 4):
                total += weights[n] * (around[n] - x)
            out[here, :] = x + total
        return carry

    lax.fori_loop(0, LEVELS, level_step, 0)


def column_strip(strip):
    rows = strip.shape[0]
    lanes = lane_ids(rows)
    ids = row_ids(rows)
    phase = lanes & 3
    group = lanes >> 2

    def spread(which):
        x = jnp.where(group == which, strip, 0.0)
        for step in (4, 8, 16, 32, 64):
            x = x + turn(x, step)
        return x

    levels = spread(20)
    v = spread(21)
    number = jnp.where(group >= LEVELS, group - LEVELS, group).astype(F32)
    wet = jnp.where((number < levels) & (group < PLANES), 1.0, 0.0)
    x = jnp.where(group < PLANES, strip, 0.0)
    open_e = wet * turn(wet, LANES - 1)
    wet_n = pltpu.roll(wet, rows - 1, 0)
    open_n = wet * wet_n
    flux_e = open_e * (turn(x, LANES - 1) - x)
    flux_n = open_n * (pltpu.roll(x, rows - 1, 0) - x)
    lap = flux_e - turn(flux_e, 1) + flux_n - pltpu.roll(flux_n, 1, 0)
    seam = jnp.where(phase == 1, flux_e, 0.0)
    added = seam - turn(seam, 1)
    base = jnp.where(phase == 1, lap, added)
    other = jnp.where(phase == 1, turn(lap, LANES - 1), turn(added, LANES - 1))
    face = 0.5 * (v + turn(v, LANES - 1)) * open_e
    flux_e = jnp.where(phase == 3, 0.0, face * (other - base))
    in_block = (ids != MARGIN - 1) & (ids != MARGIN + ROWS - 1)
    face = jnp.where(in_block, 0.5 * (v + pltpu.roll(v, rows - 1, 0)) * open_n, 0.0)
    flux_n = face * (pltpu.roll(added, rows - 1, 0) - added)
    second = flux_e - turn(flux_e, 1) + flux_n - pltpu.roll(flux_n, 1, 0)
    return wet * second, levels


def gram_pairs():
    return [(i, j) for i in range(SOLVE_ITERS) for j in range(i, SOLVE_ITERS + 1)]


def surface_kernel(
    tall, strips, mean, recv_a, recv_b,
    basis_out, flow, partial, col_patch, row_patch,
    state, height, flux, slope, basis, weights, diagonal,
):
    is_odd = odd("lon")
    rows = pl.ds(8, TALL)
    lanes = lane_ids(TALL)

    def received(start, count):
        here = pl.ds(start, count)
        got_a = recv_a[here, :]
        got_b = recv_b[here, :]
        return jnp.where(is_odd, got_b, got_a), jnp.where(is_odd, got_a, got_b)

    def ghost(east, west, f):
        return jnp.where(
            lane_ids(east.shape[0]) < 64, turn(east, (LANES - 32 * f) % LANES), turn(west, (96 - 32 * f) % LANES)
        )

    from_east, from_west = received(TALL, TALL)
    for f in range(3):
        state[f, 0, rows, :] = tall[pl.ds(f * TALL, TALL), :]
        state[f, 1, rows, :] = ghost(from_east, from_west, f)
    last = lanes == LANES - 1
    first = lanes == 0

    def lane_sides(a, b):
        n = a.shape[0]
        ea, eb, wa, wb = turn(a, LANES - 1), turn(b, LANES - 1), turn(a, 1), turn(b, 1)
        return (
            (jnp.where(last[0:n], eb, ea), jnp.where(last[0:n], ea, eb)),
            (jnp.where(first[0:n], wb, wa), jnp.where(first[0:n], wa, wb)),
        )

    own = tall[pl.ds(3 * TALL, TALL), :]
    phase = lanes & 3
    from_east, from_west = received(0, TALL)
    patches = []
    for side, strip in enumerate((jnp.where(phase < 2, own, from_east), jnp.where(phase < 2, from_west, own))):
        change, levels = column_strip(strip)
        patches.append(change)
        for comp in range(2):
            total = jnp.where((lanes >= 40 * comp) & (lanes < 40 * comp + 40), change, 0.0)
            for step in (4, 8, 16, 32, 64):
                total = total + turn(total, step)
            total = turn(total / jnp.maximum(levels, 1.0), 2)
            for half in range(2):
                here = lanes >= LANES - 2 if half == side else lanes < 2
                state[comp, half, rows, :] = state[comp, half, rows, :] - jnp.where(here, total, 0.0)
    patch = jnp.where(phase < 2, patches[0], patches[1])
    col_patch[...] = patch[MARGIN : MARGIN + ROWS]
    number = lax.broadcasted_iota(jnp.int32, (STRIP, LANES), 0)
    level_of_row = jnp.where(number >= LEVELS, number - LEVELS, number).astype(F32)
    is_plane = number < PLANES
    not_last = lane_ids(STRIP) < LANES - 1
    for s in range(2):
        from_east, from_west = received(2 * TALL + s * STRIP, STRIP)
        x, wet, v, deep = [], [], [], []
        for r in range(4):
            centre = strips[pl.ds((4 * s + r) * STRIP, STRIP), :]
            both = (centre, ghost(from_east, from_west, r))
            deep.append([b[20:21] for b in both])
            v.append([jnp.broadcast_to(b[21:22], (STRIP, LANES)) for b in both])
            wet.append([jnp.where(is_plane & (level_of_row < b[20:21]), 1.0, 0.0) for b in both])
            x.append([jnp.where(is_plane, b, 0.0) for b in both])
        half_range = range(2)
        lap = {}
        added = {}
        seam = [wet[1][h] * wet[2][h] * (x[2][h] - x[1][h]) for h in half_range]
        added[1] = seam
        added[2] = [-t for t in seam]
        along = {}
        for r in (1, 2):
            x_e = lane_sides(*x[r])[0]
            wet_e = lane_sides(*wet[r])[0]
            v_e = lane_sides(*v[r])[0]
            added_e = lane_sides(*added[r])[0]
            open_e = [wet[r][h] * wet_e[h] for h in half_range]
            edge = [open_e[h] * (x_e[h] - x[r][h]) for h in half_range]
            edge_w = lane_sides(*edge)[1]
            lap[r] = [
                edge[h]
                - edge_w[h]
                + wet[r][h] * (wet[r + 1][h] * (x[r + 1][h] - x[r][h]) + wet[r - 1][h] * (x[r - 1][h] - x[r][h]))
                for h in half_range
            ]
            edge = [
                jnp.where(not_last, 0.5 * (v[r][h] + v_e[h]) * open_e[h] * (added_e[h] - added[r][h]), 0.0)
                for h in half_range
            ]
            edge_w = lane_sides(*edge)[1]
            along[r] = [edge[h] - edge_w[h] for h in half_range]
        for h in half_range:
            face = [0.5 * (v[r][h] + v[r + 1][h]) * wet[r][h] * wet[r + 1][h] for r in range(3)]
            across = (face[0] * added[1][h], face[1] * (lap[2][h] - lap[1][h]), -face[2] * added[2][h])
            second = (
                across[0],
                across[1] - across[0] + along[1][h],
                across[2] - across[1] + along[2][h],
                -across[2],
            )
            for r in range(4):
                change = wet[r][h] * second[r]
                if h == 0 and r >= 2:
                    row_patch[pl.ds((2 * s + r - 2) * STRIP, STRIP), :] = change
                where = 8 + MARGIN + ((ROWS + 1 - r) if s == 0 else (r - 2))
                for comp in range(2):
                    mine = (number >= comp * LEVELS) & (number < (comp + 1) * LEVELS)
                    total = jnp.sum(jnp.where(mine, change, 0.0), axis=0, keepdims=True)
                    total = total / jnp.maximum(deep[r][h], 1.0)
                    state[comp, h, where : where + 1, :] = state[comp, h, where : where + 1, :] - total
    for comp in range(2):
        here = pl.ds(comp * ROWS, ROWS)
        started = state[comp, 0, pl.ds(8 + MARGIN, ROWS), :] - tall[pl.ds(comp * TALL + MARGIN, ROWS), :]
        flow[here, :] = -(started + mean[here, :])

    for half in range(2):
        slope[half, rows, :] = jnp.where(state[2, half, rows, :] > 0.0, SLOPE, 0.0)
        height[half, rows, :] = jnp.zeros((TALL, LANES), F32)

    def subcycle(step, carry):
        for half in range(2):
            flux[half, rows, :] = state[2, half, rows, :] * state[1, half, rows, :]
        east, west = lane_sides(*(state[2, half, rows, :] * state[0, half, rows, :] for half in range(2)))
        for half in range(2):
            divergence = (east[half] - west[half]) + (flux[half, pl.ds(9, TALL), :] - flux[half, pl.ds(7, TALL), :])
            height[half, rows, :] = height[half, rows, :] - slope[half, rows, :] * divergence
        east, west = lane_sides(height[0, rows, :], height[1, rows, :])
        for half in range(2):
            state[0, half, rows, :] = state[0, half, rows, :] - slope[half, rows, :] * (east[half] - west[half])
            state[1, half, rows, :] = state[1, half, rows, :] - slope[half, rows, :] * (
                height[half, pl.ds(9, TALL), :] - height[half, pl.ds(7, TALL), :]
            )
        return carry

    lax.fori_loop(0, SUBCYCLES, subcycle, 0)
    for comp in range(2):
        here = pl.ds(comp * ROWS, ROWS)
        flow[here, :] = flow[here, :] + state[comp, 0, pl.ds(8 + MARGIN, ROWS), :]
    scale = 2.0 / RADIUS
    short = ROWS + 16
    base = MARGIN

    def nine(read):
        out = [[], []]
        for off in (0, 1, -1):
            a, b = read(0, pl.ds(base + off, short)), read(1, pl.ds(base + off, short))
            east, west = lane_sides(a, b)
            for half, centre in enumerate((a, b)):
                out[half] += [centre, east[half], west[half]]
        return out

    around = nine(lambda half, where: state[2, half, where, :])
    for half in range(2):
        d = around[half][0]
        wet = d > 0.0
        total = jnp.where(wet, 0.05, 1.0)
        for n in range(1, 9):
            factor = 0.5 if n in (1, 2, 3, 6) else 0.25
            w = jnp.where(wet & (around[half][n] > 0.0), factor * (d + around[half][n]), 0.0)
            weights[n - 1, half] = scale * w
            total += w
        diagonal[half] = scale * (total - CENTRE)
        basis[0, half, pl.ds(base, short), :] = height[half, pl.ds(base, short), :]

    def applied(source):
        around = nine(lambda half, where: basis[source, half, where, :])
        out = []
        for half in range(2):
            total = diagonal[half] * around[half][0]
            for n in range(1, 9):
                total -= weights[n - 1, half] * around[half][n]
            out.append(total)
        return out

    for half, x in enumerate(applied(0)):
        basis[1, half, pl.ds(base, short), :] = 0.5 * x

    def next_basis(k, carry):
        for half, x in enumerate(applied(k)):
            basis[k + 1, half, pl.ds(base, short), :] = x - basis[k - 1, half, pl.ds(base, short), :]
        return carry

    lax.fori_loop(1, SOLVE_ITERS, next_basis, 0)
    lane = lane_ids(1)
    row = jnp.zeros((1, LANES), F32)
    mine = pl.ds(8 + MARGIN, ROWS)
    for n, (i, j) in enumerate(gram_pairs()):
        product = basis[i, 0, mine, :] * basis[j, 0, mine, :]
        row = jnp.where(lane == n, jnp.sum(jnp.sum(product, axis=0, keepdims=True), axis=1, keepdims=True), row)
    partial[...] = jnp.broadcast_to(row, partial.shape)
    for i in range(SOLVE_ITERS):
        for half in range(2):
            basis_out[i, half] = basis[i, half, pl.ds(base, short), :]


def solve_coefficients(gram):
    half = 0.5 * RADIUS

    def image_of(d):
        out = [None] * (len(d) + 1)

        def add(n, term):
            out[n] = term if out[n] is None else out[n] + term

        for j, value in enumerate(d):
            add(j, CENTRE * value)
            if j == 0:
                add(1, RADIUS * value)
            else:
                add(j + 1, half * value)
                add(j - 1, half * value)
        return out

    def inner(a, b):
        total = None
        for i, x in enumerate(a):
            for j, y in enumerate(b):
                term = x * y * gram[(min(i, j), max(i, j))]
                total = term if total is None else total + term
        return total

    one = jnp.ones((8, LANES), F32)
    residual, direction, surface = [one], [one], [0.0 * one]
    norm = gram[(0, 0)]
    for iteration in range(SOLVE_ITERS):
        image = image_of(direction)
        step = norm / inner(direction, image)
        surface = [a + step * b for a, b in zip(surface, direction)] + [0.0 * one]
        if iteration == SOLVE_ITERS - 1:
            break
        residual = [(residual[n] if n < len(residual) else 0.0) - step * x for n, x in enumerate(image)]
        fresh = inner(residual, residual)
        ratio = fresh / norm
        direction = [x + (ratio * direction[n] if n < len(direction) else 0.0) for n, x in enumerate(residual)]
        norm = fresh
    return surface[:SOLVE_ITERS]


def final_kernel(gathered, basis, flow, star, lev, col_patch, row_patch, velocity_out, surface_out, pad, change):
    sums = jnp.sum(gathered[...], axis=0, keepdims=True)
    lane = lane_ids(1)
    gram = {}
    for n, pair in enumerate(gram_pairs()):
        value = jnp.sum(jnp.where(lane == n, sums, 0.0), axis=1, keepdims=True)
        gram[pair] = jnp.broadcast_to(value, (8, LANES))
    coefficients = [c[0:1] for c in solve_coefficients(gram)]
    for half in range(2):
        total = coefficients[0] * basis[0, half]
        for i in range(1, SOLVE_ITERS):
            total += coefficients[i] * basis[i, half]
        pad[half] = total
    mine = pl.ds(8, ROWS)
    centre = pad[0, mine, :]
    ghost = pad[1, mine, :]
    surface_out[...] = centre
    lanes = lane_ids(ROWS)
    east = jnp.where(lanes == LANES - 1, turn(ghost, LANES - 1), turn(centre, LANES - 1))
    west = jnp.where(lanes == 0, turn(ghost, 1), turn(centre, 1))
    levels = lev[...]
    slope = jnp.where(levels > 0, SLOPE, 0.0)
    slopes = (east - west, pad[0, pl.ds(9, ROWS), :] - pad[0, pl.ds(7, ROWS), :])
    for comp in range(2):
        here = pl.ds(comp * ROWS, ROWS)
        change[comp] = flow[here, :] - slope * slopes[comp]

    rims = (lanes < 2) | (lanes >= LANES - 2)
    ids = row_ids(ROWS)

    def level_step(k, carry):
        wet = k < levels
        for comp in range(2):
            p = comp * LEVELS + k
            here = pl.ds(pl.multiple_of(p * ROWS, ROWS), ROWS)
            x = star[here, :] - jnp.where(rims, turn(col_patch[...], 126 - 4 * p), 0.0)
            for n, row in enumerate((ROWS - 1, ROWS - 2, 0, 1)):
                x = x - jnp.where(ids == row, row_patch[pl.ds(n * STRIP + p, 1), :], 0.0)
            velocity_out[here, :] = x + jnp.where(wet, change[comp], 0.0)
        return carry

    lax.fori_loop(0, LEVELS, level_step, 0)


def call(kernel, shapes, scratch, flops, *args):
    out = tuple(jax.ShapeDtypeStruct(s, F32) for s in shapes)
    moved = sum(4 * math.prod(a.shape) for a in args) + sum(4 * math.prod(s) for s in shapes)
    return pl.pallas_call(
        kernel,
        out_shape=out,
        scratch_shapes=[pltpu.VMEM(s, F32) for s in scratch],
        compiler_params=pltpu.CompilerParams(vmem_limit_bytes=32 * 1024 * 1024),
        cost_estimate=pl.CostEstimate(flops=flops, bytes_accessed=moved, transcendentals=0),
    )(*args)


def pair_tables(lon, lat):
    def index(i, j):
        return j * lat + i

    lat_a, lat_b, lon_a, lon_b = [], [], [], []
    for j in range(lon):
        for i in range(lat):
            lat_a.append((index(i, j), index(i ^ 1, j)))
            if i == lat - 1:
                lat_b.append((index(i, j), index(i, lon - 1 - j)))
            elif i > 0:
                lat_b.append((index(i, j), index(i + 1 if i % 2 else i - 1, j)))
            lon_a.append((index(i, j), index(i, j ^ 1)))
            lon_b.append((index(i, j), index(i, (j + 1 if j % 2 else j - 1) % lon)))
    return lat_a, lat_b, lon_a, lon_b


def per_device(lon, lat, tracers, velocity, active_levels, diffusivity, viscosity, ocean_depth, wind_forcing):
    lat_a, lat_b, lon_a, lon_b = pair_tables(lon, lat)

    def swap(x, pairs):
        return lax.ppermute(x, BOTH, pairs)

    block = (ROWS, LANES)
    tra = tracers.reshape(PLANES * ROWS, LANES)
    vel = velocity.reshape(PLANES * ROWS, LANES)
    wind = wind_forcing.reshape(2 * ROWS, LANES)
    rim = (RIMS, LANES)
    star, mean, fields, cols, north, south, send_a, send_b = call(
        block_kernel,
        [(PLANES * ROWS, LANES), (2 * ROWS, LANES), (3 * ROWS, LANES), block, rim, rim, (LAT_SEND, LANES), (LAT_SEND, LANES)],
        [(4,) + block, (4,) + block, (2,) + block, block],
        10**7,
        vel, tra, active_levels, viscosity, diffusivity, ocean_depth, wind,
    )
    got_b = swap(send_b, lat_b)
    got_a = swap(send_a, lat_a)
    tall, strips, tracer_rows, send_a, send_b = call(
        widen_kernel,
        [(4 * TALL, LANES), (8 * STRIP, LANES), (4 * STRIP, LANES), (LON_SEND, LANES), (LON_SEND, LANES)],
        [(TALL + 2 * STRIP, LANES)] * 2,
        10**6,
        fields, cols, diffusivity, north, south, got_a, got_b,
    )
    got_b = swap(send_b, lon_b)
    got_a = swap(send_a, lon_a)
    (tracers_out,) = call(
        tracer_kernel, [(PLANES * ROWS, LANES)], [block, (4,) + block, (4,) + block], 10**6,
        tra, active_levels, diffusivity, tracer_rows, got_a, got_b,
    )
    padded = (2, TALL + 16, LANES)
    short = (2, ROWS + 16, LANES)
    basis, flow, partial, col_patch, row_patch = call(
        surface_kernel,
        [(SOLVE_ITERS,) + short, (2 * ROWS, LANES), (lon * lat, LANES), block, (4 * STRIP, LANES)],
        [(3,) + padded, padded, padded, padded, (SOLVE_ITERS + 1,) + padded, (8,) + short, short],
        10**7,
        tall, strips, mean, got_a, got_b,
    )
    gathered = lax.all_to_all(partial, BOTH, 0, 0, tiled=True)
    velocity_out, surface = call(
        final_kernel, [(PLANES * ROWS, LANES), block], [short, (2,) + block], 10**6,
        gathered, basis, flow, star, active_levels, col_patch, row_patch,
    )
    return tracers_out.reshape(tracers.shape), velocity_out.reshape(velocity.shape), surface


def solution(mesh):
    placed = (
        P(None, None, "lat", "lon"),
        P(None, None, "lat", "lon"),
        P("lat", "lon"),
        P("lat", "lon"),
        P("lat", "lon"),
        P("lat", "lon"),
        P(None, "lat", "lon"),
    )
    return jax.shard_map(
        functools.partial(per_device, mesh.shape["lon"], mesh.shape["lat"]),
        mesh=mesh,
        in_specs=placed,
        out_specs=(P(None, None, "lat", "lon"), P(None, None, "lat", "lon"), P("lat", "lon")),
        check_vma=False,
    )
```

time: 72.8 us -> 58 us (0.80)
  starting transfers between devices: 38.4 us -> 26.4 us
  waiting for transfers between devices: 13.8 us -> 11.2 us
  Pallas kernels: 14.8 us -> 13 us
  local copies, waits for them, and re-layouts: 4.46 us -> 6.05 us
    ppermute x8 -> x4, starting transfers between devices: 17 us -> 6.54 us  [swap(): return lax.ppermute(x, BOTH, pairs)]
    ppermute x8 -> x4, waiting for transfers between devices: 6.61 us -> 4 us  [swap(): return lax.ppermute(x, BOTH, pairs)]
    pallas_call x7 -> x5, Pallas kernels: 14.8 us -> 13 us  [call(): pl.pallas_call(kernel, out_shape=out, scratch_shapes=[pltpu.VMEM(s, F32)...]
    unnamed x22 -> x20, local copies, waits for them, and re-layouts: 4.46 us -> 6.05 us
    all_to_all x1, starting transfers between devices: 21.3 us -> 19.9 us  [per_device(): gathered = lax.all_to_all(partial, BOTH, 0, 0, tiled=True)]
  transfers between devices with their start and end apart: 9 -> 5, of which waited for: 6 -> 3; matrix products, arithmetic and copies ran while one was open for 0% -> 0% of each run, Pallas kernels for 3% -> 4%
where the time goes in v2:
time: 58 us; the launch traced here: 57.4 us
  starting transfers between devices  26.4 us (46%)
  Pallas kernels  13 us (22%)
  waiting for transfers between devices  11.2 us (19%)
  local copies, waits for them, and re-layouts  6.05 us (10%)
  between operations  0.71 us (1%)
    all_to_all x1, starting transfers between devices, per_device(): gathered = lax.all_to_all(partial, BOTH, 0, 0, tiled=True)  19.9 us
    pallas_call x5, Pallas kernels, call(): pl.pallas_call(kernel, out_shape=out, scratch_shapes=[pltpu.VMEM(s, F32)...  13 us
    all_to_all x1, waiting for transfers between devices, per_device(): gathered = lax.all_to_all(partial, BOTH, 0, 0, tiled=True)  7.23 us
    ppermute x4, starting transfers between devices, swap(): return lax.ppermute(x, BOTH, pairs)  6.54 us
    unnamed x20, local copies, waits for them, and re-layouts  6.05 us
    ppermute x4, waiting for transfers between devices, swap(): return lax.ppermute(x, BOTH, pairs)  4 us
  transfers between devices with their start and end apart: 5, of which 3 were waited for; matrix products, arithmetic and copies ran while one was open for 0% of the time, Pallas kernels for 4%

profile of v2, /device:TPU:1, one launch (start us, length us, event | category | flops | bytes accessed | tf_op | source)
XLA Modules:
  0.0 57.4 jit_solution(2797573989122472668)
XLA Ops:
  0.6 0.0 copy-start
  0.6 1.1 %copy-done = f32[2,10,64,128]{3,2,1,0:T(8,128)S(1)} copy-done((f32[2,10,64,128]{3,2,1,0:T(8,128)S(1)}, f32[2,10,64,128]{3,2,1,0:T(8,128)}, u32[]{:S(2)}) %copy-start) | copy-done | bytes 655384
  1.7 1.1 %copy-done.2 = f32[2,10,64,128]{3,2,1,0:T(8,128)S(1)} copy-done((f32[2,10,64,128]{3,2,1,0:T(8,128)S(1)}, f32[2,10,64,128]{3,2,1,0:T(8,128)}, u32[]{:S(2)}) %copy-start.2) | copy-done | bytes 655384
  2.8 0.8 %copy-done.3 = f32[64,128]{1,0:T(8,128)S(1)} copy-done((f32[64,128]{1,0:T(8,128)S(1)}, f32[64,128]{1,0:T(8,128)}, u32[]{:S(2)}) %copy-start.3) | copy-done | bytes 32792
  3.6 0.8 %copy-done.5 = s32[64,128]{1,0:T(8,128)S(1)} copy-done((s32[64,128]{1,0:T(8,128)S(1)}, s32[64,128]{1,0:T(8,128)}, u32[]{:S(2)}) %copy-start.5) | copy-done | bytes 32792
  4.3 0.8 %copy-done.7 = f32[2,64,128]{2,1,0:T(8,128)S(1)} copy-done((f32[2,64,128]{2,1,0:T(8,128)S(1)}, f32[2,64,128]{2,1,0:T(8,128)}, u32[]{:S(2)}) %copy-start.7) | copy-done | bytes 65560
  5.2 0.8 %copy-done.8 = f32[64,128]{1,0:T(8,128)S(1)} copy-done((f32[64,128]{1,0:T(8,128)S(1)}, f32[64,128]{1,0:T(8,128)}, u32[]{:S(2)}) %copy-start.8) | copy-done | bytes 32792
  5.9 0.8 %copy-done.9 = f32[64,128]{1,0:T(8,128)S(1)} copy-done((f32[64,128]{1,0:T(8,128)S(1)}, f32[64,128]{1,0:T(8,128)}, u32[]{:S(2)}) %copy-start.9) | copy-done | bytes 32792
  6.7 2.4 %shard_map.94 = (f32[1280,128]{1,0:T(8,128)S(1)}, f32[128,128]{1,0:T(8,128)S(1)}, f32[192,128]{1,0:T(8,128)S(1)}, f32[64,128]{1,0:T(8,128)S(1)}, f32[72,128]{1,0...) custom-call(f32[1280,128]{1,0:T(8,128)S(1)} %bitcast.11, ...), custom_call_target="tpu_custom_call" | custom-call | flops 10000000 | bytes 2605056 | tf_op jit(solution)/shard_map/pallas_call | solution.py:586
  9.1 0.0 copy-start.1
  9.1 2.1 %collective-permute-start = (f32[168,128]{1,0:T(8,128)S(1)}, f32[168,128]{1,0:T(8,128)S(1)}, u32[]{:S(2)}, u32[]{:S(2)}) collective-permute-start(f32[168,128]{1,0:T(8,128)S(1)} %get-tuple-element.27), channel_id=1, source_target_pairs={{0,1},{1,0},{2,3},{3,2},{4,5},{5,4},{6,7},{7,6},{8,9},{9,8},{10,11... | collective-permute-start | bytes 258056 | tf_op jit(solution)/shard_map/ppermute | solution.py:616
  11.2 0.7 %collective-permute-start.1 = (f32[168,128]{1,0:T(8,128)S(1)}, f32[168,128]{1,0:T(8,128)S(1)}, u32[]{:S(2)}, u32[]{:S(2)}) collective-permute-start(f32[168,128]{1,0:T(8,128)S(1)} %get-tuple-element.28), channel_id=1, source_target_pairs={{1,2},{2,1},{3,4},{4,3},{5,6},{6,5},{7,127},{9,10},{10,9},{11,12},... | collective-permute-start | bytes 258056 | tf_op jit(solution)/shard_map/ppermute | solution.py:616
  11.9 1.2 %collective-permute-done.recv_a = f32[168,128]{1,0:T(8,128)S(1)} collective-permute-done((f32[168,128]{1,0:T(8,128)S(1)}, f32[168,128]{1,0:T(8,128)S(1)}, u32[]{:S(2)}, u32[]{:S(2)}) %collective-permute-start) | collective-permute-done | bytes 86048 | tf_op jit(solution)/shard_map/ppermute | solution.py:616
  13.1 0.0 collective-permute-done.1.recv_b
  13.1 0.2 shard_map.95
  13.3 2.1 %collective-permute-start.2 = (f32[272,128]{1,0:T(8,128)S(1)}, f32[272,128]{1,0:T(8,128)S(1)}, u32[]{:S(2)}, u32[]{:S(2)}) collective-permute-start(f32[272,128]{1,0:T(8,128)S(1)} %get-tuple-element.30), channel_id=1, source_target_pairs={{0,8},{1,9},{2,10},{3,11},{4,12},{5,13},{6,14},{7,15},{8,0},{9,1},... | collective-permute-start | bytes 417800 | tf_op jit(solution)/shard_map/ppermute | solution.py:616
  15.4 1.7 %collective-permute-start.3 = (f32[272,128]{1,0:T(8,128)S(1)}, f32[272,128]{1,0:T(8,128)S(1)}, u32[]{:S(2)}, u32[]{:S(2)}) collective-permute-start(f32[272,128]{1,0:T(8,128)S(1)} %get-tuple-element.31), channel_id=1, source_target_pairs={{0,120},{1,121},{2,122},{3,123},{4,124},{5,125},{6,126},{7,127},{8... | collective-permute-start | bytes 417800 | tf_op jit(solution)/shard_map/ppermute | solution.py:616
  17.1 0.0 collective-permute-done.2.recv_a
  17.1 2.8 %collective-permute-done.3.recv_b = f32[272,128]{1,0:T(8,128)S(1)} collective-permute-done((f32[272,128]{1,0:T(8,128)S(1)}, f32[272,128]{1,0:T(8,128)S(1)}, u32[]{:S(2)}, u32[]{:S(2)}) %collective-permute-start.3) | collective-permute-done | bytes 139296 | tf_op jit(solution)/shard_map/ppermute | solution.py:616
  19.8 6.0 %shard_map.97 = (f32[4,2,80,128]{3,2,1,0:T(8,128)S(1)}, f32[128,128]{1,0:T(8,128)S(1)}, f32[128,128]{1,0:T(8,128)}, f32[64,128]{1,0:T(8,128)S(1)}, f32[96,128]{1,0:T(8,128)S(1)}) custom-call(f32[448,128]{1,0:T(8,128)S(1)} %get-tuple-element.32.tall, f32[192,128]{1,0:T(8,128)S(1)} %get-tuple-element.33.strips, f32[128,128]{1,0:T(8,128)S(1)} %get-tuple-element.34.mean, ...), custom_call_target="tpu_custom_call" | custom-call | flops 10000000 | bytes 1212416 | tf_op jit(solution)/shard_map/pallas_call | solution.py:586
  25.9 19.9 %all-to-all-start = ((f32[128,1,128]{2,1,0:T(1,128)}), f32[128,1,128]{2,1,0:T(1,128)S(1)}, u32[]{:S(2)}, u32[]{:S(2)}) async-start(f32[128,1,128]{2,1,0:T(1,128)} %bitcast.5), calls=%async_computation | async-start | bytes 131072 | tf_op jit(solution)/shard_map/all_to_all | solution.py:654
  45.8 2.3 %shard_map.96 = f32[1280,128]{1,0:T(8,128)} custom-call(f32[1280,128]{1,0:T(8,128)S(1)} %bitcast.10, s32[64,128]{1,0:T(8,128)S(1)} %copy-done.6, f32[64,128]{1,0:T(8,128)S(1)} %copy-done.4, f32[96,128]{1,0:T(8,128)S(1)} %get-tuple-element.29.tracer_rows, f32[272,128]{1,0:T(8,128)S(1)} %collective-permute-done.2.recv_a, ...), custom_call_target="tpu_custom_call" | custom-call | flops 1000000 | bytes 1703936 | tf_op jit(solution)/shard_map/pallas_call | solution.py:586
  48.1 7.2 %all-to-all-done = f32[128,1,128]{2,1,0:T(1,128)S(1)} async-done(((f32[128,1,128]{2,1,0:T(1,128)}), f32[128,1,128]{2,1,0:T(1,128)S(1)}, u32[]{:S(2)}, u32[]{:S(2)}) %all-to-all-start) | async-done | bytes 65568 | tf_op jit(solution)/shard_map/all_to_all | solution.py:654
  55.3 2.1 %shard_map.98 = (f32[1280,128]{1,0:T(8,128)}, f32[64,128]{1,0:T(8,128)}) custom-call(f32[128,128]{1,0:T(8,128)S(1)} %bitcast.12, f32[4,2,80,128]{3,2,1,0:T(8,128)S(1)} %get-tuple-element.36.basis, f32[128,128]{1,0:T(8,128)S(1)} %get-tuple-element.37.flow, f32[1280,128]{1,0:T(8,128)S(1)} %get-tuple-element.38.star, s32[64,128]{1,0:T(8,128)S(1)} %copy-done.6, ...), custom_call_target="tpu_custom_call" | custom-call | flops 1000000 | bytes 1916928 | tf_op jit(solution)/shard_map/pallas_call | solution.py:586
  (11 shorter events, 0.0 us)
Async XLA Ops:
  0.6 1.1 %copy-start = (f32[2,10,64,128]{3,2,1,0:T(8,128)S(1)}, f32[2,10,64,128]{3,2,1,0:T(8,128)}, u32[]{:S(2)}) copy-start(f32[2,10,64,128]{3,2,1,0:T(8,128)} %param.7) | copy-start | bytes 1966084
  1.7 1.1 %copy-start.2 = (f32[2,10,64,128]{3,2,1,0:T(8,128)S(1)}, f32[2,10,64,128]{3,2,1,0:T(8,128)}, u32[]{:S(2)}) copy-start(f32[2,10,64,128]{3,2,1,0:T(8,128)} %param.8) | copy-start | bytes 1966084
  2.8 0.8 %copy-start.3 = (f32[64,128]{1,0:T(8,128)S(1)}, f32[64,128]{1,0:T(8,128)}, u32[]{:S(2)}) copy-start(f32[64,128]{1,0:T(8,128)} %diff.5) | copy-start | bytes 98308
  3.6 0.8 %copy-start.5 = (s32[64,128]{1,0:T(8,128)S(1)}, s32[64,128]{1,0:T(8,128)}, u32[]{:S(2)}) copy-start(s32[64,128]{1,0:T(8,128)} %lev.5) | copy-start | bytes 98308
  4.3 0.8 %copy-start.7 = (f32[2,64,128]{2,1,0:T(8,128)S(1)}, f32[2,64,128]{2,1,0:T(8,128)}, u32[]{:S(2)}) copy-start(f32[2,64,128]{2,1,0:T(8,128)} %param.13) | copy-start | bytes 196612
  5.2 0.8 %copy-start.8 = (f32[64,128]{1,0:T(8,128)S(1)}, f32[64,128]{1,0:T(8,128)}, u32[]{:S(2)}) copy-start(f32[64,128]{1,0:T(8,128)} %visc.1) | copy-start | bytes 98308
  5.9 0.8 %copy-start.9 = (f32[64,128]{1,0:T(8,128)S(1)}, f32[64,128]{1,0:T(8,128)}, u32[]{:S(2)}) copy-start(f32[64,128]{1,0:T(8,128)} %depth.1) | copy-start | bytes 98308
  9.1 36.7 %copy-start.1 = (f32[2,10,64,128]{3,2,1,0:T(8,128)S(1)}, f32[2,10,64,128]{3,2,1,0:T(8,128)}, u32[]{:S(2)}) copy-start(f32[2,10,64,128]{3,2,1,0:T(8,128)} %param.7) | copy-start | bytes 1966084
  9.1 4.0 %collective-permute-start = (f32[168,128]{1,0:T(8,128)S(1)}, f32[168,128]{1,0:T(8,128)S(1)}, u32[]{:S(2)}, u32[]{:S(2)}) collective-permute-start(f32[168,128]{1,0:T(8,128)S(1)} %get-tuple-element.27), channel_id=1, source_target_pairs={{0,1},{1,0},{2,3},{3,2},{4,5},{5,4},{6,7},{7,6},{8,9},{9,8},{10,11... | collective-permute-start | bytes 258056 | tf_op jit(solution)/shard_map/ppermute | solution.py:616
  11.2 1.9 %collective-permute-start.1 = (f32[168,128]{1,0:T(8,128)S(1)}, f32[168,128]{1,0:T(8,128)S(1)}, u32[]{:S(2)}, u32[]{:S(2)}) collective-permute-start(f32[168,128]{1,0:T(8,128)S(1)} %get-tuple-element.28), channel_id=1, source_target_pairs={{1,2},{2,1},{3,4},{4,3},{5,6},{6,5},{7,127},{9,10},{10,9},{11,12},... | collective-permute-start | bytes 258056 | tf_op jit(solution)/shard_map/ppermute | solution.py:616
  13.3 3.8 %collective-permute-start.2 = (f32[272,128]{1,0:T(8,128)S(1)}, f32[272,128]{1,0:T(8,128)S(1)}, u32[]{:S(2)}, u32[]{:S(2)}) collective-permute-start(f32[272,128]{1,0:T(8,128)S(1)} %get-tuple-element.30), channel_id=1, source_target_pairs={{0,8},{1,9},{2,10},{3,11},{4,12},{5,13},{6,14},{7,15},{8,0},{9,1},... | collective-permute-start | bytes 417800 | tf_op jit(solution)/shard_map/ppermute | solution.py:616
  15.4 4.5 %collective-permute-start.3 = (f32[272,128]{1,0:T(8,128)S(1)}, f32[272,128]{1,0:T(8,128)S(1)}, u32[]{:S(2)}, u32[]{:S(2)}) collective-permute-start(f32[272,128]{1,0:T(8,128)S(1)} %get-tuple-element.31), channel_id=1, source_target_pairs={{0,120},{1,121},{2,122},{3,123},{4,124},{5,125},{6,126},{7,127},{8... | collective-permute-start | bytes 417800 | tf_op jit(solution)/shard_map/ppermute | solution.py:616
  25.9 19.9 %copy-start.4 = (f32[64,128]{1,0:T(8,128)S(1)}, f32[64,128]{1,0:T(8,128)}, u32[]{:S(2)}) copy-start(f32[64,128]{1,0:T(8,128)} %diff.5) | copy-start | bytes 98308
  25.9 19.9 %copy-start.6 = (s32[64,128]{1,0:T(8,128)S(1)}, s32[64,128]{1,0:T(8,128)}, u32[]{:S(2)}) copy-start(s32[64,128]{1,0:T(8,128)} %lev.5) | copy-start | bytes 98308
  25.9 29.4 %all-to-all-start = ((f32[128,1,128]{2,1,0:T(1,128)}), f32[128,1,128]{2,1,0:T(1,128)S(1)}, u32[]{:S(2)}, u32[]{:S(2)}) async-start(f32[128,1,128]{2,1,0:T(1,128)} %bitcast.5), calls=%async_computation | async-start | bytes 131072 | tf_op jit(solution)/shard_map/all_to_all | solution.py:654

commit v3 on v2

--- a/solution.py
+++ b/solution.py
@@ -18,8 +18,8 @@
 TALL = ROWS + 2 * MARGIN
 RIM = 32
 SLOPE = 0.15
-CENTRE = 9.0
-RADIUS = 9.1
+CENTRE = 5.0
+RADIUS = 5.0
 F32 = jnp.float32
 BOTH = ("lon", "lat")
 
@@ -72,10 +72,16 @@
 
 
 def block_kernel(
-    vel, tra, lev, visc, diff, depth, wind,
+    vel_far, tra_far, lev_far, visc_far, diff_far, depth_far, wind_far,
     star, mean, fields, cols, north, south, send_a, send_b,
-    faces, face_levels, sums, turning,
+    faces, face_levels, sums, turning, vel, tra, visc, diff, depth, wind, lev, done,
 ):
+    pairs = ((lev_far, lev), (visc_far, visc), (vel_far, vel), (tra_far, tra), (wind_far, wind), (depth_far, depth), (diff_far, diff))
+    copies = [pltpu.make_async_copy(far, near, done.at[n]) for n, (far, near) in enumerate(pairs)]
+    for copy in copies:
+        copy.start()
+    for copy in copies[:2]:
+        copy.wait()
     lanes = lane_ids(ROWS)
     ids = row_ids(ROWS)
     levels = lev[...].astype(F32)
@@ -89,6 +95,8 @@
     sums[...] = jnp.zeros((2, ROWS, LANES), F32)
     acc = jnp.where((lanes >> 2) == 20, turn(levels, 82), 0.0)
     cols[...] = jnp.where((lanes >> 2) == 21, turn(v, 86), acc)
+    for copy in copies[2:]:
+        copy.wait()
 
     def level_step(k, carry):
         level = k.astype(F32)
@@ -417,19 +425,24 @@
         slope[half, rows, :] = jnp.where(state[2, half, rows, :] > 0.0, SLOPE, 0.0)
         height[half, rows, :] = jnp.zeros((TALL, LANES), F32)
 
+    halves = range(2)
+
     def subcycle(step, carry):
-        for half in range(2):
-            flux[half, rows, :] = state[2, half, rows, :] * state[1, half, rows, :]
-        east, west = lane_sides(*(state[2, half, rows, :] * state[0, half, rows, :] for half in range(2)))
-        for half in range(2):
-            divergence = (east[half] - west[half]) + (flux[half, pl.ds(9, TALL), :] - flux[half, pl.ds(7, TALL), :])
-            height[half, rows, :] = height[half, rows, :] - slope[half, rows, :] * divergence
-        east, west = lane_sides(height[0, rows, :], height[1, rows, :])
-        for half in range(2):
-            state[0, half, rows, :] = state[0, half, rows, :] - slope[half, rows, :] * (east[half] - west[half])
-            state[1, half, rows, :] = state[1, half, rows, :] - slope[half, rows, :] * (
-                height[half, pl.ds(9, TALL), :] - height[half, pl.ds(7, TALL), :]
-            )
+        for tile in range(8, 8 + TALL, 8):
+            here, above, below = (pl.ds(tile + off, 8) for off in (0, 1, -1))
+            east, west = lane_sides(*(state[2, h, here, :] * state[0, h, here, :] for h in halves))
+            for h in halves:
+                north = state[2, h, above, :] * state[1, h, above, :]
+                south = state[2, h, below, :] * state[1, h, below, :]
+                divergence = (east[h] - west[h]) + (north - south)
+                height[h, here, :] = height[h, here, :] - slope[h, here, :] * divergence
+        for tile in range(8, 8 + TALL, 8):
+            here, above, below = (pl.ds(tile + off, 8) for off in (0, 1, -1))
+            east, west = lane_sides(height[0, here, :], height[1, here, :])
+            for h in halves:
+                factor = slope[h, here, :]
+                state[0, h, here, :] = state[0, h, here, :] - factor * (east[h] - west[h])
+                state[1, h, here, :] = state[1, h, here, :] - factor * (height[h, above, :] - height[h, below, :])
         return carry
 
     lax.fori_loop(0, SUBCYCLES, subcycle, 0)
@@ -440,44 +453,52 @@
     short = ROWS + 16
     base = MARGIN
 
-    def nine(read):
+    tiles = range(0, short, 8)
+
+    def nine(read, tile):
         out = [[], []]
         for off in (0, 1, -1):
-            a, b = read(0, pl.ds(base + off, short)), read(1, pl.ds(base + off, short))
+            a, b = (read(h, pl.ds(base + tile + off, 8)) for h in halves)
             east, west = lane_sides(a, b)
-            for half, centre in enumerate((a, b)):
-                out[half] += [centre, east[half], west[half]]
+            for h, centre in enumerate((a, b)):
+                out[h] += [centre, east[h], west[h]]
         return out
 
-    around = nine(lambda half, where: state[2, half, where, :])
-    for half in range(2):
-        d = around[half][0]
-        wet = d > 0.0
-        total = jnp.where(wet, 0.05, 1.0)
-        for n in range(1, 9):
-            factor = 0.5 if n in (1, 2, 3, 6) else 0.25
-            w = jnp.where(wet & (around[half][n] > 0.0), factor * (d + around[half][n]), 0.0)
-            weights[n - 1, half] = scale * w
-            total += w
-        diagonal[half] = scale * (total - CENTRE)
-        basis[0, half, pl.ds(base, short), :] = height[half, pl.ds(base, short), :]
-
-    def applied(source):
-        around = nine(lambda half, where: basis[source, half, where, :])
+    for tile in tiles:
+        here = pl.ds(tile, 8)
+        around = nine(lambda h, where: state[2, h, where, :], tile)
+        for h in halves:
+            d = around[h][0]
+            wet = d > 0.0
+            total = jnp.where(wet, 0.05, 1.0)
+            for n in range(1, 9):
+                factor = 0.5 if n in (1, 2, 3, 6) else 0.25
+                w = jnp.where(wet & (around[h][n] > 0.0), factor * (d + around[h][n]), 0.0)
+                weights[n - 1, h, here, :] = scale * w
+                total += w
+            diagonal[h, here, :] = scale * (total - CENTRE)
+            basis[0, h, pl.ds(base + tile, 8), :] = height[h, pl.ds(base + tile, 8), :]
+
+    def applied(source, tile):
+        around = nine(lambda h, where: basis[source, h, where, :], tile)
         out = []
-        for half in range(2):
-            total = diagonal[half] * around[half][0]
+        for h in halves:
+            here = pl.ds(tile, 8)
+            total = diagonal[h, here, :] * around[h][0]
             for n in range(1, 9):
-                total -= weights[n - 1, half] * around[half][n]
+                total -= weights[n - 1, h, here, :] * around[h][n]
             out.append(total)
         return out
 
-    for half, x in enumerate(applied(0)):
-        basis[1, half, pl.ds(base, short), :] = 0.5 * x
+    for tile in tiles:
+        for h, x in enumerate(applied(0, tile)):
+            basis[1, h, pl.ds(base + tile, 8), :] = 0.5 * x
 
     def next_basis(k, carry):
-        for half, x in enumerate(applied(k)):
-            basis[k + 1, half, pl.ds(base, short), :] = x - basis[k - 1, half, pl.ds(base, short), :]
+        for tile in tiles:
+            here = pl.ds(base + tile, 8)
+            for h, x in enumerate(applied(k, tile)):
+                basis[k + 1, h, here, :] = x - basis[k - 1, h, here, :]
         return carry
 
     lax.fori_loop(1, SOLVE_ITERS, next_basis, 0)
@@ -536,7 +557,7 @@
     return surface[:SOLVE_ITERS]
 
 
-def final_kernel(gathered, basis, flow, star, lev, col_patch, row_patch, velocity_out, surface_out, pad, change):
+def final_kernel(gathered, basis, flow, star, lev, velocity_out, surface_out, pad, change):
     sums = jnp.sum(gathered[...], axis=0, keepdims=True)
     lane = lane_ids(1)
     gram = {}
@@ -563,30 +584,46 @@
         here = pl.ds(comp * ROWS, ROWS)
         change[comp] = flow[here, :] - slope * slopes[comp]
 
-    rims = (lanes < 2) | (lanes >= LANES - 2)
-    ids = row_ids(ROWS)
 
     def level_step(k, carry):
         wet = k < levels
         for comp in range(2):
-            p = comp * LEVELS + k
-            here = pl.ds(pl.multiple_of(p * ROWS, ROWS), ROWS)
-            x = star[here, :] - jnp.where(rims, turn(col_patch[...], 126 - 4 * p), 0.0)
-            for n, row in enumerate((ROWS - 1, ROWS - 2, 0, 1)):
+            here = pl.ds(pl.multiple_of((comp * LEVELS + k) * ROWS, ROWS), ROWS)
+            velocity_out[here, :] = star[here, :] + jnp.where(wet, change[comp], 0.0)
+        return carry
+
+    lax.fori_loop(0, LEVELS, level_step, 0)
+
+
+def patch_kernel(star, col_patch, row_patch, out):
+    lanes = lane_ids(ROWS)
+    rims = (lanes < 2) | (lanes >= LANES - 2)
+    ids = row_ids(8)
+
+    def plane(p, carry):
+        here = pl.ds(pl.multiple_of(p * ROWS, ROWS), ROWS)
+        out[here, :] = star[here, :] - jnp.where(rims, turn(col_patch[...], 126 - 4 * p), 0.0)
+        for first, pieces in ((ROWS - 8, ((7, 0), (6, 1))), (0, ((0, 2), (1, 3)))):
+            here = pl.ds(pl.multiple_of(p * ROWS + first, 8), 8)
+            x = out[here, :]
+            for row, n in pieces:
                 x = x - jnp.where(ids == row, row_patch[pl.ds(n * STRIP + p, 1), :], 0.0)
-            velocity_out[here, :] = x + jnp.where(wet, change[comp], 0.0)
+            out[here, :] = x
         return carry
 
-    lax.fori_loop(0, LEVELS, level_step, 0)
-
-
-def call(kernel, shapes, scratch, flops, *args):
+    lax.fori_loop(0, PLANES, plane, 0)
+
+
+def call(kernel, shapes, scratch, flops, *args, far=False):
     out = tuple(jax.ShapeDtypeStruct(s, F32) for s in shapes)
     moved = sum(4 * math.prod(a.shape) for a in args) + sum(4 * math.prod(s) for s in shapes)
+    if far:
+        args = [pltpu.with_memory_space_constraint(a, pltpu.HBM) for a in args]
     return pl.pallas_call(
         kernel,
         out_shape=out,
-        scratch_shapes=[pltpu.VMEM(s, F32) for s in scratch],
+        in_specs=[pl.BlockSpec(memory_space=pltpu.HBM if far else pltpu.VMEM)] * len(args),
+        scratch_shapes=[pltpu.VMEM(s, F32) if isinstance(s, tuple) else s for s in scratch],
         compiler_params=pltpu.CompilerParams(vmem_limit_bytes=32 * 1024 * 1024),
         cost_estimate=pl.CostEstimate(flops=flops, bytes_accessed=moved, transcendentals=0),
     )(*args)
@@ -623,9 +660,11 @@
     star, mean, fields, cols, north, south, send_a, send_b = call(
         block_kernel,
         [(PLANES * ROWS, LANES), (2 * ROWS, LANES), (3 * ROWS, LANES), block, rim, rim, (LAT_SEND, LANES), (LAT_SEND, LANES)],
-        [(4,) + block, (4,) + block, (2,) + block, block],
+        [(4,) + block, (4,) + block, (2,) + block, block, vel.shape, vel.shape, block, block, block, wind.shape,
+         pltpu.VMEM(block, jnp.int32), pltpu.SemaphoreType.DMA((7,))],
         10**7,
         vel, tra, active_levels, viscosity, diffusivity, ocean_depth, wind,
+        far=True,
     )
     got_b = swap(send_b, lat_b)
     got_a = swap(send_a, lat_a)
@@ -652,9 +691,10 @@
         tall, strips, mean, got_a, got_b,
     )
     gathered = lax.all_to_all(partial, BOTH, 0, 0, tiled=True)
+    (star,) = call(patch_kernel, [(PLANES * ROWS, LANES)], [], 10**6, star, col_patch, row_patch)
     velocity_out, surface = call(
         final_kernel, [(PLANES * ROWS, LANES), block], [short, (2,) + block], 10**6,
-        gathered, basis, flow, star, active_levels, col_patch, row_patch,
+        gathered, basis, flow, star, active_levels,
     )
     return tracers_out.reshape(tracers.shape), velocity_out.reshape(velocity.shape), surface
 

time: 58 us -> 51.3 us (0.88)
  local copies, waits for them, and re-layouts: 6.05 us -> 0.02 us
  waiting for transfers between devices: 11.2 us -> 9.66 us
  Pallas kernels: 13 us -> 14.5 us
    unnamed x20 -> x6, local copies, waits for them, and re-layouts: 6.05 us -> 0.02 us
    all_to_all x1, waiting for transfers between devices: 7.23 us -> 5.67 us  [per_device(): gathered = lax.all_to_all(partial, BOTH, 0, 0, tiled=True)]
    pallas_call x5 -> x6, Pallas kernels: 13 us -> 14.5 us  [call(): pl.pallas_call(kernel, out_shape=out, in_specs=[pl.BlockSpec(memory_space...]
  transfers between devices with their start and end apart: 5 -> 5, of which waited for: 3 -> 3; matrix products, arithmetic and copies ran while one was open for 0% -> 0% of each run, Pallas kernels for 4% -> 7%
where the time goes in v3:
time: 51.3 us; the launch traced here: 51.2 us
  starting transfers between devices  26.3 us (51%)
  Pallas kernels  14.5 us (28%)
  waiting for transfers between devices  9.66 us (19%)
  between operations  0.71 us (1%)
    all_to_all x1, starting transfers between devices, per_device(): gathered = lax.all_to_all(partial, BOTH, 0, 0, tiled=True)  19.8 us
    pallas_call x6, Pallas kernels, call(): pl.pallas_call(kernel, out_shape=out, in_specs=[pl.BlockSpec(memory_space...  14.5 us
    ppermute x4, starting transfers between devices, swap(): return lax.ppermute(x, BOTH, pairs)  6.54 us
    all_to_all x1, waiting for transfers between devices, per_device(): gathered = lax.all_to_all(partial, BOTH, 0, 0, tiled=True)  5.67 us
    ppermute x4, waiting for transfers between devices, swap(): return lax.ppermute(x, BOTH, pairs)  4 us
  transfers between devices with their start and end apart: 5, of which 3 were waited for; matrix products, arithmetic and copies ran while one was open for 0% of the time, Pallas kernels for 7%

profile of v3, /device:TPU:1, one launch (start us, length us, event | category | flops | bytes accessed | tf_op | source)
XLA Modules:
  0.0 51.2 jit_solution(16991168879311942872)
XLA Ops:
  0.6 0.0 copy-start.1
  0.6 3.6 %shard_map.94 = (f32[1280,128]{1,0:T(8,128)S(1)}, f32[128,128]{1,0:T(8,128)S(1)}, f32[192,128]{1,0:T(8,128)S(1)}, f32[64,128]{1,0:T(8,128)S(1)}, f32[72,128]{1,0...) custom-call(f32[1280,128]{1,0:T(8,128)} %bitcast.12, f32[1280,128]{1,0:T(8,128)} %bitcast.9, ...), custom_call_target="tpu_custom_call" | custom-call | flops 10000000 | bytes 2605056 | tf_op jit(solution)/shard_map/pallas_call | solution.py:622
  4.3 2.1 %collective-permute-start = (f32[168,128]{1,0:T(8,128)S(1)}, f32[168,128]{1,0:T(8,128)S(1)}, u32[]{:S(2)}, u32[]{:S(2)}) collective-permute-start(f32[168,128]{1,0:T(8,128)S(1)} %get-tuple-element.27), channel_id=1, source_target_pairs={{0,1},{1,0},{2,3},{3,2},{4,5},{5,4},{6,7},{7,6},{8,9},{9,8},{10,11... | collective-permute-start | bytes 258056 | tf_op jit(solution)/shard_map/ppermute | solution.py:653
  6.4 0.7 %collective-permute-start.1 = (f32[168,128]{1,0:T(8,128)S(1)}, f32[168,128]{1,0:T(8,128)S(1)}, u32[]{:S(2)}, u32[]{:S(2)}) collective-permute-start(f32[168,128]{1,0:T(8,128)S(1)} %get-tuple-element.28), channel_id=1, source_target_pairs={{1,2},{2,1},{3,4},{4,3},{5,6},{6,5},{7,127},{9,10},{10,9},{11,12},... | collective-permute-start | bytes 258056 | tf_op jit(solution)/shard_map/ppermute | solution.py:653
  7.0 1.2 %collective-permute-done.recv_a = f32[168,128]{1,0:T(8,128)S(1)} collective-permute-done((f32[168,128]{1,0:T(8,128)S(1)}, f32[168,128]{1,0:T(8,128)S(1)}, u32[]{:S(2)}, u32[]{:S(2)}) %collective-permute-start) | collective-permute-done | bytes 86048 | tf_op jit(solution)/shard_map/ppermute | solution.py:653
  8.3 0.0 collective-permute-done.1.recv_b
  8.3 0.0 copy-done.1
  8.3 0.2 shard_map.95
  8.5 2.1 %collective-permute-start.2 = (f32[272,128]{1,0:T(8,128)S(1)}, f32[272,128]{1,0:T(8,128)S(1)}, u32[]{:S(2)}, u32[]{:S(2)}) collective-permute-start(f32[272,128]{1,0:T(8,128)S(1)} %get-tuple-element.30), channel_id=1, source_target_pairs={{0,8},{1,9},{2,10},{3,11},{4,12},{5,13},{6,14},{7,15},{8,0},{9,1},... | collective-permute-start | bytes 417800 | tf_op jit(solution)/shard_map/ppermute | solution.py:653
  10.5 1.7 %collective-permute-start.3 = (f32[272,128]{1,0:T(8,128)S(1)}, f32[272,128]{1,0:T(8,128)S(1)}, u32[]{:S(2)}, u32[]{:S(2)}) collective-permute-start(f32[272,128]{1,0:T(8,128)S(1)} %get-tuple-element.31), channel_id=1, source_target_pairs={{0,120},{1,121},{2,122},{3,123},{4,124},{5,125},{6,126},{7,127},{8... | collective-permute-start | bytes 417800 | tf_op jit(solution)/shard_map/ppermute | solution.py:653
  12.2 0.0 collective-permute-done.2.recv_a
  12.2 2.8 %collective-permute-done.3.recv_b = f32[272,128]{1,0:T(8,128)S(1)} collective-permute-done((f32[272,128]{1,0:T(8,128)S(1)}, f32[272,128]{1,0:T(8,128)S(1)}, u32[]{:S(2)}, u32[]{:S(2)}) %collective-permute-start.3) | collective-permute-done | bytes 139296 | tf_op jit(solution)/shard_map/ppermute | solution.py:653
  15.0 5.6 %shard_map.97 = (f32[4,2,80,128]{3,2,1,0:T(8,128)S(1)}, f32[128,128]{1,0:T(8,128)S(1)}, f32[128,128]{1,0:T(8,128)}, f32[64,128]{1,0:T(8,128)S(1)}, f32[96,128]{1,0:T(8,128)S(1)}) custom-call(f32[448,128]{1,0:T(8,128)S(1)} %get-tuple-element.32.tall, f32[192,128]{1,0:T(8,128)S(1)} %get-tuple-element.33.strips, f32[128,128]{1,0:T(8,128)S(1)} %get-tuple-element.34.mean, ...), custom_call_target="tpu_custom_call" | custom-call | flops 10000000 | bytes 1212416 | tf_op jit(solution)/shard_map/pallas_call | solution.py:622
  20.6 19.8 %all-to-all-start = ((f32[128,1,128]{2,1,0:T(1,128)}), f32[128,1,128]{2,1,0:T(1,128)S(1)}, u32[]{:S(2)}, u32[]{:S(2)}) async-start(f32[128,1,128]{2,1,0:T(1,128)} %bitcast.5), calls=%async_computation | async-start | bytes 131072 | tf_op jit(solution)/shard_map/all_to_all | solution.py:693
  40.4 0.0 copy-start
  40.4 0.0 copy-start.2
  40.4 1.6 %shard_map.98.star = f32[1280,128]{1,0:T(8,128)S(1)} custom-call(f32[1280,128]{1,0:T(8,128)S(1)} %get-tuple-element.38.star, f32[64,128]{1,0:T(8,128)S(1)} %get-tuple-element.39.col_patch, f32[96,128]{1,0:T(8,128)S(1)} %get-tuple-element.40.row_patch), custom_call_target="tpu_custom_call" | custom-call | flops 1000000 | bytes 1392640 | tf_op jit(solution)/shard_map/pallas_call | solution.py:622
  41.9 0.0 copy-done
  41.9 0.0 copy-done.2
  42.0 2.3 %shard_map.96 = f32[1280,128]{1,0:T(8,128)} custom-call(f32[1280,128]{1,0:T(8,128)S(1)} %bitcast.10, s32[64,128]{1,0:T(8,128)S(1)} %copy-done.2, f32[64,128]{1,0:T(8,128)S(1)} %copy-done.1, f32[96,128]{1,0:T(8,128)S(1)} %get-tuple-element.29.tracer_rows, f32[272,128]{1,0:T(8,128)S(1)} %collective-permute-done.2.recv_a, ...), custom_call_target="tpu_custom_call" | custom-call | flops 1000000 | bytes 1703936 | tf_op jit(solution)/shard_map/pallas_call | solution.py:622
  44.2 5.7 %all-to-all-done = f32[128,1,128]{2,1,0:T(1,128)S(1)} async-done(((f32[128,1,128]{2,1,0:T(1,128)}), f32[128,1,128]{2,1,0:T(1,128)S(1)}, u32[]{:S(2)}, u32[]{:S(2)}) %all-to-all-start) | async-done | bytes 65568 | tf_op jit(solution)/shard_map/all_to_all | solution.py:693
  49.9 1.3 %shard_map.99 = (f32[1280,128]{1,0:T(8,128)}, f32[64,128]{1,0:T(8,128)}) custom-call(f32[128,128]{1,0:T(8,128)S(1)} %bitcast.11, f32[4,2,80,128]{3,2,1,0:T(8,128)S(1)} %get-tuple-element.36.basis, f32[128,128]{1,0:T(8,128)S(1)} %get-tuple-element.37.flow, f32[1280,128]{1,0:T(8,128)S(1)} %shard_map.98.star, s32[64,128]{1,0:T(8,128)S(1)} %copy-done.2), custom_call_target="tpu_custom_call" | custom-call | flops 1000000 | bytes 1835008 | tf_op jit(solution)/shard_map/pallas_call | solution.py:622
Async XLA Ops:
  0.6 7.6 %copy-start.1 = (f32[64,128]{1,0:T(8,128)S(1)}, f32[64,128]{1,0:T(8,128)}, u32[]{:S(2)}) copy-start(f32[64,128]{1,0:T(8,128)} %diff.3) | copy-start | bytes 98308
  4.3 4.0 %collective-permute-start = (f32[168,128]{1,0:T(8,128)S(1)}, f32[168,128]{1,0:T(8,128)S(1)}, u32[]{:S(2)}, u32[]{:S(2)}) collective-permute-start(f32[168,128]{1,0:T(8,128)S(1)} %get-tuple-element.27), channel_id=1, source_target_pairs={{0,1},{1,0},{2,3},{3,2},{4,5},{5,4},{6,7},{7,6},{8,9},{9,8},{10,11... | collective-permute-start | bytes 258056 | tf_op jit(solution)/shard_map/ppermute | solution.py:653
  6.4 1.9 %collective-permute-start.1 = (f32[168,128]{1,0:T(8,128)S(1)}, f32[168,128]{1,0:T(8,128)S(1)}, u32[]{:S(2)}, u32[]{:S(2)}) collective-permute-start(f32[168,128]{1,0:T(8,128)S(1)} %get-tuple-element.28), channel_id=1, source_target_pairs={{1,2},{2,1},{3,4},{4,3},{5,6},{6,5},{7,127},{9,10},{10,9},{11,12},... | collective-permute-start | bytes 258056 | tf_op jit(solution)/shard_map/ppermute | solution.py:653
  8.5 3.8 %collective-permute-start.2 = (f32[272,128]{1,0:T(8,128)S(1)}, f32[272,128]{1,0:T(8,128)S(1)}, u32[]{:S(2)}, u32[]{:S(2)}) collective-permute-start(f32[272,128]{1,0:T(8,128)S(1)} %get-tuple-element.30), channel_id=1, source_target_pairs={{0,8},{1,9},{2,10},{3,11},{4,12},{5,13},{6,14},{7,15},{8,0},{9,1},... | collective-permute-start | bytes 417800 | tf_op jit(solution)/shard_map/ppermute | solution.py:653
  10.5 4.5 %collective-permute-start.3 = (f32[272,128]{1,0:T(8,128)S(1)}, f32[272,128]{1,0:T(8,128)S(1)}, u32[]{:S(2)}, u32[]{:S(2)}) collective-permute-start(f32[272,128]{1,0:T(8,128)S(1)} %get-tuple-element.31), channel_id=1, source_target_pairs={{0,120},{1,121},{2,122},{3,123},{4,124},{5,125},{6,126},{7,127},{8... | collective-permute-start | bytes 417800 | tf_op jit(solution)/shard_map/ppermute | solution.py:653
  20.6 29.3 %all-to-all-start = ((f32[128,1,128]{2,1,0:T(1,128)}), f32[128,1,128]{2,1,0:T(1,128)S(1)}, u32[]{:S(2)}, u32[]{:S(2)}) async-start(f32[128,1,128]{2,1,0:T(1,128)} %bitcast.5), calls=%async_computation | async-start | bytes 131072 | tf_op jit(solution)/shard_map/all_to_all | solution.py:693
  40.4 1.6 %copy-start = (f32[2,10,64,128]{3,2,1,0:T(8,128)S(1)}, f32[2,10,64,128]{3,2,1,0:T(8,128)}, u32[]{:S(2)}) copy-start(f32[2,10,64,128]{3,2,1,0:T(8,128)} %param.7) | copy-start | bytes 1966084
  40.4 1.6 %copy-start.2 = (s32[64,128]{1,0:T(8,128)S(1)}, s32[64,128]{1,0:T(8,128)}, u32[]{:S(2)}) copy-start(s32[64,128]{1,0:T(8,128)} %lev.3) | copy-start | bytes 98308

commit v4 on v3

--- a/solution.py
+++ b/solution.py
@@ -41,12 +41,12 @@
     return pltpu.roll(x, shift, 1)
 
 
-def flip_lanes(x, bits=7):
-    lanes = lane_ids(x.shape[0])
-    for bit in range(bits):
-        step = 1 << bit
-        x = jnp.where((lanes & step) != 0, turn(x, step), turn(x, LANES - step))
-    return x
+def pick(x, index):
+    return jnp.take_along_axis(x, index, axis=1)
+
+
+def flip_lanes(x, mask=LANES - 1):
+    return pick(x, lane_ids(x.shape[0]) ^ mask)
 
 
 def flip_rows(x):
@@ -74,10 +74,13 @@
 def block_kernel(
     vel_far, tra_far, lev_far, visc_far, diff_far, depth_far, wind_far,
     star, mean, fields, cols, north, south, send_a, send_b,
-    faces, face_levels, sums, turning, vel, tra, visc, diff, depth, wind, lev, done,
+    faces, face_levels, sums, turning, vel, tra, visc, diff, depth, wind, levels_kept, lap_pad, lev, done,
 ):
     pairs = ((lev_far, lev), (visc_far, visc), (vel_far, vel), (tra_far, tra), (wind_far, wind), (depth_far, depth), (diff_far, diff))
-    copies = [pltpu.make_async_copy(far, near, done.at[n]) for n, (far, near) in enumerate(pairs)]
+    copies = [
+        pltpu.make_async_copy(far, near.at[pl.ds(8, PLANES * ROWS)] if near is vel else near, done.at[n])
+        for n, (far, near) in enumerate(pairs)
+    ]
     for copy in copies:
         copy.start()
     for copy in copies[:2]:
@@ -93,39 +96,52 @@
     row = (lax.axis_index("lat") * ROWS).astype(F32) + ids.astype(F32)
     turning[...] = 0.25 * jnp.sin(math.pi * ((row + 0.5) / (ROWS * lax.axis_size("lat")) - 0.5))
     sums[...] = jnp.zeros((2, ROWS, LANES), F32)
+    levels_kept[...] = levels
+    for comp in range(2):
+        lap_pad[comp, 0:8, :] = jnp.zeros((8, LANES), F32)
+        lap_pad[comp, ROWS + 8 : ROWS + 16, :] = jnp.zeros((8, LANES), F32)
+    vel[0:8, :] = jnp.zeros((8, LANES), F32)
+    vel[PLANES * ROWS + 8 : PLANES * ROWS + 16, :] = jnp.zeros((8, LANES), F32)
     acc = jnp.where((lanes >> 2) == 20, turn(levels, 82), 0.0)
     cols[...] = jnp.where((lanes >> 2) == 21, turn(v, 86), acc)
-    for copy in copies[2:]:
-        copy.wait()
+    copies[2].wait()
 
     def level_step(k, carry):
         level = k.astype(F32)
         open_faces = [level < face_levels[n] for n in range(4)]
-        wet = level < lev[...].astype(F32)
+        wet = level < levels_kept[...]
         weights = [jnp.where(o, faces[n], 0.0) for n, o in enumerate(open_faces)]
-        values = [
-            vel[pl.ds(pl.multiple_of((comp * LEVELS + k) * ROWS, ROWS), ROWS), :] for comp in range(2)
-        ]
+        starts = [8 + pl.multiple_of((comp * LEVELS + k) * ROWS, ROWS) for comp in range(2)]
+        values = [vel[pl.ds(s, ROWS), :] for s in starts]
         packed = cols[...]
         for comp, x in enumerate(values):
             p = comp * LEVELS + k
-            lap = jnp.zeros((ROWS, LANES), F32)
-            for n, x_n in enumerate(shifted(x)):
-                lap += jnp.where(open_faces[n], x_n - x, 0.0)
-            second = jnp.zeros((ROWS, LANES), F32)
-            for n, lap_n in enumerate(shifted(lap)):
-                second += weights[n] * (lap_n - lap)
+            around = (turn(x, LANES - 1), turn(x, 1), vel[pl.ds(starts[comp] + 1, ROWS), :], vel[pl.ds(starts[comp] - 1, ROWS), :])
+            lap = jnp.where(open_faces[0], around[0] - x, 0.0)
+            for n in range(1, 4):
+                lap += jnp.where(open_faces[n], around[n] - x, 0.0)
+            lap_pad[comp, pl.ds(8, ROWS), :] = lap
+            around = (turn(lap, LANES - 1), turn(lap, 1), lap_pad[comp, pl.ds(9, ROWS), :], lap_pad[comp, pl.ds(7, ROWS), :])
+            second = weights[0] * (around[0] - lap)
+            for n in range(1, 4):
+                second += weights[n] * (around[n] - lap)
             rotated = values[1] if comp == 0 else -values[0]
             out = jnp.where(wet, x - second + turning[...] * rotated, 0.0)
             star[pl.ds(pl.multiple_of(p * ROWS, ROWS), ROWS), :] = out
             sums[comp] += out
             packed = jnp.where((lanes >> 2) == p, turn(x, 4 * p + 2), packed)
-            t = tra[pl.ds(pl.multiple_of(p * ROWS, ROWS), ROWS), :]
-            packed = jnp.where((lanes >> 1) == 44 + p, turn(t, lax.rem(89 + 2 * p, LANES)), packed)
         cols[...] = packed
         return carry
 
-    lax.fori_loop(0, LEVELS, level_step, 0)
+    lax.fori_loop(0, LEVELS, level_step, 0, unroll=2)
+    for copy in copies[3:]:
+        copy.wait()
+
+    def tracer_step(p, acc):
+        t = tra[pl.ds(pl.multiple_of(p * ROWS, ROWS), ROWS), :]
+        return jnp.where((lanes >> 1) == 44 + p, turn(t, lax.rem(89 + 2 * p, LANES)), acc)
+
+    cols[...] = lax.fori_loop(0, PLANES, tracer_step, cols[...], unroll=True)
     ocean = levels > 0.0
     for comp in range(2):
         here = pl.ds(comp * ROWS, ROWS)
@@ -137,7 +153,7 @@
         out[...] = jnp.zeros((RIMS, LANES), F32)
         for d in range(2):
             r = edge + d * step
-            out[pl.ds(d * STRIP, PLANES), :] = vel[pl.ds(r, PLANES, stride=ROWS), :]
+            out[pl.ds(d * STRIP, PLANES), :] = vel[pl.ds(8 + r, PLANES, stride=ROWS), :]
             out[pl.ds(d * STRIP + 20, 1), :] = levels[r : r + 1]
             out[pl.ds(d * STRIP + 21, 1), :] = visc[pl.ds(r, 1), :]
         out[pl.ds(2 * STRIP, PLANES), :] = tra[pl.ds(edge, PLANES, stride=ROWS), :]
@@ -163,11 +179,11 @@
         r = row_ids(RIMS)
         is_velocity = (r < PLANES) | ((r >= STRIP) & (r < STRIP + PLANES))
         send_b[pl.ds(3 * MARGIN, RIMS), :] = jnp.where(is_velocity, -turned, turned)
-        turned = flip_rows(flip_lanes(cols[ROWS - MARGIN : ROWS, :], 2))
+        turned = flip_rows(flip_lanes(cols[ROWS - MARGIN : ROWS, :], 3))
         send_b[pl.ds(3 * MARGIN + RIMS, MARGIN), :] = jnp.where(lane_ids(MARGIN) < 4 * PLANES, -turned, turned)
 
 
-def widen_kernel(fields, cols, diff, north, south, recv_a, recv_b, tall, strips, tracer_rows, send_a, send_b, east, west):
+def widen_kernel(fields, cols, diff, north, south, recv_b, recv_a, tall, strips, tracer_rows, send_a, send_b, east, west):
     lat_odd = odd("lat")
     lon_odd = odd("lon")
     group = lane_ids(TALL) >> 5
@@ -214,7 +230,7 @@
     send_b[rest, :] = jnp.where(lon_odd, e, w)
 
 
-def tracer_kernel(tra, lev, diff, tracer_rows, recv_a, recv_b, out, swap, faces, face_levels):
+def tracer_kernel(tra, lev, diff, tracer_rows, recv_b, recv_a, out, swap, faces, face_levels):
     is_odd = odd("lon")
     lanes = lane_ids(ROWS)
     ids = row_ids(ROWS)
@@ -260,7 +276,7 @@
             out[here, :] = x + total
         return carry
 
-    lax.fori_loop(0, LEVELS, level_step, 0)
+    lax.fori_loop(0, LEVELS, level_step, 0, unroll=2)
 
 
 def column_strip(strip):
@@ -270,14 +286,8 @@
     phase = lanes & 3
     group = lanes >> 2
 
-    def spread(which):
-        x = jnp.where(group == which, strip, 0.0)
-        for step in (4, 8, 16, 32, 64):
-            x = x + turn(x, step)
-        return x
-
-    levels = spread(20)
-    v = spread(21)
+    levels = pick(strip, phase + 80)
+    v = pick(strip, phase + 84)
     number = jnp.where(group >= LEVELS, group - LEVELS, group).astype(F32)
     wet = jnp.where((number < levels) & (group < PLANES), 1.0, 0.0)
     x = jnp.where(group < PLANES, strip, 0.0)
@@ -297,7 +307,7 @@
     face = jnp.where(in_block, 0.5 * (v + pltpu.roll(v, rows - 1, 0)) * open_n, 0.0)
     flux_n = face * (pltpu.roll(added, rows - 1, 0) - added)
     second = flux_e - turn(flux_e, 1) + flux_n - pltpu.roll(flux_n, 1, 0)
-    return wet * second, levels
+    return wet * second
 
 
 def gram_pairs():
@@ -305,7 +315,7 @@
 
 
 def surface_kernel(
-    tall, strips, mean, recv_a, recv_b,
+    tall, strips, mean, recv_b, recv_a,
     basis_out, flow, partial, col_patch, row_patch,
     state, height, flux, slope, basis, weights, diagonal,
 ):
@@ -342,20 +352,20 @@
     own = tall[pl.ds(3 * TALL, TALL), :]
     phase = lanes & 3
     from_east, from_west = received(0, TALL)
-    patches = []
-    for side, strip in enumerate((jnp.where(phase < 2, own, from_east), jnp.where(phase < 2, from_west, own))):
-        change, levels = column_strip(strip)
-        patches.append(change)
+    to_east = column_strip(jnp.where(phase < 2, own, from_east))
+    to_west = column_strip(jnp.where(phase < 2, from_west, own))
+    changes = (jnp.where(phase < 2, to_east, to_west), jnp.where(phase < 2, to_west, to_east))
+    deep = (own, jnp.where(phase < 2, from_west, from_east))
+    col_patch[...] = changes[0][MARGIN : MARGIN + ROWS]
+    rims = (lanes < 2) | (lanes >= LANES - 2)
+    for half in range(2):
+        pairs = changes[half] + turn(changes[half], LANES - 4)
+        fours = pairs + turn(pairs, LANES - 8)
+        total = fours + turn(fours, LANES - 16) + turn(pairs, LANES - 32)
+        total = total / jnp.maximum(pick(deep[half], phase + 80), 1.0)
         for comp in range(2):
-            total = jnp.where((lanes >= 40 * comp) & (lanes < 40 * comp + 40), change, 0.0)
-            for step in (4, 8, 16, 32, 64):
-                total = total + turn(total, step)
-            total = turn(total / jnp.maximum(levels, 1.0), 2)
-            for half in range(2):
-                here = lanes >= LANES - 2 if half == side else lanes < 2
-                state[comp, half, rows, :] = state[comp, half, rows, :] - jnp.where(here, total, 0.0)
-    patch = jnp.where(phase < 2, patches[0], patches[1])
-    col_patch[...] = patch[MARGIN : MARGIN + ROWS]
+            here = turn(total, LANES - 2 - 40 * comp)
+            state[comp, half, rows, :] = state[comp, half, rows, :] - jnp.where(rims, here, 0.0)
     number = lax.broadcasted_iota(jnp.int32, (STRIP, LANES), 0)
     level_of_row = jnp.where(number >= LEVELS, number - LEVELS, number).astype(F32)
     is_plane = number < PLANES
@@ -427,8 +437,8 @@
 
     halves = range(2)
 
-    def subcycle(step, carry):
-        for tile in range(8, 8 + TALL, 8):
+    def subcycle(cut, step, carry):
+        for tile in range(8 + cut, 8 + TALL - cut, 8):
             here, above, below = (pl.ds(tile + off, 8) for off in (0, 1, -1))
             east, west = lane_sides(*(state[2, h, here, :] * state[0, h, here, :] for h in halves))
             for h in halves:
@@ -436,7 +446,7 @@
                 south = state[2, h, below, :] * state[1, h, below, :]
                 divergence = (east[h] - west[h]) + (north - south)
                 height[h, here, :] = height[h, here, :] - slope[h, here, :] * divergence
-        for tile in range(8, 8 + TALL, 8):
+        for tile in range(8 + cut, 8 + TALL - cut, 8):
             here, above, below = (pl.ds(tile + off, 8) for off in (0, 1, -1))
             east, west = lane_sides(height[0, here, :], height[1, here, :])
             for h in halves:
@@ -445,7 +455,8 @@
                 state[1, h, here, :] = state[1, h, here, :] - factor * (height[h, above, :] - height[h, below, :])
         return carry
 
-    lax.fori_loop(0, SUBCYCLES, subcycle, 0)
+    for cut, start, stop in ((0, 0, 1), (8, 1, 5), (16, 5, SUBCYCLES)):
+        lax.fori_loop(start, stop, functools.partial(subcycle, cut), 0, unroll=True)
     for comp in range(2):
         here = pl.ds(comp * ROWS, ROWS)
         flow[here, :] = flow[here, :] + state[comp, 0, pl.ds(8 + MARGIN, ROWS), :]
@@ -501,7 +512,7 @@
                 basis[k + 1, h, here, :] = x - basis[k - 1, h, here, :]
         return carry
 
-    lax.fori_loop(1, SOLVE_ITERS, next_basis, 0)
+    lax.fori_loop(1, SOLVE_ITERS, next_basis, 0, unroll=True)
     lane = lane_ids(1)
     row = jnp.zeros((1, LANES), F32)
     mine = pl.ds(8 + MARGIN, ROWS)
@@ -592,7 +603,7 @@
             velocity_out[here, :] = star[here, :] + jnp.where(wet, change[comp], 0.0)
         return carry
 
-    lax.fori_loop(0, LEVELS, level_step, 0)
+    lax.fori_loop(0, LEVELS, level_step, 0, unroll=True)
 
 
 def patch_kernel(star, col_patch, row_patch, out):
@@ -611,7 +622,7 @@
             out[here, :] = x
         return carry
 
-    lax.fori_loop(0, PLANES, plane, 0)
+    lax.fori_loop(0, PLANES, plane, 0, unroll=10)
 
 
 def call(kernel, shapes, scratch, flops, *args, far=False):
@@ -660,26 +671,27 @@
     star, mean, fields, cols, north, south, send_a, send_b = call(
         block_kernel,
         [(PLANES * ROWS, LANES), (2 * ROWS, LANES), (3 * ROWS, LANES), block, rim, rim, (LAT_SEND, LANES), (LAT_SEND, LANES)],
-        [(4,) + block, (4,) + block, (2,) + block, block, vel.shape, vel.shape, block, block, block, wind.shape,
+        [(4,) + block, (4,) + block, (2,) + block, block, (PLANES * ROWS + 16, LANES), vel.shape, block, block, block, wind.shape,
+         block, (2, ROWS + 16, LANES),
          pltpu.VMEM(block, jnp.int32), pltpu.SemaphoreType.DMA((7,))],
         10**7,
         vel, tra, active_levels, viscosity, diffusivity, ocean_depth, wind,
         far=True,
     )
+    got_a = swap(send_a, lat_a)
     got_b = swap(send_b, lat_b)
-    got_a = swap(send_a, lat_a)
     tall, strips, tracer_rows, send_a, send_b = call(
         widen_kernel,
         [(4 * TALL, LANES), (8 * STRIP, LANES), (4 * STRIP, LANES), (LON_SEND, LANES), (LON_SEND, LANES)],
         [(TALL + 2 * STRIP, LANES)] * 2,
         10**6,
-        fields, cols, diffusivity, north, south, got_a, got_b,
+        fields, cols, diffusivity, north, south, got_b, got_a,
     )
+    got_a = swap(send_a, lon_a)
     got_b = swap(send_b, lon_b)
-    got_a = swap(send_a, lon_a)
     (tracers_out,) = call(
         tracer_kernel, [(PLANES * ROWS, LANES)], [block, (4,) + block, (4,) + block], 10**6,
-        tra, active_levels, diffusivity, tracer_rows, got_a, got_b,
+        tra, active_levels, diffusivity, tracer_rows, got_b, got_a,
     )
     padded = (2, TALL + 16, LANES)
     short = (2, ROWS + 16, LANES)
@@ -688,12 +700,13 @@
         [(SOLVE_ITERS,) + short, (2 * ROWS, LANES), (lon * lat, LANES), block, (4 * STRIP, LANES)],
         [(3,) + padded, padded, padded, padded, (SOLVE_ITERS + 1,) + padded, (8,) + short, short],
         10**7,
-        tall, strips, mean, got_a, got_b,
+        tall, strips, mean, got_b, got_a,
     )
     gathered = lax.all_to_all(partial, BOTH, 0, 0, tiled=True)
     (star,) = call(patch_kernel, [(PLANES * ROWS, LANES)], [], 10**6, star, col_patch, row_patch)
     velocity_out, surface = call(
-        final_kernel, [(PLANES * ROWS, LANES), block], [short, (2,) + block], 10**6,
+        final_kernel, [(PLANES * ROWS, LANES), block],
+        [short, (2,) + block], 10**6,
         gathered, basis, flow, star, active_levels,
     )
     return tracers_out.reshape(tracers.shape), velocity_out.reshape(velocity.shape), surface

time: 51.3 us -> 48.7 us (0.949)
  Pallas kernels: 14.5 us -> 11.2 us
  local copies, waits for them, and re-layouts: 0.02 us -> 0.77 us
    ppermute x4, starting transfers between devices: 6.54 us -> 12.1 us  [swap(): return lax.ppermute(x, BOTH, pairs)]
    all_to_all x1, starting transfers between devices: 19.8 us -> 14.4 us  [per_device(): gathered = lax.all_to_all(partial, BOTH, 0, 0, tiled=True)]
    pallas_call x6, Pallas kernels: 14.5 us -> 11.2 us  [call(): pl.pallas_call(kernel, out_shape=out, in_specs=[pl.BlockSpec(memory_space...]
    ppermute x4, waiting for transfers between devices: 4 us -> 2.87 us  [swap(): return lax.ppermute(x, BOTH, pairs)]
    all_to_all x1, waiting for transfers between devices: 5.67 us -> 6.55 us  [per_device(): gathered = lax.all_to_all(partial, BOTH, 0, 0, tiled=True)]
    unnamed x6, local copies, waits for them, and re-layouts: 0.02 us -> 0.77 us
  transfers between devices with their start and end apart: 5 -> 5, of which waited for: 3 -> 3; matrix products, arithmetic and copies ran while one was open for 0% -> 0% of each run, Pallas kernels for 7% -> 5%
where the time goes in v4:
time: 48.7 us; the launch traced here: 48.6 us
  starting transfers between devices  26.5 us (54%)
  Pallas kernels  11.2 us (23%)
  waiting for transfers between devices  9.42 us (19%)
  local copies, waits for them, and re-layouts  0.77 us (2%)
  between operations  0.7 us (1%)
    all_to_all x1, starting transfers between devices, per_device(): gathered = lax.all_to_all(partial, BOTH, 0, 0, tiled=True)  14.4 us
    ppermute x4, starting transfers between devices, swap(): return lax.ppermute(x, BOTH, pairs)  12.1 us
    pallas_call x6, Pallas kernels, call(): pl.pallas_call(kernel, out_shape=out, in_specs=[pl.BlockSpec(memory_space...  11.2 us
    all_to_all x1, waiting for transfers between devices, per_device(): gathered = lax.all_to_all(partial, BOTH, 0, 0, tiled=True)  6.55 us
    ppermute x4, waiting for transfers between devices, swap(): return lax.ppermute(x, BOTH, pairs)  2.87 us
  transfers between devices with their start and end apart: 5, of which 3 were waited for; matrix products, arithmetic and copies ran while one was open for 0% of the time, Pallas kernels for 5%

profile of v4, /device:TPU:1, one launch (start us, length us, event | category | flops | bytes accessed | tf_op | source)
XLA Modules:
  0.0 48.6 jit_solution(1538537586070265095)
XLA Ops:
  0.6 0.0 copy-start.1
  0.6 3.2 %shard_map.94 = (f32[1280,128]{1,0:T(8,128)S(1)}, f32[128,128]{1,0:T(8,128)S(1)}, f32[192,128]{1,0:T(8,128)S(1)}, f32[64,128]{1,0:T(8,128)S(1)}, f32[72,128]{1,0...) custom-call(f32[1280,128]{1,0:T(8,128)} %bitcast.12, f32[1280,128]{1,0:T(8,128)} %bitcast.9, ...), custom_call_target="tpu_custom_call" | custom-call | flops 10000000 | bytes 2605056 | tf_op jit(solution)/shard_map/pallas_call | solution.py:633
  3.8 0.7 %collective-permute-start = (f32[168,128]{1,0:T(8,128)S(1)}, f32[168,128]{1,0:T(8,128)S(1)}, u32[]{:S(2)}, u32[]{:S(2)}) collective-permute-start(f32[168,128]{1,0:T(8,128)S(1)} %get-tuple-element.27), channel_id=1, source_target_pairs={{1,2},{2,1},{3,4},{4,3},{5,6},{6,5},{7,127},{9,10},{10,9},{11,12},... | collective-permute-start | bytes 258056 | tf_op jit(solution)/shard_map/ppermute | solution.py:664
  4.5 4.6 %collective-permute-start.1 = (f32[168,128]{1,0:T(8,128)S(1)}, f32[168,128]{1,0:T(8,128)S(1)}, u32[]{:S(2)}, u32[]{:S(2)}) collective-permute-start(f32[168,128]{1,0:T(8,128)S(1)} %get-tuple-element.28), channel_id=1, source_target_pairs={{0,1},{1,0},{2,3},{3,2},{4,5},{5,4},{6,7},{7,6},{8,9},{9,8},{10,11... | collective-permute-start | bytes 258056 | tf_op jit(solution)/shard_map/ppermute | solution.py:664
  9.1 0.0 collective-permute-done.recv_b
  9.1 1.9 %collective-permute-done.1.recv_a = f32[168,128]{1,0:T(8,128)S(1)} collective-permute-done((f32[168,128]{1,0:T(8,128)S(1)}, f32[168,128]{1,0:T(8,128)S(1)}, u32[]{:S(2)}, u32[]{:S(2)}) %collective-permute-start.1) | collective-permute-done | bytes 86048 | tf_op jit(solution)/shard_map/ppermute | solution.py:664
  10.9 0.0 copy-done.1
  10.9 0.2 shard_map.95
  11.2 3.4 %collective-permute-start.2 = (f32[272,128]{1,0:T(8,128)S(1)}, f32[272,128]{1,0:T(8,128)S(1)}, u32[]{:S(2)}, u32[]{:S(2)}) collective-permute-start(f32[272,128]{1,0:T(8,128)S(1)} %get-tuple-element.30), channel_id=1, source_target_pairs={{0,120},{1,121},{2,122},{3,123},{4,124},{5,125},{6,126},{7,127},{8... | collective-permute-start | bytes 417800 | tf_op jit(solution)/shard_map/ppermute | solution.py:664
  14.6 3.4 %collective-permute-start.3 = (f32[272,128]{1,0:T(8,128)S(1)}, f32[272,128]{1,0:T(8,128)S(1)}, u32[]{:S(2)}, u32[]{:S(2)}) collective-permute-start(f32[272,128]{1,0:T(8,128)S(1)} %get-tuple-element.31), channel_id=1, source_target_pairs={{0,8},{1,9},{2,10},{3,11},{4,12},{5,13},{6,14},{7,15},{8,0},{9,1},... | collective-permute-start | bytes 417800 | tf_op jit(solution)/shard_map/ppermute | solution.py:664
  18.0 0.0 collective-permute-done.2.recv_b
  18.0 1.0 %collective-permute-done.3.recv_a = f32[272,128]{1,0:T(8,128)S(1)} collective-permute-done((f32[272,128]{1,0:T(8,128)S(1)}, f32[272,128]{1,0:T(8,128)S(1)}, u32[]{:S(2)}, u32[]{:S(2)}) %collective-permute-start.3) | collective-permute-done | bytes 139296 | tf_op jit(solution)/shard_map/ppermute | solution.py:664
  19.0 4.4 %shard_map.97 = (f32[4,2,80,128]{3,2,1,0:T(8,128)S(1)}, f32[128,128]{1,0:T(8,128)S(1)}, f32[128,128]{1,0:T(8,128)}, f32[64,128]{1,0:T(8,128)S(1)}, f32[96,128]{1,0:T(8,128)S(1)}) custom-call(f32[448,128]{1,0:T(8,128)S(1)} %get-tuple-element.32.tall, f32[192,128]{1,0:T(8,128)S(1)} %get-tuple-element.33.strips, f32[128,128]{1,0:T(8,128)S(1)} %get-tuple-element.34.mean, ...), custom_call_target="tpu_custom_call" | custom-call | flops 10000000 | bytes 1212416 | tf_op jit(solution)/shard_map/pallas_call | solution.py:633
  23.4 14.4 %all-to-all-start = ((f32[128,1,128]{2,1,0:T(1,128)}), f32[128,1,128]{2,1,0:T(1,128)S(1)}, u32[]{:S(2)}, u32[]{:S(2)}) async-start(f32[128,1,128]{2,1,0:T(1,128)} %bitcast.5), calls=%async_computation | async-start | bytes 131072 | tf_op jit(solution)/shard_map/all_to_all | solution.py:705
  37.8 0.0 copy-start
  37.8 0.0 copy-start.2
  37.8 0.3 shard_map.98.star
  38.2 0.8 %copy-done = f32[2,10,64,128]{3,2,1,0:T(8,128)S(1)} copy-done((f32[2,10,64,128]{3,2,1,0:T(8,128)S(1)}, f32[2,10,64,128]{3,2,1,0:T(8,128)}, u32[]{:S(2)}) %copy-start) | copy-done | bytes 655384
  38.9 0.0 copy-done.2
  38.9 1.9 %shard_map.96 = f32[1280,128]{1,0:T(8,128)} custom-call(f32[1280,128]{1,0:T(8,128)S(1)} %bitcast.10, s32[64,128]{1,0:T(8,128)S(1)} %copy-done.2, f32[64,128]{1,0:T(8,128)S(1)} %copy-done.1, f32[96,128]{1,0:T(8,128)S(1)} %get-tuple-element.29.tracer_rows, f32[272,128]{1,0:T(8,128)S(1)} %collective-permute-done.2.recv_b, ...), custom_call_target="tpu_custom_call" | custom-call | flops 1000000 | bytes 1703936 | tf_op jit(solution)/shard_map/pallas_call | solution.py:633
  40.8 6.5 %all-to-all-done = f32[128,1,128]{2,1,0:T(1,128)S(1)} async-done(((f32[128,1,128]{2,1,0:T(1,128)}), f32[128,1,128]{2,1,0:T(1,128)S(1)}, u32[]{:S(2)}, u32[]{:S(2)}) %all-to-all-start) | async-done | bytes 65568 | tf_op jit(solution)/shard_map/all_to_all | solution.py:705
  47.3 1.2 %shard_map.99 = (f32[1280,128]{1,0:T(8,128)}, f32[64,128]{1,0:T(8,128)}) custom-call(f32[128,128]{1,0:T(8,128)S(1)} %bitcast.11, f32[4,2,80,128]{3,2,1,0:T(8,128)S(1)} %get-tuple-element.36.basis, f32[128,128]{1,0:T(8,128)S(1)} %get-tuple-element.37.flow, f32[1280,128]{1,0:T(8,128)S(1)} %shard_map.98.star, s32[64,128]{1,0:T(8,128)S(1)} %copy-done.2), custom_call_target="tpu_custom_call" | custom-call | flops 1000000 | bytes 1835008 | tf_op jit(solution)/shard_map/pallas_call | solution.py:633
Async XLA Ops:
  0.6 10.3 %copy-start.1 = (f32[64,128]{1,0:T(8,128)S(1)}, f32[64,128]{1,0:T(8,128)}, u32[]{:S(2)}) copy-start(f32[64,128]{1,0:T(8,128)} %diff.3) | copy-start | bytes 98308
  3.8 5.3 %collective-permute-start = (f32[168,128]{1,0:T(8,128)S(1)}, f32[168,128]{1,0:T(8,128)S(1)}, u32[]{:S(2)}, u32[]{:S(2)}) collective-permute-start(f32[168,128]{1,0:T(8,128)S(1)} %get-tuple-element.27), channel_id=1, source_target_pairs={{1,2},{2,1},{3,4},{4,3},{5,6},{6,5},{7,127},{9,10},{10,9},{11,12},... | collective-permute-start | bytes 258056 | tf_op jit(solution)/shard_map/ppermute | solution.py:664
  4.5 6.4 %collective-permute-start.1 = (f32[168,128]{1,0:T(8,128)S(1)}, f32[168,128]{1,0:T(8,128)S(1)}, u32[]{:S(2)}, u32[]{:S(2)}) collective-permute-start(f32[168,128]{1,0:T(8,128)S(1)} %get-tuple-element.28), channel_id=1, source_target_pairs={{0,1},{1,0},{2,3},{3,2},{4,5},{5,4},{6,7},{7,6},{8,9},{9,8},{10,11... | collective-permute-start | bytes 258056 | tf_op jit(solution)/shard_map/ppermute | solution.py:664
  11.2 6.9 %collective-permute-start.2 = (f32[272,128]{1,0:T(8,128)S(1)}, f32[272,128]{1,0:T(8,128)S(1)}, u32[]{:S(2)}, u32[]{:S(2)}) collective-permute-start(f32[272,128]{1,0:T(8,128)S(1)} %get-tuple-element.30), channel_id=1, source_target_pairs={{0,120},{1,121},{2,122},{3,123},{4,124},{5,125},{6,126},{7,127},{8... | collective-permute-start | bytes 417800 | tf_op jit(solution)/shard_map/ppermute | solution.py:664
  14.6 4.4 %collective-permute-start.3 = (f32[272,128]{1,0:T(8,128)S(1)}, f32[272,128]{1,0:T(8,128)S(1)}, u32[]{:S(2)}, u32[]{:S(2)}) collective-permute-start(f32[272,128]{1,0:T(8,128)S(1)} %get-tuple-element.31), channel_id=1, source_target_pairs={{0,8},{1,9},{2,10},{3,11},{4,12},{5,13},{6,14},{7,15},{8,0},{9,1},... | collective-permute-start | bytes 417800 | tf_op jit(solution)/shard_map/ppermute | solution.py:664
  23.4 23.9 %all-to-all-start = ((f32[128,1,128]{2,1,0:T(1,128)}), f32[128,1,128]{2,1,0:T(1,128)S(1)}, u32[]{:S(2)}, u32[]{:S(2)}) async-start(f32[128,1,128]{2,1,0:T(1,128)} %bitcast.5), calls=%async_computation | async-start | bytes 131072 | tf_op jit(solution)/shard_map/all_to_all | solution.py:705
  37.8 1.1 %copy-start = (f32[2,10,64,128]{3,2,1,0:T(8,128)S(1)}, f32[2,10,64,128]{3,2,1,0:T(8,128)}, u32[]{:S(2)}) copy-start(f32[2,10,64,128]{3,2,1,0:T(8,128)} %param.7) | copy-start | bytes 1966084
  37.8 1.1 %copy-start.2 = (s32[64,128]{1,0:T(8,128)S(1)}, s32[64,128]{1,0:T(8,128)}, u32[]{:S(2)}) copy-start(s32[64,128]{1,0:T(8,128)} %lev.3) | copy-start | bytes 98308

commit v5 on v4

--- a/solution.py
+++ b/solution.py
@@ -74,7 +74,7 @@
 def block_kernel(
     vel_far, tra_far, lev_far, visc_far, diff_far, depth_far, wind_far,
     star, mean, fields, cols, north, south, send_a, send_b,
-    faces, face_levels, sums, turning, vel, tra, visc, diff, depth, wind, levels_kept, lap_pad, lev, done,
+    faces, face_levels, sums, turning, vel, tra, visc, diff, depth, wind, levels_kept, laps, lev, done,
 ):
     pairs = ((lev_far, lev), (visc_far, visc), (vel_far, vel), (tra_far, tra), (wind_far, wind), (depth_far, depth), (diff_far, diff))
     copies = [
@@ -97,43 +97,51 @@
     turning[...] = 0.25 * jnp.sin(math.pi * ((row + 0.5) / (ROWS * lax.axis_size("lat")) - 0.5))
     sums[...] = jnp.zeros((2, ROWS, LANES), F32)
     levels_kept[...] = levels
-    for comp in range(2):
-        lap_pad[comp, 0:8, :] = jnp.zeros((8, LANES), F32)
-        lap_pad[comp, ROWS + 8 : ROWS + 16, :] = jnp.zeros((8, LANES), F32)
-    vel[0:8, :] = jnp.zeros((8, LANES), F32)
-    vel[PLANES * ROWS + 8 : PLANES * ROWS + 16, :] = jnp.zeros((8, LANES), F32)
+    for padded in (vel, laps):
+        padded[0:8, :] = jnp.zeros((8, LANES), F32)
+        padded[PLANES * ROWS + 8 : PLANES * ROWS + 16, :] = jnp.zeros((8, LANES), F32)
     acc = jnp.where((lanes >> 2) == 20, turn(levels, 82), 0.0)
     cols[...] = jnp.where((lanes >> 2) == 21, turn(v, 86), acc)
     copies[2].wait()
 
-    def level_step(k, carry):
+    def lap_step(k, carry):
         level = k.astype(F32)
         open_faces = [level < face_levels[n] for n in range(4)]
-        wet = level < levels_kept[...]
-        weights = [jnp.where(o, faces[n], 0.0) for n, o in enumerate(open_faces)]
-        starts = [8 + pl.multiple_of((comp * LEVELS + k) * ROWS, ROWS) for comp in range(2)]
-        values = [vel[pl.ds(s, ROWS), :] for s in starts]
+        ones = [jnp.where(o, 1.0, 0.0) for o in open_faces]
+        count = (ones[0] + ones[1]) + (ones[2] + ones[3])
         packed = cols[...]
-        for comp, x in enumerate(values):
+        for comp in range(2):
             p = comp * LEVELS + k
-            around = (turn(x, LANES - 1), turn(x, 1), vel[pl.ds(starts[comp] + 1, ROWS), :], vel[pl.ds(starts[comp] - 1, ROWS), :])
-            lap = jnp.where(open_faces[0], around[0] - x, 0.0)
-            for n in range(1, 4):
-                lap += jnp.where(open_faces[n], around[n] - x, 0.0)
-            lap_pad[comp, pl.ds(8, ROWS), :] = lap
-            around = (turn(lap, LANES - 1), turn(lap, 1), lap_pad[comp, pl.ds(9, ROWS), :], lap_pad[comp, pl.ds(7, ROWS), :])
-            second = weights[0] * (around[0] - lap)
-            for n in range(1, 4):
-                second += weights[n] * (around[n] - lap)
-            rotated = values[1] if comp == 0 else -values[0]
-            out = jnp.where(wet, x - second + turning[...] * rotated, 0.0)
-            star[pl.ds(pl.multiple_of(p * ROWS, ROWS), ROWS), :] = out
-            sums[comp] += out
+            start = 8 + pl.multiple_of(p * ROWS, ROWS)
+            x = vel[pl.ds(start, ROWS), :]
+            around = (turn(x, LANES - 1), turn(x, 1), vel[pl.ds(start + 1, ROWS), :], vel[pl.ds(start - 1, ROWS), :])
+            picked = [jnp.where(open_faces[n], around[n], 0.0) for n in range(4)]
+            laps[pl.ds(start, ROWS), :] = (picked[0] + picked[1]) + (picked[2] + picked[3]) - count * x
             packed = jnp.where((lanes >> 2) == p, turn(x, 4 * p + 2), packed)
         cols[...] = packed
         return carry
 
-    lax.fori_loop(0, LEVELS, level_step, 0, unroll=2)
+    def star_step(k, carry):
+        level = k.astype(F32)
+        wet = level < levels_kept[...]
+        weights = [jnp.where(level < face_levels[n], faces[n], 0.0) for n in range(4)]
+        weight = (weights[0] + weights[1]) + (weights[2] + weights[3])
+        starts = [8 + pl.multiple_of((comp * LEVELS + k) * ROWS, ROWS) for comp in range(2)]
+        values = [vel[pl.ds(s, ROWS), :] for s in starts]
+        for comp, x in enumerate(values):
+            start = starts[comp]
+            lap = laps[pl.ds(start, ROWS), :]
+            around = (turn(lap, LANES - 1), turn(lap, 1), laps[pl.ds(start + 1, ROWS), :], laps[pl.ds(start - 1, ROWS), :])
+            terms = [weights[n] * around[n] for n in range(4)]
+            second = (terms[0] + terms[1]) + (terms[2] + terms[3]) - weight * lap
+            rotated = values[1] if comp == 0 else -values[0]
+            out = jnp.where(wet, x - second + turning[...] * rotated, 0.0)
+            star[pl.ds(pl.multiple_of((comp * LEVELS + k) * ROWS, ROWS), ROWS), :] = out
+            sums[comp] += out
+        return carry
+
+    lax.fori_loop(0, LEVELS, lap_step, 0, unroll=10)
+    lax.fori_loop(0, LEVELS, star_step, 0, unroll=10)
     for copy in copies[3:]:
         copy.wait()
 
@@ -357,15 +365,26 @@
     changes = (jnp.where(phase < 2, to_east, to_west), jnp.where(phase < 2, to_west, to_east))
     deep = (own, jnp.where(phase < 2, from_west, from_east))
     col_patch[...] = changes[0][MARGIN : MARGIN + ROWS]
-    rims = (lanes < 2) | (lanes >= LANES - 2)
+    to_lane = lax.broadcasted_iota(jnp.int32, (LANES, 2 * LANES), 1)
+    from_lane = lax.broadcasted_iota(jnp.int32, (LANES, 2 * LANES), 0)
+    column = to_lane & (LANES - 1)
+    comp_of = jnp.where(from_lane < 4 * LEVELS, 0, 1)
+    chosen = (
+        ((column < 2) | (column >= LANES - 2))
+        & ((from_lane & 3) == ((to_lane + 2) & 3))
+        & (comp_of == (to_lane >> 7))
+        & (from_lane < 4 * PLANES)
+    )
+    chooser = jnp.where(chosen, 1.0, 0.0)
     for half in range(2):
-        pairs = changes[half] + turn(changes[half], LANES - 4)
-        fours = pairs + turn(pairs, LANES - 8)
-        total = fours + turn(fours, LANES - 16) + turn(pairs, LANES - 32)
-        total = total / jnp.maximum(pick(deep[half], phase + 80), 1.0)
+        total = lax.dot_general(
+            changes[half], chooser, (((1,), (0,)), ((), ())),
+            precision=lax.Precision.HIGHEST, preferred_element_type=F32,
+        )
+        share = 1.0 / jnp.maximum(pick(deep[half], ((lanes + 2) & 3) + 80), 1.0)
         for comp in range(2):
-            here = turn(total, LANES - 2 - 40 * comp)
-            state[comp, half, rows, :] = state[comp, half, rows, :] - jnp.where(rims, here, 0.0)
+            change = total[:, comp * LANES : (comp + 1) * LANES] * share
+            state[comp, half, rows, :] = state[comp, half, rows, :] - change
     number = lax.broadcasted_iota(jnp.int32, (STRIP, LANES), 0)
     level_of_row = jnp.where(number >= LEVELS, number - LEVELS, number).astype(F32)
     is_plane = number < PLANES
@@ -490,10 +509,10 @@
             diagonal[h, here, :] = scale * (total - CENTRE)
             basis[0, h, pl.ds(base + tile, 8), :] = height[h, pl.ds(base + tile, 8), :]
 
-    def applied(source, tile):
+    def applied(source, tile, count=2):
         around = nine(lambda h, where: basis[source, h, where, :], tile)
         out = []
-        for h in halves:
+        for h in range(count):
             here = pl.ds(tile, 8)
             total = diagonal[h, here, :] * around[h][0]
             for n in range(1, 9):
@@ -505,14 +524,14 @@
         for h, x in enumerate(applied(0, tile)):
             basis[1, h, pl.ds(base + tile, 8), :] = 0.5 * x
 
-    def next_basis(k, carry):
+    for k in range(1, SOLVE_ITERS - 1):
         for tile in tiles:
             here = pl.ds(base + tile, 8)
             for h, x in enumerate(applied(k, tile)):
                 basis[k + 1, h, here, :] = x - basis[k - 1, h, here, :]
-        return carry
-
-    lax.fori_loop(1, SOLVE_ITERS, next_basis, 0, unroll=True)
+    for tile in tiles[1:-1]:
+        here = pl.ds(base + tile, 8)
+        basis[SOLVE_ITERS, 0, here, :] = applied(SOLVE_ITERS - 1, tile, 1)[0] - basis[SOLVE_ITERS - 2, 0, here, :]
     lane = lane_ids(1)
     row = jnp.zeros((1, LANES), F32)
     mine = pl.ds(8 + MARGIN, ROWS)
@@ -672,7 +691,7 @@
         block_kernel,
         [(PLANES * ROWS, LANES), (2 * ROWS, LANES), (3 * ROWS, LANES), block, rim, rim, (LAT_SEND, LANES), (LAT_SEND, LANES)],
         [(4,) + block, (4,) + block, (2,) + block, block, (PLANES * ROWS + 16, LANES), vel.shape, block, block, block, wind.shape,
-         block, (2, ROWS + 16, LANES),
+         block, (PLANES * ROWS + 16, LANES),
          pltpu.VMEM(block, jnp.int32), pltpu.SemaphoreType.DMA((7,))],
         10**7,
         vel, tra, active_levels, viscosity, diffusivity, ocean_depth, wind,

time: 48.7 us -> 47.6 us (0.977)
  Pallas kernels: 11.2 us -> 10 us
    pallas_call x6, Pallas kernels: 11.2 us -> 10 us  [call(): pl.pallas_call(kernel, out_shape=out, in_specs=[pl.BlockSpec(memory_space...]
where the time goes in v5:
time: 47.6 us; the launch traced here: 47.4 us
  starting transfers between devices  26.5 us (56%)
  Pallas kernels  10 us (21%)
  waiting for transfers between devices  9.42 us (20%)
  local copies, waits for them, and re-layouts  0.77 us (2%)
  between operations  0.7 us (1%)
    all_to_all x1, starting transfers between devices, per_device(): gathered = lax.all_to_all(partial, BOTH, 0, 0, tiled=True)  14.4 us
    ppermute x4, starting transfers between devices, swap(): return lax.ppermute(x, BOTH, pairs)  12.1 us
    pallas_call x6, Pallas kernels, call(): pl.pallas_call(kernel, out_shape=out, in_specs=[pl.BlockSpec(memory_space...  10 us
    all_to_all x1, waiting for transfers between devices, per_device(): gathered = lax.all_to_all(partial, BOTH, 0, 0, tiled=True)  6.55 us
    ppermute x4, waiting for transfers between devices, swap(): return lax.ppermute(x, BOTH, pairs)  2.87 us
  transfers between devices with their start and end apart: 5, of which 3 were waited for; matrix products, arithmetic and copies ran while one was open for 0% of the time, Pallas kernels for 5%

profile of v5, /device:TPU:1, one launch (start us, length us, event | category | flops | bytes accessed | tf_op | source)
XLA Modules:
  0.0 47.4 jit_solution(1244042019203380673)
XLA Ops:
  0.6 0.0 copy-start.1
  0.6 2.6 %shard_map.94 = (f32[1280,128]{1,0:T(8,128)S(1)}, f32[128,128]{1,0:T(8,128)S(1)}, f32[192,128]{1,0:T(8,128)S(1)}, f32[64,128]{1,0:T(8,128)S(1)}, f32[72,128]{1,0...) custom-call(f32[1280,128]{1,0:T(8,128)} %bitcast.12, f32[1280,128]{1,0:T(8,128)} %bitcast.9, ...), custom_call_target="tpu_custom_call" | custom-call | flops 10000000 | bytes 2605056 | tf_op jit(solution)/shard_map/pallas_call | solution.py:652
  3.2 0.7 %collective-permute-start = (f32[168,128]{1,0:T(8,128)S(1)}, f32[168,128]{1,0:T(8,128)S(1)}, u32[]{:S(2)}, u32[]{:S(2)}) collective-permute-start(f32[168,128]{1,0:T(8,128)S(1)} %get-tuple-element.27), channel_id=1, source_target_pairs={{1,2},{2,1},{3,4},{4,3},{5,6},{6,5},{7,127},{9,10},{10,9},{11,12},... | collective-permute-start | bytes 258056 | tf_op jit(solution)/shard_map/ppermute | solution.py:683
  3.9 4.6 %collective-permute-start.1 = (f32[168,128]{1,0:T(8,128)S(1)}, f32[168,128]{1,0:T(8,128)S(1)}, u32[]{:S(2)}, u32[]{:S(2)}) collective-permute-start(f32[168,128]{1,0:T(8,128)S(1)} %get-tuple-element.28), channel_id=1, source_target_pairs={{0,1},{1,0},{2,3},{3,2},{4,5},{5,4},{6,7},{7,6},{8,9},{9,8},{10,11... | collective-permute-start | bytes 258056 | tf_op jit(solution)/shard_map/ppermute | solution.py:683
  8.5 0.0 collective-permute-done.recv_b
  8.5 1.9 %collective-permute-done.1.recv_a = f32[168,128]{1,0:T(8,128)S(1)} collective-permute-done((f32[168,128]{1,0:T(8,128)S(1)}, f32[168,128]{1,0:T(8,128)S(1)}, u32[]{:S(2)}, u32[]{:S(2)}) %collective-permute-start.1) | collective-permute-done | bytes 86048 | tf_op jit(solution)/shard_map/ppermute | solution.py:683
  10.3 0.0 copy-done.1
  10.3 0.2 shard_map.95
  10.6 3.4 %collective-permute-start.2 = (f32[272,128]{1,0:T(8,128)S(1)}, f32[272,128]{1,0:T(8,128)S(1)}, u32[]{:S(2)}, u32[]{:S(2)}) collective-permute-start(f32[272,128]{1,0:T(8,128)S(1)} %get-tuple-element.30), channel_id=1, source_target_pairs={{0,120},{1,121},{2,122},{3,123},{4,124},{5,125},{6,126},{7,127},{8... | collective-permute-start | bytes 417800 | tf_op jit(solution)/shard_map/ppermute | solution.py:683
  14.0 3.4 %collective-permute-start.3 = (f32[272,128]{1,0:T(8,128)S(1)}, f32[272,128]{1,0:T(8,128)S(1)}, u32[]{:S(2)}, u32[]{:S(2)}) collective-permute-start(f32[272,128]{1,0:T(8,128)S(1)} %get-tuple-element.31), channel_id=1, source_target_pairs={{0,8},{1,9},{2,10},{3,11},{4,12},{5,13},{6,14},{7,15},{8,0},{9,1},... | collective-permute-start | bytes 417800 | tf_op jit(solution)/shard_map/ppermute | solution.py:683
  17.4 0.0 collective-permute-done.2.recv_b
  17.4 1.0 %collective-permute-done.3.recv_a = f32[272,128]{1,0:T(8,128)S(1)} collective-permute-done((f32[272,128]{1,0:T(8,128)S(1)}, f32[272,128]{1,0:T(8,128)S(1)}, u32[]{:S(2)}, u32[]{:S(2)}) %collective-permute-start.3) | collective-permute-done | bytes 139296 | tf_op jit(solution)/shard_map/ppermute | solution.py:683
  18.4 3.8 %shard_map.97 = (f32[4,2,80,128]{3,2,1,0:T(8,128)S(1)}, f32[128,128]{1,0:T(8,128)S(1)}, f32[128,128]{1,0:T(8,128)}, f32[64,128]{1,0:T(8,128)S(1)}, f32[96,128]{1,0:T(8,128)S(1)}) custom-call(f32[448,128]{1,0:T(8,128)S(1)} %get-tuple-element.32.tall, f32[192,128]{1,0:T(8,128)S(1)} %get-tuple-element.33.strips, f32[128,128]{1,0:T(8,128)S(1)} %get-tuple-element.34.mean, ...), custom_call_target="tpu_custom_call" | custom-call | flops 10000000 | bytes 1212416 | tf_op jit(solution)/shard_map/pallas_call | solution.py:652
  22.3 14.4 %all-to-all-start = ((f32[128,1,128]{2,1,0:T(1,128)}), f32[128,1,128]{2,1,0:T(1,128)S(1)}, u32[]{:S(2)}, u32[]{:S(2)}) async-start(f32[128,1,128]{2,1,0:T(1,128)} %bitcast.5), calls=%async_computation | async-start | bytes 131072 | tf_op jit(solution)/shard_map/all_to_all | solution.py:724
  36.6 0.0 copy-start
  36.7 0.0 copy-start.2
  36.7 0.3 shard_map.98.star
  37.0 0.8 %copy-done = f32[2,10,64,128]{3,2,1,0:T(8,128)S(1)} copy-done((f32[2,10,64,128]{3,2,1,0:T(8,128)S(1)}, f32[2,10,64,128]{3,2,1,0:T(8,128)}, u32[]{:S(2)}) %copy-start) | copy-done | bytes 655384
  37.7 0.0 copy-done.2
  37.7 1.9 %shard_map.96 = f32[1280,128]{1,0:T(8,128)} custom-call(f32[1280,128]{1,0:T(8,128)S(1)} %bitcast.10, s32[64,128]{1,0:T(8,128)S(1)} %copy-done.2, f32[64,128]{1,0:T(8,128)S(1)} %copy-done.1, f32[96,128]{1,0:T(8,128)S(1)} %get-tuple-element.29.tracer_rows, f32[272,128]{1,0:T(8,128)S(1)} %collective-permute-done.2.recv_b, ...), custom_call_target="tpu_custom_call" | custom-call | flops 1000000 | bytes 1703936 | tf_op jit(solution)/shard_map/pallas_call | solution.py:652
  39.6 6.5 %all-to-all-done = f32[128,1,128]{2,1,0:T(1,128)S(1)} async-done(((f32[128,1,128]{2,1,0:T(1,128)}), f32[128,1,128]{2,1,0:T(1,128)S(1)}, u32[]{:S(2)}, u32[]{:S(2)}) %all-to-all-start) | async-done | bytes 65568 | tf_op jit(solution)/shard_map/all_to_all | solution.py:724
  46.2 1.2 %shard_map.99 = (f32[1280,128]{1,0:T(8,128)}, f32[64,128]{1,0:T(8,128)}) custom-call(f32[128,128]{1,0:T(8,128)S(1)} %bitcast.11, f32[4,2,80,128]{3,2,1,0:T(8,128)S(1)} %get-tuple-element.36.basis, f32[128,128]{1,0:T(8,128)S(1)} %get-tuple-element.37.flow, f32[1280,128]{1,0:T(8,128)S(1)} %shard_map.98.star, s32[64,128]{1,0:T(8,128)S(1)} %copy-done.2), custom_call_target="tpu_custom_call" | custom-call | flops 1000000 | bytes 1835008 | tf_op jit(solution)/shard_map/pallas_call | solution.py:652
Async XLA Ops:
  0.6 9.7 %copy-start.1 = (f32[64,128]{1,0:T(8,128)S(1)}, f32[64,128]{1,0:T(8,128)}, u32[]{:S(2)}) copy-start(f32[64,128]{1,0:T(8,128)} %diff.3) | copy-start | bytes 98308
  3.2 5.3 %collective-permute-start = (f32[168,128]{1,0:T(8,128)S(1)}, f32[168,128]{1,0:T(8,128)S(1)}, u32[]{:S(2)}, u32[]{:S(2)}) collective-permute-start(f32[168,128]{1,0:T(8,128)S(1)} %get-tuple-element.27), channel_id=1, source_target_pairs={{1,2},{2,1},{3,4},{4,3},{5,6},{6,5},{7,127},{9,10},{10,9},{11,12},... | collective-permute-start | bytes 258056 | tf_op jit(solution)/shard_map/ppermute | solution.py:683
  3.9 6.4 %collective-permute-start.1 = (f32[168,128]{1,0:T(8,128)S(1)}, f32[168,128]{1,0:T(8,128)S(1)}, u32[]{:S(2)}, u32[]{:S(2)}) collective-permute-start(f32[168,128]{1,0:T(8,128)S(1)} %get-tuple-element.28), channel_id=1, source_target_pairs={{0,1},{1,0},{2,3},{3,2},{4,5},{5,4},{6,7},{7,6},{8,9},{9,8},{10,11... | collective-permute-start | bytes 258056 | tf_op jit(solution)/shard_map/ppermute | solution.py:683
  10.6 6.9 %collective-permute-start.2 = (f32[272,128]{1,0:T(8,128)S(1)}, f32[272,128]{1,0:T(8,128)S(1)}, u32[]{:S(2)}, u32[]{:S(2)}) collective-permute-start(f32[272,128]{1,0:T(8,128)S(1)} %get-tuple-element.30), channel_id=1, source_target_pairs={{0,120},{1,121},{2,122},{3,123},{4,124},{5,125},{6,126},{7,127},{8... | collective-permute-start | bytes 417800 | tf_op jit(solution)/shard_map/ppermute | solution.py:683
  14.0 4.4 %collective-permute-start.3 = (f32[272,128]{1,0:T(8,128)S(1)}, f32[272,128]{1,0:T(8,128)S(1)}, u32[]{:S(2)}, u32[]{:S(2)}) collective-permute-start(f32[272,128]{1,0:T(8,128)S(1)} %get-tuple-element.31), channel_id=1, source_target_pairs={{0,8},{1,9},{2,10},{3,11},{4,12},{5,13},{6,14},{7,15},{8,0},{9,1},... | collective-permute-start | bytes 417800 | tf_op jit(solution)/shard_map/ppermute | solution.py:683
  22.3 23.9 %all-to-all-start = ((f32[128,1,128]{2,1,0:T(1,128)}), f32[128,1,128]{2,1,0:T(1,128)S(1)}, u32[]{:S(2)}, u32[]{:S(2)}) async-start(f32[128,1,128]{2,1,0:T(1,128)} %bitcast.5), calls=%async_computation | async-start | bytes 131072 | tf_op jit(solution)/shard_map/all_to_all | solution.py:724
  36.6 1.1 %copy-start = (f32[2,10,64,128]{3,2,1,0:T(8,128)S(1)}, f32[2,10,64,128]{3,2,1,0:T(8,128)}, u32[]{:S(2)}) copy-start(f32[2,10,64,128]{3,2,1,0:T(8,128)} %param.7) | copy-start | bytes 1966084
  36.7 1.1 %copy-start.2 = (s32[64,128]{1,0:T(8,128)S(1)}, s32[64,128]{1,0:T(8,128)}, u32[]{:S(2)}) copy-start(s32[64,128]{1,0:T(8,128)} %lev.3) | copy-start | bytes 98308

commit v6 on v5

--- a/solution.py
+++ b/solution.py
@@ -25,8 +25,13 @@
 
 STRIP = 24
 RIMS = 3 * STRIP
-LAT_SEND = 3 * MARGIN + RIMS + MARGIN
-LON_SEND = 2 * TALL + 2 * STRIP
+SENT = 20
+FULL = 22
+EDGE = 21
+NEAR, NEXT, LAST, COLS = 3 * SENT, 3 * SENT + FULL, 3 * SENT + 2 * FULL, 128
+LAT_SEND = COLS + MARGIN
+LON_SEND = 2 * TALL
+WIDE = 21
 
 
 def lane_ids(rows):
@@ -174,65 +179,81 @@
         send_b[here, :] = jnp.where(lat_odd, up, down)
 
     for f in range(3):
-        put(f * MARGIN, fields[pl.ds((f + 1) * ROWS - MARGIN, MARGIN), :], fields[pl.ds(f * ROWS, MARGIN), :])
-    put(3 * MARGIN, north[...], south[...])
-    put(3 * MARGIN + RIMS, cols[ROWS - MARGIN : ROWS, :], cols[0:MARGIN, :])
+        put(f * SENT, fields[pl.ds((f + 1) * ROWS - SENT, SENT), :], fields[pl.ds(f * ROWS, SENT), :])
+    for start, first, count in ((NEAR, 0, FULL), (NEXT, STRIP, FULL), (LAST, 2 * STRIP, EDGE)):
+        put(start, north[pl.ds(first, count), :], south[pl.ds(first, count), :])
+    put(COLS, cols[ROWS - MARGIN : ROWS, :], cols[0:MARGIN, :])
+    for send in (send_a, send_b):
+        send[LAST + EDGE : COLS, :] = jnp.zeros((COLS - LAST - EDGE, LANES), F32)
 
     @pl.when(at_fold())
     def _():
         for f in range(3):
-            turned = flip_rows(flip_lanes(fields[pl.ds((f + 1) * ROWS - MARGIN, MARGIN), :]))
-            send_b[pl.ds(f * MARGIN, MARGIN), :] = turned if f == 2 else -turned
+            turned = flip_rows(flip_lanes(fields[pl.ds((f + 1) * ROWS - MARGIN, MARGIN), :]))[0:SENT]
+            send_b[pl.ds(f * SENT, SENT), :] = turned if f == 2 else -turned
         turned = flip_lanes(north[...])
         r = row_ids(RIMS)
         is_velocity = (r < PLANES) | ((r >= STRIP) & (r < STRIP + PLANES))
-        send_b[pl.ds(3 * MARGIN, RIMS), :] = jnp.where(is_velocity, -turned, turned)
+        turned = jnp.where(is_velocity, -turned, turned)
+        for start, first, count in ((NEAR, 0, FULL), (NEXT, STRIP, FULL), (LAST, 2 * STRIP, EDGE)):
+            send_b[pl.ds(start, count), :] = turned[first : first + count]
         turned = flip_rows(flip_lanes(cols[ROWS - MARGIN : ROWS, :], 3))
-        send_b[pl.ds(3 * MARGIN + RIMS, MARGIN), :] = jnp.where(lane_ids(MARGIN) < 4 * PLANES, -turned, turned)
+        send_b[pl.ds(COLS, MARGIN), :] = jnp.where(lane_ids(MARGIN) < 4 * PLANES, -turned, turned)
 
 
 def widen_kernel(fields, cols, diff, north, south, recv_b, recv_a, tall, strips, tracer_rows, send_a, send_b, east, west):
     lat_odd = odd("lat")
     lon_odd = odd("lon")
-    group = lane_ids(TALL) >> 5
-
     def received(start, count):
         here = pl.ds(start, count)
         got_a = recv_a[here, :]
         got_b = recv_b[here, :]
         return jnp.where(lat_odd, got_b, got_a), jnp.where(lat_odd, got_a, got_b)
 
+    lanes = lane_ids(TALL)
     acc_east = jnp.zeros((TALL, LANES), F32)
     acc_west = jnp.zeros((TALL, LANES), F32)
-    for f in range(4):
-        from_north, from_south = received(f * MARGIN if f < 3 else 3 * MARGIN + RIMS, MARGIN)
-        tall[pl.ds(f * TALL, MARGIN), :] = from_south
-        tall[pl.ds(f * TALL + MARGIN, ROWS), :] = fields[pl.ds(f * ROWS, ROWS), :] if f < 3 else cols[...]
-        tall[pl.ds(f * TALL + MARGIN + ROWS, MARGIN), :] = from_north
-        if f < 3:
-            x = tall[pl.ds(f * TALL, TALL), :]
-            acc_east = jnp.where(group == f, turn(x, 32 * (f + 1)), acc_east)
-            acc_west = jnp.where(group == f, turn(x, 32 * f), acc_west)
-    for out, acc, shift in ((east, acc_east, 97), (west, acc_west, 96)):
-        out[pl.ds(0, TALL), :] = acc
-        out[pl.ds(MARGIN, ROWS), :] = jnp.where(lane_ids(ROWS) == 96, turn(diff[...], shift), acc[MARGIN : MARGIN + ROWS])
-    rims = received(3 * MARGIN, RIMS)
-    for s, (own, rim) in enumerate(((north, rims[0]), (south, rims[1]))):
-        pieces = (rim[STRIP : 2 * STRIP], rim[0:STRIP], own[0:STRIP, :], own[STRIP : 2 * STRIP, :])
-        acc_east = jnp.zeros((STRIP, LANES), F32)
-        acc_west = jnp.zeros((STRIP, LANES), F32)
+    for f in range(3):
+        from_north, from_south = received(f * SENT, SENT)
+        unused = jnp.zeros((MARGIN - SENT, LANES), F32)
+        tall[pl.ds(f * TALL, MARGIN - SENT), :] = unused
+        tall[pl.ds(f * TALL + MARGIN - SENT, SENT), :] = from_south
+        tall[pl.ds(f * TALL + MARGIN, ROWS), :] = fields[pl.ds(f * ROWS, ROWS), :]
+        tall[pl.ds(f * TALL + MARGIN + ROWS, SENT), :] = from_north
+        tall[pl.ds(f * TALL + MARGIN + ROWS + SENT, MARGIN - SENT), :] = unused
+        x = tall[pl.ds(f * TALL, TALL), :]
+        here = (lanes >= f * WIDE) & (lanes < (f + 1) * WIDE)
+        acc_east = jnp.where(here, turn(x, (f + 1) * WIDE), acc_east)
+        acc_west = jnp.where(here, turn(x, f * WIDE), acc_west)
+    from_north, from_south = received(COLS, MARGIN)
+    tall[pl.ds(3 * TALL, MARGIN), :] = from_south
+    tall[pl.ds(3 * TALL + MARGIN, ROWS), :] = cols[...]
+    tall[pl.ds(3 * TALL + MARGIN + ROWS, MARGIN), :] = from_north
+    for out, acc, shift in ((east, acc_east, 64), (west, acc_west, 63)):
+        out[...] = acc
+        out[pl.ds(MARGIN, ROWS), :] = jnp.where(lane_ids(ROWS) == 63, turn(diff[...], shift), acc[MARGIN : MARGIN + ROWS])
+    near, next_to, last = received(NEAR, FULL), received(NEXT, FULL), received(LAST, EDGE)
+    unused = jnp.zeros((STRIP - FULL, LANES), F32)
+    group = lane_ids(STRIP) >> 5
+    for s, own in enumerate((north, south)):
+        pieces = (
+            jnp.concatenate([next_to[s], unused], axis=0),
+            jnp.concatenate([near[s], unused], axis=0),
+            own[0:STRIP, :],
+            own[STRIP : 2 * STRIP, :],
+        )
         for r, x in enumerate(pieces):
             strips[pl.ds((4 * s + r) * STRIP, STRIP), :] = x
-            acc_east = jnp.where(group[0:STRIP] == r, turn(x, (32 * (r + 1)) % LANES), acc_east)
-            acc_west = jnp.where(group[0:STRIP] == r, turn(x, 32 * r), acc_west)
-        east[pl.ds(TALL + s * STRIP, STRIP), :] = acc_east
-        west[pl.ds(TALL + s * STRIP, STRIP), :] = acc_west
-        tracer_rows[pl.ds(2 * s * STRIP, STRIP), :] = rim[2 * STRIP : 3 * STRIP]
-        tracer_rows[pl.ds((2 * s + 1) * STRIP, STRIP), :] = rim[0:STRIP]
+            block, g = divmod(4 * s + r, 2)
+            here = pl.ds(block * STRIP, STRIP)
+            east[here, :] = jnp.where(group == 2 + g, turn(x, (96 + 32 * g) % LANES), east[here, :])
+            west[here, :] = jnp.where(group == 2 + g, turn(x, 64 + 32 * g), west[here, :])
+        tracer_rows[pl.ds(2 * s * STRIP, EDGE), :] = last[s]
+        tracer_rows[pl.ds((2 * s + 1) * STRIP, STRIP), :] = pieces[1]
     k = tall[pl.ds(3 * TALL, TALL), :]
     send_a[pl.ds(0, TALL), :] = k
     send_b[pl.ds(0, TALL), :] = k
-    rest = pl.ds(TALL, TALL + 2 * STRIP)
+    rest = pl.ds(TALL, TALL)
     e, w = east[...], west[...]
     send_a[rest, :] = jnp.where(lon_odd, w, e)
     send_b[rest, :] = jnp.where(lon_odd, e, w)
@@ -265,7 +286,7 @@
     level = lev[...].astype(F32)
     level_halo = jnp.where(lanes == LANES - 1, turn(east_cols, 45), turn(west_cols, 47))
     d = diff[...]
-    d_halo = jnp.where(lanes == LANES - 1, turn(east_rest, 31), turn(west_rest, 32))
+    d_halo = jnp.where(lanes == LANES - 1, turn(east_rest, 64), turn(west_rest, 65))
     for n, other in enumerate(sides(level, level_halo, STRIP + 20)):
         face_levels[n] = jnp.minimum(level, other)
     for n, other in enumerate(sides(d, d_halo, 20)):
@@ -325,7 +346,7 @@
 def surface_kernel(
     tall, strips, mean, recv_b, recv_a,
     basis_out, flow, partial, col_patch, row_patch,
-    state, height, flux, slope, basis, weights, diagonal,
+    state, height, heights, transport, force, faces, slope, basis, weights, diagonal,
 ):
     is_odd = odd("lon")
     rows = pl.ds(8, TALL)
@@ -337,15 +358,15 @@
         got_b = recv_b[here, :]
         return jnp.where(is_odd, got_b, got_a), jnp.where(is_odd, got_a, got_b)
 
-    def ghost(east, west, f):
+    def ghost(east, west, first, count):
         return jnp.where(
-            lane_ids(east.shape[0]) < 64, turn(east, (LANES - 32 * f) % LANES), turn(west, (96 - 32 * f) % LANES)
+            lane_ids(east.shape[0]) < 64, turn(east, (LANES - first) % LANES), turn(west, LANES - first - count)
         )
 
     from_east, from_west = received(TALL, TALL)
     for f in range(3):
         state[f, 0, rows, :] = tall[pl.ds(f * TALL, TALL), :]
-        state[f, 1, rows, :] = ghost(from_east, from_west, f)
+        state[f, 1, rows, :] = ghost(from_east, from_west, f * WIDE, WIDE)
     last = lanes == LANES - 1
     first = lanes == 0
 
@@ -390,11 +411,11 @@
     is_plane = number < PLANES
     not_last = lane_ids(STRIP) < LANES - 1
     for s in range(2):
-        from_east, from_west = received(2 * TALL + s * STRIP, STRIP)
         x, wet, v, deep = [], [], [], []
         for r in range(4):
             centre = strips[pl.ds((4 * s + r) * STRIP, STRIP), :]
-            both = (centre, ghost(from_east, from_west, r))
+            block, g = divmod(4 * s + r, 2)
+            both = (centre, ghost(*received(TALL + block * STRIP, STRIP), 64 + 32 * g, 32))
             deep.append([b[20:21] for b in both])
             v.append([jnp.broadcast_to(b[21:22], (STRIP, LANES)) for b in both])
             wet.append([jnp.where(is_plane & (level_of_row < b[20:21]), 1.0, 0.0) for b in both])
@@ -450,35 +471,63 @@
         started = state[comp, 0, pl.ds(8 + MARGIN, ROWS), :] - tall[pl.ds(comp * TALL + MARGIN, ROWS), :]
         flow[here, :] = -(started + mean[here, :])
 
-    for half in range(2):
-        slope[half, rows, :] = jnp.where(state[2, half, rows, :] > 0.0, SLOPE, 0.0)
-        height[half, rows, :] = jnp.zeros((TALL, LANES), F32)
-
     halves = range(2)
-
-    def subcycle(cut, step, carry):
+    ahead = lanes[0:8] >= LANES - 2
+    behind = lanes[0:8] < 2
+
+    def far_sides(a, b):
+        ea, eb, wa, wb = turn(a, LANES - 2), turn(b, LANES - 2), turn(a, 2), turn(b, 2)
+        return (
+            (jnp.where(ahead, eb, ea), jnp.where(ahead, ea, eb)),
+            (jnp.where(behind, wb, wa), jnp.where(behind, wa, wb)),
+        )
+
+    for half in halves:
+        d = state[2, half, rows, :]
+        slope[half, rows, :] = jnp.where(d > 0.0, SLOPE, 0.0)
+        force[half, rows, :] = SLOPE * d
+        transport[half, rows, :] = d * state[1, half, rows, :]
+    tiles = range(8, 8 + TALL, 8)
+    for tile in tiles:
+        here, above, below = (pl.ds(tile + off, 8) for off in (0, 1, -1))
+        east, west = lane_sides(force[0, here, :], force[1, here, :])
+        for h in halves:
+            faces[0, h, here, :] = east[h]
+            faces[1, h, here, :] = west[h]
+            faces[2, h, here, :] = force[h, above, :]
+            faces[3, h, here, :] = force[h, below, :]
+    for tile in tiles:
+        here, above, below = (pl.ds(tile + off, 8) for off in (0, 1, -1))
+        east, west = lane_sides(*(state[2, h, here, :] * state[0, h, here, :] for h in halves))
+        for h in halves:
+            divergence = (east[h] - west[h]) + (transport[h, above, :] - transport[h, below, :])
+            force[h, here, :] = divergence
+            new = -slope[h, here, :] * divergence
+            heights[0, h, here, :] = new
+            height[h, here, :] = new
+    for step in range(1, SUBCYCLES):
+        cut = min(8 * ((6 + 2 * step) // 8), 16)
+        now, later = heights.at[(step - 1) % 2], heights.at[step % 2]
         for tile in range(8 + cut, 8 + TALL - cut, 8):
-            here, above, below = (pl.ds(tile + off, 8) for off in (0, 1, -1))
-            east, west = lane_sides(*(state[2, h, here, :] * state[0, h, here, :] for h in halves))
-            for h in halves:
-                north = state[2, h, above, :] * state[1, h, above, :]
-                south = state[2, h, below, :] * state[1, h, below, :]
-                divergence = (east[h] - west[h]) + (north - south)
-                height[h, here, :] = height[h, here, :] - slope[h, here, :] * divergence
-        for tile in range(8 + cut, 8 + TALL - cut, 8):
-            here, above, below = (pl.ds(tile + off, 8) for off in (0, 1, -1))
-            east, west = lane_sides(height[0, here, :], height[1, here, :])
-            for h in halves:
-                factor = slope[h, here, :]
-                state[0, h, here, :] = state[0, h, here, :] - factor * (east[h] - west[h])
-                state[1, h, here, :] = state[1, h, here, :] - factor * (height[h, above, :] - height[h, below, :])
-        return carry
-
-    for cut, start, stop in ((0, 0, 1), (8, 1, 5), (16, 5, SUBCYCLES)):
-        lax.fori_loop(start, stop, functools.partial(subcycle, cut), 0, unroll=True)
-    for comp in range(2):
+            here, above, below = (pl.ds(tile + off, 8) for off in (0, 2, -2))
+            centres = [now[h, here, :] for h in halves]
+            east, west = far_sides(*centres)
+            for h, x in enumerate(centres):
+                along = faces[0, h, here, :] * (east[h] - x) - faces[1, h, here, :] * (x - west[h])
+                across = faces[2, h, here, :] * (now[h, above, :] - x) - faces[3, h, here, :] * (x - now[h, below, :])
+                change = force[h, here, :] - (along + across)
+                force[h, here, :] = change
+                new = x - slope[h, here, :] * change
+                later[h, here, :] = new
+                height[h, here, :] = height[h, here, :] + new
+    mine = pl.ds(8 + MARGIN, ROWS)
+    east, west = lane_sides(height[0, mine, :], height[1, mine, :])
+    inner = slope[0, mine, :]
+    north, south = (height[0, pl.ds(8 + MARGIN + off, ROWS), :] for off in (1, -1))
+    for comp, gradient in enumerate((east[0] - west[0], north - south)):
         here = pl.ds(comp * ROWS, ROWS)
-        flow[here, :] = flow[here, :] + state[comp, 0, pl.ds(8 + MARGIN, ROWS), :]
+        flow[here, :] = flow[here, :] + (state[comp, 0, mine, :] - inner * gradient)
+    final = heights.at[(SUBCYCLES - 1) % 2]
     scale = 2.0 / RADIUS
     short = ROWS + 16
     base = MARGIN
@@ -507,17 +556,17 @@
                 weights[n - 1, h, here, :] = scale * w
                 total += w
             diagonal[h, here, :] = scale * (total - CENTRE)
-            basis[0, h, pl.ds(base + tile, 8), :] = height[h, pl.ds(base + tile, 8), :]
+            basis[0, h, pl.ds(base + tile, 8), :] = final[h, pl.ds(base + tile, 8), :]
 
     def applied(source, tile, count=2):
         around = nine(lambda h, where: basis[source, h, where, :], tile)
         out = []
         for h in range(count):
             here = pl.ds(tile, 8)
-            total = diagonal[h, here, :] * around[h][0]
-            for n in range(1, 9):
-                total -= weights[n - 1, h, here, :] * around[h][n]
-            out.append(total)
+            terms = [weights[n - 1, h, here, :] * around[h][n] for n in range(1, 9)]
+            while len(terms) > 1:
+                terms = [a + b for a, b in zip(terms[::2], terms[1::2])]
+            out.append(diagonal[h, here, :] * around[h][0] - terms[0])
         return out
 
     for tile in tiles:
@@ -702,7 +751,7 @@
     tall, strips, tracer_rows, send_a, send_b = call(
         widen_kernel,
         [(4 * TALL, LANES), (8 * STRIP, LANES), (4 * STRIP, LANES), (LON_SEND, LANES), (LON_SEND, LANES)],
-        [(TALL + 2 * STRIP, LANES)] * 2,
+        [(TALL, LANES)] * 2,
         10**6,
         fields, cols, diffusivity, north, south, got_b, got_a,
     )
@@ -717,7 +766,7 @@
     basis, flow, partial, col_patch, row_patch = call(
         surface_kernel,
         [(SOLVE_ITERS,) + short, (2 * ROWS, LANES), (lon * lat, LANES), block, (4 * STRIP, LANES)],
-        [(3,) + padded, padded, padded, padded, (SOLVE_ITERS + 1,) + padded, (8,) + short, short],
+        [(3,) + padded, padded, (2,) + padded, padded, padded, (4,) + padded, padded, (SOLVE_ITERS + 1,) + padded, (8,) + short, short],
         10**7,
         tall, strips, mean, got_b, got_a,
     )

time: 47.6 us -> 46.6 us (0.979)
  Pallas kernels: 10 us -> 9.5 us
    pallas_call x6, Pallas kernels: 10 us -> 9.5 us  [call(): pl.pallas_call(kernel, out_shape=out, in_specs=[pl.BlockSpec(memory_space...]
where the time goes in v6:
time: 46.6 us; the launch traced here: 46.4 us
  starting transfers between devices  26.2 us (56%)
  Pallas kernels  9.5 us (20%)
  waiting for transfers between devices  9.3 us (20%)
  local copies, waits for them, and re-layouts  0.77 us (2%)
  between operations  0.7 us (2%)
    all_to_all x1, starting transfers between devices, per_device(): gathered = lax.all_to_all(partial, BOTH, 0, 0, tiled=True)  14.1 us
    ppermute x4, starting transfers between devices, swap(): return lax.ppermute(x, BOTH, pairs)  12.1 us
    pallas_call x6, Pallas kernels, call(): pl.pallas_call(kernel, out_shape=out, in_specs=[pl.BlockSpec(memory_space...  9.5 us
    all_to_all x1, waiting for transfers between devices, per_device(): gathered = lax.all_to_all(partial, BOTH, 0, 0, tiled=True)  6.55 us
    ppermute x4, waiting for transfers between devices, swap(): return lax.ppermute(x, BOTH, pairs)  2.75 us
  transfers between devices with their start and end apart: 5, of which 3 were waited for; matrix products, arithmetic and copies ran while one was open for 0% of the time, Pallas kernels for 5%

profile of v6, /device:TPU:1, one launch (start us, length us, event | category | flops | bytes accessed | tf_op | source)
XLA Modules:
  0.0 46.4 jit_solution(12369920970014037027)
XLA Ops:
  0.6 0.0 copy-start.1
  0.6 2.6 %shard_map.94 = (f32[1280,128]{1,0:T(8,128)S(1)}, f32[128,128]{1,0:T(8,128)S(1)}, f32[192,128]{1,0:T(8,128)S(1)}, f32[64,128]{1,0:T(8,128)S(1)}, f32[72,128]{1,0...) custom-call(f32[1280,128]{1,0:T(8,128)} %bitcast.13, f32[1280,128]{1,0:T(8,128)} %bitcast.9, ...), custom_call_target="tpu_custom_call" | custom-call | flops 10000000 | bytes 2588672 | tf_op jit(solution)/shard_map/pallas_call | solution.py:701
  3.2 0.7 %collective-permute-start = (f32[152,128]{1,0:T(8,128)S(1)}, f32[152,128]{1,0:T(8,128)S(1)}, u32[]{:S(2)}, u32[]{:S(2)}) collective-permute-start(f32[152,128]{1,0:T(8,128)S(1)} %get-tuple-element.27), channel_id=1, source_target_pairs={{1,2},{2,1},{3,4},{4,3},{5,6},{6,5},{7,127},{9,10},{10,9},{11,12},... | collective-permute-start | bytes 233480 | tf_op jit(solution)/shard_map/ppermute | solution.py:732
  3.9 4.6 %collective-permute-start.1 = (f32[152,128]{1,0:T(8,128)S(1)}, f32[152,128]{1,0:T(8,128)S(1)}, u32[]{:S(2)}, u32[]{:S(2)}) collective-permute-start(f32[152,128]{1,0:T(8,128)S(1)} %get-tuple-element.28), channel_id=1, source_target_pairs={{0,1},{1,0},{2,3},{3,2},{4,5},{5,4},{6,7},{7,6},{8,9},{9,8},{10,11... | collective-permute-start | bytes 233480 | tf_op jit(solution)/shard_map/ppermute | solution.py:732
  8.5 0.0 collective-permute-done.recv_b
  8.5 1.8 %collective-permute-done.1.recv_a = f32[152,128]{1,0:T(8,128)S(1)} collective-permute-done((f32[152,128]{1,0:T(8,128)S(1)}, f32[152,128]{1,0:T(8,128)S(1)}, u32[]{:S(2)}, u32[]{:S(2)}) %collective-permute-start.1) | collective-permute-done | bytes 77856 | tf_op jit(solution)/shard_map/ppermute | solution.py:732
  10.3 0.0 copy-done.1
  10.3 0.2 shard_map.95
  10.5 3.4 %collective-permute-start.2 = (f32[224,128]{1,0:T(8,128)S(1)}, f32[224,128]{1,0:T(8,128)S(1)}, u32[]{:S(2)}, u32[]{:S(2)}) collective-permute-start(f32[224,128]{1,0:T(8,128)S(1)} %get-tuple-element.30), channel_id=1, source_target_pairs={{0,120},{1,121},{2,122},{3,123},{4,124},{5,125},{6,126},{7,127},{8... | collective-permute-start | bytes 344072 | tf_op jit(solution)/shard_map/ppermute | solution.py:732
  13.9 3.4 %collective-permute-start.3 = (f32[224,128]{1,0:T(8,128)S(1)}, f32[224,128]{1,0:T(8,128)S(1)}, u32[]{:S(2)}, u32[]{:S(2)}) collective-permute-start(f32[224,128]{1,0:T(8,128)S(1)} %get-tuple-element.31), channel_id=1, source_target_pairs={{0,8},{1,9},{2,10},{3,11},{4,12},{5,13},{6,14},{7,15},{8,0},{9,1},... | collective-permute-start | bytes 344072 | tf_op jit(solution)/shard_map/ppermute | solution.py:732
  17.3 0.0 collective-permute-done.2.recv_b
  17.3 1.0 %collective-permute-done.3.recv_a = f32[224,128]{1,0:T(8,128)S(1)} collective-permute-done((f32[224,128]{1,0:T(8,128)S(1)}, f32[224,128]{1,0:T(8,128)S(1)}, u32[]{:S(2)}, u32[]{:S(2)}) %collective-permute-start.3) | collective-permute-done | bytes 114720 | tf_op jit(solution)/shard_map/ppermute | solution.py:732
  18.3 3.3 %shard_map.97 = (f32[4,2,80,128]{3,2,1,0:T(8,128)S(1)}, f32[128,128]{1,0:T(8,128)S(1)}, f32[128,128]{1,0:T(8,128)}, f32[64,128]{1,0:T(8,128)S(1)}, f32[96,128]{1,0:T(8,128)S(1)}) custom-call(f32[448,128]{1,0:T(8,128)S(1)} %get-tuple-element.32.tall, f32[192,128]{1,0:T(8,128)S(1)} %get-tuple-element.33.strips, f32[128,128]{1,0:T(8,128)S(1)} %get-tuple-element.34.mean, ...), custom_call_target="tpu_custom_call" | custom-call | flops 10000000 | bytes 1163264 | tf_op jit(solution)/shard_map/pallas_call | solution.py:701
  21.6 14.1 %all-to-all-start = ((f32[128,1,128]{2,1,0:T(1,128)}), f32[128,1,128]{2,1,0:T(1,128)S(1)}, u32[]{:S(2)}, u32[]{:S(2)}) async-start(f32[128,1,128]{2,1,0:T(1,128)} %bitcast.5), calls=%async_computation | async-start | bytes 131072 | tf_op jit(solution)/shard_map/all_to_all | solution.py:773
  35.7 0.0 copy-start
  35.7 0.0 copy-start.2
  35.7 0.3 shard_map.98.star
  36.0 0.8 %copy-done = f32[2,10,64,128]{3,2,1,0:T(8,128)S(1)} copy-done((f32[2,10,64,128]{3,2,1,0:T(8,128)S(1)}, f32[2,10,64,128]{3,2,1,0:T(8,128)}, u32[]{:S(2)}) %copy-start) | copy-done | bytes 655384
  36.8 0.0 copy-done.2
  36.8 1.9 %shard_map.96 = f32[1280,128]{1,0:T(8,128)} custom-call(f32[1280,128]{1,0:T(8,128)S(1)} %bitcast.10, s32[64,128]{1,0:T(8,128)S(1)} %copy-done.2, f32[64,128]{1,0:T(8,128)S(1)} %copy-done.1, f32[96,128]{1,0:T(8,128)S(1)} %get-tuple-element.29.tracer_rows, f32[224,128]{1,0:T(8,128)S(1)} %collective-permute-done.2.recv_b, ...), custom_call_target="tpu_custom_call" | custom-call | flops 1000000 | bytes 1654784 | tf_op jit(solution)/shard_map/pallas_call | solution.py:701
  38.7 6.5 %all-to-all-done = f32[128,1,128]{2,1,0:T(1,128)S(1)} async-done(((f32[128,1,128]{2,1,0:T(1,128)}), f32[128,1,128]{2,1,0:T(1,128)S(1)}, u32[]{:S(2)}, u32[]{:S(2)}) %all-to-all-start) | async-done | bytes 65568 | tf_op jit(solution)/shard_map/all_to_all | solution.py:773
  45.2 1.2 %shard_map.99 = (f32[1280,128]{1,0:T(8,128)}, f32[64,128]{1,0:T(8,128)}) custom-call(f32[128,128]{1,0:T(8,128)S(1)} %bitcast.11, f32[4,2,80,128]{3,2,1,0:T(8,128)S(1)} %get-tuple-element.36.basis, f32[128,128]{1,0:T(8,128)S(1)} %get-tuple-element.37.flow, f32[1280,128]{1,0:T(8,128)S(1)} %shard_map.98.star, s32[64,128]{1,0:T(8,128)S(1)} %copy-done.2), custom_call_target="tpu_custom_call" | custom-call | flops 1000000 | bytes 1835008 | tf_op jit(solution)/shard_map/pallas_call | solution.py:701
Async XLA Ops:
  0.6 9.6 %copy-start.1 = (f32[64,128]{1,0:T(8,128)S(1)}, f32[64,128]{1,0:T(8,128)}, u32[]{:S(2)}) copy-start(f32[64,128]{1,0:T(8,128)} %diff.3) | copy-start | bytes 98308
  3.2 5.3 %collective-permute-start = (f32[152,128]{1,0:T(8,128)S(1)}, f32[152,128]{1,0:T(8,128)S(1)}, u32[]{:S(2)}, u32[]{:S(2)}) collective-permute-start(f32[152,128]{1,0:T(8,128)S(1)} %get-tuple-element.27), channel_id=1, source_target_pairs={{1,2},{2,1},{3,4},{4,3},{5,6},{6,5},{7,127},{9,10},{10,9},{11,12},... | collective-permute-start | bytes 233480 | tf_op jit(solution)/shard_map/ppermute | solution.py:732
  3.9 6.4 %collective-permute-start.1 = (f32[152,128]{1,0:T(8,128)S(1)}, f32[152,128]{1,0:T(8,128)S(1)}, u32[]{:S(2)}, u32[]{:S(2)}) collective-permute-start(f32[152,128]{1,0:T(8,128)S(1)} %get-tuple-element.28), channel_id=1, source_target_pairs={{0,1},{1,0},{2,3},{3,2},{4,5},{5,4},{6,7},{7,6},{8,9},{9,8},{10,11... | collective-permute-start | bytes 233480 | tf_op jit(solution)/shard_map/ppermute | solution.py:732
  10.5 6.9 %collective-permute-start.2 = (f32[224,128]{1,0:T(8,128)S(1)}, f32[224,128]{1,0:T(8,128)S(1)}, u32[]{:S(2)}, u32[]{:S(2)}) collective-permute-start(f32[224,128]{1,0:T(8,128)S(1)} %get-tuple-element.30), channel_id=1, source_target_pairs={{0,120},{1,121},{2,122},{3,123},{4,124},{5,125},{6,126},{7,127},{8... | collective-permute-start | bytes 344072 | tf_op jit(solution)/shard_map/ppermute | solution.py:732
  13.9 4.4 %collective-permute-start.3 = (f32[224,128]{1,0:T(8,128)S(1)}, f32[224,128]{1,0:T(8,128)S(1)}, u32[]{:S(2)}, u32[]{:S(2)}) collective-permute-start(f32[224,128]{1,0:T(8,128)S(1)} %get-tuple-element.31), channel_id=1, source_target_pairs={{0,8},{1,9},{2,10},{3,11},{4,12},{5,13},{6,14},{7,15},{8,0},{9,1},... | collective-permute-start | bytes 344072 | tf_op jit(solution)/shard_map/ppermute | solution.py:732
  21.6 23.6 %all-to-all-start = ((f32[128,1,128]{2,1,0:T(1,128)}), f32[128,1,128]{2,1,0:T(1,128)S(1)}, u32[]{:S(2)}, u32[]{:S(2)}) async-start(f32[128,1,128]{2,1,0:T(1,128)} %bitcast.5), calls=%async_computation | async-start | bytes 131072 | tf_op jit(solution)/shard_map/all_to_all | solution.py:773
  35.7 1.1 %copy-start = (f32[2,10,64,128]{3,2,1,0:T(8,128)S(1)}, f32[2,10,64,128]{3,2,1,0:T(8,128)}, u32[]{:S(2)}) copy-start(f32[2,10,64,128]{3,2,1,0:T(8,128)} %param.7) | copy-start | bytes 1966084
  35.7 1.1 %copy-start.2 = (s32[64,128]{1,0:T(8,128)S(1)}, s32[64,128]{1,0:T(8,128)}, u32[]{:S(2)}) copy-start(s32[64,128]{1,0:T(8,128)} %lev.3) | copy-start | bytes 98308

commit v7 on v6

--- a/solution.py
+++ b/solution.py
@@ -79,9 +79,12 @@
 def block_kernel(
     vel_far, tra_far, lev_far, visc_far, diff_far, depth_far, wind_far,
     star, mean, fields, cols, north, south, send_a, send_b,
-    faces, face_levels, sums, turning, vel, tra, visc, diff, depth, wind, levels_kept, laps, lev, done,
+    faces, face_levels, sums, turning, vel, tra_north, tra_south, visc, diff, depth, wind, levels_kept, laps, lev, done,
 ):
-    pairs = ((lev_far, lev), (visc_far, visc), (vel_far, vel), (tra_far, tra), (wind_far, wind), (depth_far, depth), (diff_far, diff))
+    pairs = (
+        (lev_far, lev), (visc_far, visc), (vel_far, vel), (tra_far.at[:, pl.ds(ROWS - 8, 8)], tra_north),
+        (tra_far.at[:, pl.ds(0, 8)], tra_south), (wind_far, wind), (depth_far, depth), (diff_far, diff),
+    )
     copies = [
         pltpu.make_async_copy(far, near.at[pl.ds(8, PLANES * ROWS)] if near is vel else near, done.at[n])
         for n, (far, near) in enumerate(pairs)
@@ -150,11 +153,6 @@
     for copy in copies[3:]:
         copy.wait()
 
-    def tracer_step(p, acc):
-        t = tra[pl.ds(pl.multiple_of(p * ROWS, ROWS), ROWS), :]
-        return jnp.where((lanes >> 1) == 44 + p, turn(t, lax.rem(89 + 2 * p, LANES)), acc)
-
-    cols[...] = lax.fori_loop(0, PLANES, tracer_step, cols[...], unroll=True)
     ocean = levels > 0.0
     for comp in range(2):
         here = pl.ds(comp * ROWS, ROWS)
@@ -162,14 +160,14 @@
         mean[here, :] = column_mean
         fields[here, :] = column_mean + jnp.where(ocean, wind[here, :], 0.0)
     fields[pl.ds(2 * ROWS, ROWS), :] = jnp.where(ocean, depth[...], 0.0)
-    for edge, step, out in ((ROWS - 1, -1, north), (0, 1, south)):
+    for edge, step, out, tra in ((ROWS - 1, -1, north, tra_north), (0, 1, south, tra_south)):
         out[...] = jnp.zeros((RIMS, LANES), F32)
         for d in range(2):
             r = edge + d * step
             out[pl.ds(d * STRIP, PLANES), :] = vel[pl.ds(8 + r, PLANES, stride=ROWS), :]
             out[pl.ds(d * STRIP + 20, 1), :] = levels[r : r + 1]
             out[pl.ds(d * STRIP + 21, 1), :] = visc[pl.ds(r, 1), :]
-        out[pl.ds(2 * STRIP, PLANES), :] = tra[pl.ds(edge, PLANES, stride=ROWS), :]
+        out[pl.ds(2 * STRIP, PLANES), :] = tra[:, edge % 8, :]
         out[pl.ds(2 * STRIP + 20, 1), :] = diff[pl.ds(edge, 1), :]
     lat_odd = odd("lat")
 
@@ -201,7 +199,17 @@
         send_b[pl.ds(COLS, MARGIN), :] = jnp.where(lane_ids(MARGIN) < 4 * PLANES, -turned, turned)
 
 
-def widen_kernel(fields, cols, diff, north, south, recv_b, recv_a, tall, strips, tracer_rows, send_a, send_b, east, west):
+def tracer_rim_kernel(tra, out):
+    lanes = lane_ids(ROWS)
+
+    def tracer_step(p, acc):
+        t = tra[pl.ds(pl.multiple_of(p * ROWS, ROWS), ROWS), :]
+        return jnp.where((lanes >> 1) == 44 + p, turn(t, lax.rem(89 + 2 * p, LANES)), acc)
+
+    out[...] = lax.fori_loop(0, PLANES, tracer_step, jnp.zeros((ROWS, LANES), F32), unroll=True)
+
+
+def widen_kernel(fields, cols, tracer_cols, diff, north, south, recv_b, recv_a, tall, strips, tracer_rows, send_a, send_b, east, west):
     lat_odd = odd("lat")
     lon_odd = odd("lon")
     def received(start, count):
@@ -227,7 +235,7 @@
         acc_west = jnp.where(here, turn(x, f * WIDE), acc_west)
     from_north, from_south = received(COLS, MARGIN)
     tall[pl.ds(3 * TALL, MARGIN), :] = from_south
-    tall[pl.ds(3 * TALL + MARGIN, ROWS), :] = cols[...]
+    tall[pl.ds(3 * TALL + MARGIN, ROWS), :] = jnp.where(lane_ids(ROWS) < 88, cols[...], tracer_cols[...])
     tall[pl.ds(3 * TALL + MARGIN + ROWS, MARGIN), :] = from_north
     for out, acc, shift in ((east, acc_east, 64), (west, acc_west, 63)):
         out[...] = acc
@@ -316,27 +324,25 @@
     group = lanes >> 2
 
     levels = pick(strip, phase + 80)
-    v = pick(strip, phase + 84)
-    number = jnp.where(group >= LEVELS, group - LEVELS, group).astype(F32)
-    wet = jnp.where((number < levels) & (group < PLANES), 1.0, 0.0)
-    x = jnp.where(group < PLANES, strip, 0.0)
+    v = 0.5 * pick(strip, phase + 84)
+    number = jnp.where(group >= LEVELS, group - LEVELS, group)
+    number = jnp.where(group < PLANES, number, LEVELS).astype(F32)
+    wet = jnp.where(number < levels, 1.0, 0.0)
+    x = strip
     open_e = wet * turn(wet, LANES - 1)
-    wet_n = pltpu.roll(wet, rows - 1, 0)
-    open_n = wet * wet_n
+    open_n = wet * pltpu.roll(wet, rows - 1, 0)
     flux_e = open_e * (turn(x, LANES - 1) - x)
     flux_n = open_n * (pltpu.roll(x, rows - 1, 0) - x)
-    lap = flux_e - turn(flux_e, 1) + flux_n - pltpu.roll(flux_n, 1, 0)
+    lap = (flux_e - turn(flux_e, 1)) + (flux_n - pltpu.roll(flux_n, 1, 0))
     seam = jnp.where(phase == 1, flux_e, 0.0)
-    added = seam - turn(seam, 1)
-    base = jnp.where(phase == 1, lap, added)
-    other = jnp.where(phase == 1, turn(lap, LANES - 1), turn(added, LANES - 1))
-    face = 0.5 * (v + turn(v, LANES - 1)) * open_e
-    flux_e = jnp.where(phase == 3, 0.0, face * (other - base))
+    seam_west = turn(seam, 1)
+    added = seam - seam_west
+    step = jnp.where(phase == 1, turn(lap, LANES - 1) - lap, turn(seam, LANES - 1) + seam_west)
+    flux_e = (v + turn(v, LANES - 1)) * open_e * step
     in_block = (ids != MARGIN - 1) & (ids != MARGIN + ROWS - 1)
-    face = jnp.where(in_block, 0.5 * (v + pltpu.roll(v, rows - 1, 0)) * open_n, 0.0)
+    face = jnp.where(in_block, (v + pltpu.roll(v, rows - 1, 0)) * open_n, 0.0)
     flux_n = face * (pltpu.roll(added, rows - 1, 0) - added)
-    second = flux_e - turn(flux_e, 1) + flux_n - pltpu.roll(flux_n, 1, 0)
-    return wet * second
+    return (flux_e - turn(flux_e, 1)) + (flux_n - pltpu.roll(flux_n, 1, 0))
 
 
 def gram_pairs():
@@ -346,7 +352,7 @@
 def surface_kernel(
     tall, strips, mean, recv_b, recv_a,
     basis_out, flow, partial, col_patch, row_patch,
-    state, height, heights, transport, force, faces, slope, basis, weights, diagonal,
+    state, height, heights, transport, force, faces, slope, basis, weights, diagonal, sides,
 ):
     is_odd = odd("lon")
     rows = pl.ds(8, TALL)
@@ -457,7 +463,7 @@
                 -across[2],
             )
             for r in range(4):
-                change = wet[r][h] * second[r]
+                change = second[r]
                 if h == 0 and r >= 2:
                     row_patch[pl.ds((2 * s + r - 2) * STRIP, STRIP), :] = change
                 where = 8 + MARGIN + ((ROWS + 1 - r) if s == 0 else (r - 2))
@@ -534,53 +540,62 @@
 
     tiles = range(0, short, 8)
 
-    def nine(read, tile):
-        out = [[], []]
+    def spin(tile, a, b):
+        here = pl.ds(base + tile, 8)
+        for n, pair in enumerate(lane_sides(a, b)):
+            for h in halves:
+                sides[n, h, here, :] = pair[h]
+
+    def nine(read, tile, h):
+        out = []
         for off in (0, 1, -1):
-            a, b = (read(h, pl.ds(base + tile + off, 8)) for h in halves)
-            east, west = lane_sides(a, b)
-            for h, centre in enumerate((a, b)):
-                out[h] += [centre, east[h], west[h]]
+            where = pl.ds(base + tile + off, 8)
+            out += [read(h, where), sides[0, h, where, :], sides[1, h, where, :]]
         return out
 
+    for tile in tiles:
+        here = pl.ds(base + tile, 8)
+        spin(tile, state[2, 0, here, :], state[2, 1, here, :])
     for tile in tiles:
         here = pl.ds(tile, 8)
-        around = nine(lambda h, where: state[2, h, where, :], tile)
         for h in halves:
-            d = around[h][0]
+            around = nine(lambda h, where: state[2, h, where, :], tile, h)
+            d = around[0]
             wet = d > 0.0
             total = jnp.where(wet, 0.05, 1.0)
             for n in range(1, 9):
                 factor = 0.5 if n in (1, 2, 3, 6) else 0.25
-                w = jnp.where(wet & (around[h][n] > 0.0), factor * (d + around[h][n]), 0.0)
+                w = jnp.where(wet & (around[n] > 0.0), factor * (d + around[n]), 0.0)
                 weights[n - 1, h, here, :] = scale * w
                 total += w
             diagonal[h, here, :] = scale * (total - CENTRE)
-            basis[0, h, pl.ds(base + tile, 8), :] = final[h, pl.ds(base + tile, 8), :]
-
-    def applied(source, tile, count=2):
-        around = nine(lambda h, where: basis[source, h, where, :], tile)
-        out = []
-        for h in range(count):
-            here = pl.ds(tile, 8)
-            terms = [weights[n - 1, h, here, :] * around[h][n] for n in range(1, 9)]
-            while len(terms) > 1:
-                terms = [a + b for a, b in zip(terms[::2], terms[1::2])]
-            out.append(diagonal[h, here, :] * around[h][0] - terms[0])
-        return out
+
+    def applied(source, tile, h):
+        around = nine(lambda h, where: basis[source, h, where, :], tile, h)
+        here = pl.ds(tile, 8)
+        terms = [weights[n - 1, h, here, :] * around[n] for n in range(1, 9)]
+        while len(terms) > 1:
+            terms = [a + b for a, b in zip(terms[::2], terms[1::2])]
+        return diagonal[h, here, :] * around[0] - terms[0]
 
     for tile in tiles:
-        for h, x in enumerate(applied(0, tile)):
-            basis[1, h, pl.ds(base + tile, 8), :] = 0.5 * x
-
-    for k in range(1, SOLVE_ITERS - 1):
+        here = pl.ds(base + tile, 8)
+        pair = [final[h, here, :] for h in halves]
+        for h in halves:
+            basis[0, h, here, :] = pair[h]
+        spin(tile, *pair)
+    for k in range(1, SOLVE_ITERS):
         for tile in tiles:
             here = pl.ds(base + tile, 8)
-            for h, x in enumerate(applied(k, tile)):
-                basis[k + 1, h, here, :] = x - basis[k - 1, h, here, :]
+            for h in halves:
+                x = applied(k - 1, tile, h)
+                basis[k, h, here, :] = 0.5 * x if k == 1 else x - basis[k - 2, h, here, :]
+        for tile in tiles:
+            here = pl.ds(base + tile, 8)
+            spin(tile, basis[k, 0, here, :], basis[k, 1, here, :])
     for tile in tiles[1:-1]:
         here = pl.ds(base + tile, 8)
-        basis[SOLVE_ITERS, 0, here, :] = applied(SOLVE_ITERS - 1, tile, 1)[0] - basis[SOLVE_ITERS - 2, 0, here, :]
+        basis[SOLVE_ITERS, 0, here, :] = applied(SOLVE_ITERS - 1, tile, 0) - basis[SOLVE_ITERS - 2, 0, here, :]
     lane = lane_ids(1)
     row = jnp.zeros((1, LANES), F32)
     mine = pl.ds(8 + MARGIN, ROWS)
@@ -739,21 +754,22 @@
     star, mean, fields, cols, north, south, send_a, send_b = call(
         block_kernel,
         [(PLANES * ROWS, LANES), (2 * ROWS, LANES), (3 * ROWS, LANES), block, rim, rim, (LAT_SEND, LANES), (LAT_SEND, LANES)],
-        [(4,) + block, (4,) + block, (2,) + block, block, (PLANES * ROWS + 16, LANES), vel.shape, block, block, block, wind.shape,
+        [(4,) + block, (4,) + block, (2,) + block, block, (PLANES * ROWS + 16, LANES), (PLANES, 8, LANES), (PLANES, 8, LANES), block, block, block, wind.shape,
          block, (PLANES * ROWS + 16, LANES),
-         pltpu.VMEM(block, jnp.int32), pltpu.SemaphoreType.DMA((7,))],
+         pltpu.VMEM(block, jnp.int32), pltpu.SemaphoreType.DMA((8,))],
         10**7,
-        vel, tra, active_levels, viscosity, diffusivity, ocean_depth, wind,
+        vel, tra.reshape(PLANES, ROWS, LANES), active_levels, viscosity, diffusivity, ocean_depth, wind,
         far=True,
     )
     got_a = swap(send_a, lat_a)
     got_b = swap(send_b, lat_b)
+    (tracer_cols,) = call(tracer_rim_kernel, [block], [], 10**5, tra)
     tall, strips, tracer_rows, send_a, send_b = call(
         widen_kernel,
         [(4 * TALL, LANES), (8 * STRIP, LANES), (4 * STRIP, LANES), (LON_SEND, LANES), (LON_SEND, LANES)],
         [(TALL, LANES)] * 2,
         10**6,
-        fields, cols, diffusivity, north, south, got_b, got_a,
+        fields, cols, tracer_cols, diffusivity, north, south, got_b, got_a,
     )
     got_a = swap(send_a, lon_a)
     got_b = swap(send_b, lon_b)
@@ -766,7 +782,7 @@
     basis, flow, partial, col_patch, row_patch = call(
         surface_kernel,
         [(SOLVE_ITERS,) + short, (2 * ROWS, LANES), (lon * lat, LANES), block, (4 * STRIP, LANES)],
-        [(3,) + padded, padded, (2,) + padded, padded, padded, (4,) + padded, padded, (SOLVE_ITERS + 1,) + padded, (8,) + short, short],
+        [(3,) + padded, padded, (2,) + padded, padded, padded, (4,) + padded, padded, (SOLVE_ITERS + 1,) + padded, (8,) + short, short, (2,) + padded],
         10**7,
         tall, strips, mean, got_b, got_a,
     )

time: 46.6 us -> 46.5 us (level)
    pallas_call x6 -> x7, Pallas kernels: 9.5 us -> 9.53 us  [call(): pl.pallas_call(kernel, out_shape=out, in_specs=[pl.BlockSpec(memory_space...]
where the time goes in v7:
time: 46.5 us; the launch traced here: 46.2 us
  starting transfers between devices  26.2 us (56%)
  Pallas kernels  9.53 us (20%)
  waiting for transfers between devices  9.39 us (20%)
  between operations  0.7 us (2%)
    all_to_all x1, starting transfers between devices, per_device(): gathered = lax.all_to_all(partial, BOTH, 0, 0, tiled=True)  14.1 us
    ppermute x4, starting transfers between devices, swap(): return lax.ppermute(x, BOTH, pairs)  12.1 us
    pallas_call x7, Pallas kernels, call(): pl.pallas_call(kernel, out_shape=out, in_specs=[pl.BlockSpec(memory_space...  9.53 us
    all_to_all x1, waiting for transfers between devices, per_device(): gathered = lax.all_to_all(partial, BOTH, 0, 0, tiled=True)  6.88 us
    ppermute x4, waiting for transfers between devices, swap(): return lax.ppermute(x, BOTH, pairs)  2.51 us
  transfers between devices with their start and end apart: 5, of which 3 were waited for; matrix products, arithmetic and copies ran while one was open for 0% of the time, Pallas kernels for 5%

profile of v7, /device:TPU:1, one launch (start us, length us, event | category | flops | bytes accessed | tf_op | source)
XLA Modules:
  0.0 46.2 jit_solution(16069254667350103055)
XLA Ops:
  0.6 0.0 copy-start
  0.6 2.5 %shard_map.94 = (f32[1280,128]{1,0:T(8,128)S(1)}, f32[128,128]{1,0:T(8,128)S(1)}, f32[192,128]{1,0:T(8,128)S(1)}, f32[64,128]{1,0:T(8,128)S(1)}, f32[72,128]{1,0...) custom-call(f32[1280,128]{1,0:T(8,128)} %bitcast.15, ...), custom_call_target="tpu_custom_call" | custom-call | flops 10000000 | bytes 2588672 | tf_op jit(solution)/shard_map/pallas_call | solution.py:716
  3.1 0.7 %collective-permute-start = (f32[152,128]{1,0:T(8,128)S(1)}, f32[152,128]{1,0:T(8,128)S(1)}, u32[]{:S(2)}, u32[]{:S(2)}) collective-permute-start(f32[152,128]{1,0:T(8,128)S(1)} %get-tuple-element.27), channel_id=1, source_target_pairs={{1,2},{2,1},{3,4},{4,3},{5,6},{6,5},{7,127},{9,10},{10,9},{11,12},... | collective-permute-start | bytes 233480 | tf_op jit(solution)/shard_map/ppermute | solution.py:747
  3.8 4.6 %collective-permute-start.1 = (f32[152,128]{1,0:T(8,128)S(1)}, f32[152,128]{1,0:T(8,128)S(1)}, u32[]{:S(2)}, u32[]{:S(2)}) collective-permute-start(f32[152,128]{1,0:T(8,128)S(1)} %get-tuple-element.28), channel_id=1, source_target_pairs={{0,1},{1,0},{2,3},{3,2},{4,5},{5,4},{6,7},{7,6},{8,9},{9,8},{10,11... | collective-permute-start | bytes 233480 | tf_op jit(solution)/shard_map/ppermute | solution.py:747
  8.4 0.0 copy-done
  8.4 0.0 copy-start.2
  8.4 0.2 shard_map.95.tracer_cols
  8.6 0.0 collective-permute-done.recv_b
  8.6 1.5 %collective-permute-done.1.recv_a = f32[152,128]{1,0:T(8,128)S(1)} collective-permute-done((f32[152,128]{1,0:T(8,128)S(1)}, f32[152,128]{1,0:T(8,128)S(1)}, u32[]{:S(2)}, u32[]{:S(2)}) %collective-permute-start.1) | collective-permute-done | bytes 77856 | tf_op jit(solution)/shard_map/ppermute | solution.py:747
  10.1 0.0 copy-done.2
  10.1 0.2 shard_map.96
  10.4 3.4 %collective-permute-start.2 = (f32[224,128]{1,0:T(8,128)S(1)}, f32[224,128]{1,0:T(8,128)S(1)}, u32[]{:S(2)}, u32[]{:S(2)}) collective-permute-start(f32[224,128]{1,0:T(8,128)S(1)} %get-tuple-element.30), channel_id=1, source_target_pairs={{0,120},{1,121},{2,122},{3,123},{4,124},{5,125},{6,126},{7,127},{8... | collective-permute-start | bytes 344072 | tf_op jit(solution)/shard_map/ppermute | solution.py:747
  13.8 3.4 %collective-permute-start.3 = (f32[224,128]{1,0:T(8,128)S(1)}, f32[224,128]{1,0:T(8,128)S(1)}, u32[]{:S(2)}, u32[]{:S(2)}) collective-permute-start(f32[224,128]{1,0:T(8,128)S(1)} %get-tuple-element.31), channel_id=1, source_target_pairs={{0,8},{1,9},{2,10},{3,11},{4,12},{5,13},{6,14},{7,15},{8,0},{9,1},... | collective-permute-start | bytes 344072 | tf_op jit(solution)/shard_map/ppermute | solution.py:747
  17.2 0.0 collective-permute-done.2.recv_b
  17.2 1.0 %collective-permute-done.3.recv_a = f32[224,128]{1,0:T(8,128)S(1)} collective-permute-done((f32[224,128]{1,0:T(8,128)S(1)}, f32[224,128]{1,0:T(8,128)S(1)}, u32[]{:S(2)}, u32[]{:S(2)}) %collective-permute-start.3) | collective-permute-done | bytes 114720 | tf_op jit(solution)/shard_map/ppermute | solution.py:747
  18.2 3.2 %shard_map.98 = (f32[4,2,80,128]{3,2,1,0:T(8,128)S(1)}, f32[128,128]{1,0:T(8,128)S(1)}, f32[128,128]{1,0:T(8,128)}, f32[64,128]{1,0:T(8,128)S(1)}, f32[96,128]{1,0:T(8,128)S(1)}) custom-call(f32[448,128]{1,0:T(8,128)S(1)} %get-tuple-element.32.tall, f32[192,128]{1,0:T(8,128)S(1)} %get-tuple-element.33.strips, f32[128,128]{1,0:T(8,128)S(1)} %get-tuple-element.34.mean, ...), custom_call_target="tpu_custom_call" | custom-call | flops 10000000 | bytes 1163264 | tf_op jit(solution)/shard_map/pallas_call | solution.py:716
  21.4 14.1 %all-to-all-start = ((f32[128,1,128]{2,1,0:T(1,128)}), f32[128,1,128]{2,1,0:T(1,128)S(1)}, u32[]{:S(2)}, u32[]{:S(2)}) async-start(f32[128,1,128]{2,1,0:T(1,128)} %bitcast.6), calls=%async_computation | async-start | bytes 131072 | tf_op jit(solution)/shard_map/all_to_all | solution.py:789
  35.5 0.0 copy-start.1
  35.5 0.3 shard_map.99.star
  35.8 0.4 copy-done.1
  36.3 1.9 %shard_map.97 = f32[1280,128]{1,0:T(8,128)} custom-call(f32[1280,128]{1,0:T(8,128)S(1)} %bitcast.12, s32[64,128]{1,0:T(8,128)S(1)} %copy-done.1, f32[64,128]{1,0:T(8,128)S(1)} %copy-done.2, f32[96,128]{1,0:T(8,128)S(1)} %get-tuple-element.29.tracer_rows, f32[224,128]{1,0:T(8,128)S(1)} %collective-permute-done.2.recv_b, ...), custom_call_target="tpu_custom_call" | custom-call | flops 1000000 | bytes 1654784 | tf_op jit(solution)/shard_map/pallas_call | solution.py:716
  38.1 6.9 %all-to-all-done = f32[128,1,128]{2,1,0:T(1,128)S(1)} async-done(((f32[128,1,128]{2,1,0:T(1,128)}), f32[128,1,128]{2,1,0:T(1,128)S(1)}, u32[]{:S(2)}, u32[]{:S(2)}) %all-to-all-start) | async-done | bytes 65568 | tf_op jit(solution)/shard_map/all_to_all | solution.py:789
  45.0 1.2 %shard_map.100 = (f32[1280,128]{1,0:T(8,128)}, f32[64,128]{1,0:T(8,128)}) custom-call(f32[128,128]{1,0:T(8,128)S(1)} %bitcast.13, f32[4,2,80,128]{3,2,1,0:T(8,128)S(1)} %get-tuple-element.36.basis, f32[128,128]{1,0:T(8,128)S(1)} %get-tuple-element.37.flow, f32[1280,128]{1,0:T(8,128)S(1)} %shard_map.99.star, s32[64,128]{1,0:T(8,128)S(1)} %copy-done.1), custom_call_target="tpu_custom_call" | custom-call | flops 1000000 | bytes 1835008 | tf_op jit(solution)/shard_map/pallas_call | solution.py:716
Async XLA Ops:
  0.6 7.7 %copy-start = (f32[2,10,64,128]{3,2,1,0:T(8,128)S(1)}, f32[2,10,64,128]{3,2,1,0:T(8,128)}, u32[]{:S(2)}) copy-start(f32[2,10,64,128]{3,2,1,0:T(8,128)} %param.7) | copy-start | bytes 1966084
  3.1 5.5 %collective-permute-start = (f32[152,128]{1,0:T(8,128)S(1)}, f32[152,128]{1,0:T(8,128)S(1)}, u32[]{:S(2)}, u32[]{:S(2)}) collective-permute-start(f32[152,128]{1,0:T(8,128)S(1)} %get-tuple-element.27), channel_id=1, source_target_pairs={{1,2},{2,1},{3,4},{4,3},{5,6},{6,5},{7,127},{9,10},{10,9},{11,12},... | collective-permute-start | bytes 233480 | tf_op jit(solution)/shard_map/ppermute | solution.py:747
  3.8 6.4 %collective-permute-start.1 = (f32[152,128]{1,0:T(8,128)S(1)}, f32[152,128]{1,0:T(8,128)S(1)}, u32[]{:S(2)}, u32[]{:S(2)}) collective-permute-start(f32[152,128]{1,0:T(8,128)S(1)} %get-tuple-element.28), channel_id=1, source_target_pairs={{0,1},{1,0},{2,3},{3,2},{4,5},{5,4},{6,7},{7,6},{8,9},{9,8},{10,11... | collective-permute-start | bytes 233480 | tf_op jit(solution)/shard_map/ppermute | solution.py:747
  8.4 1.8 %copy-start.2 = (f32[64,128]{1,0:T(8,128)S(1)}, f32[64,128]{1,0:T(8,128)}, u32[]{:S(2)}) copy-start(f32[64,128]{1,0:T(8,128)} %diff.3) | copy-start | bytes 98308
  10.4 6.9 %collective-permute-start.2 = (f32[224,128]{1,0:T(8,128)S(1)}, f32[224,128]{1,0:T(8,128)S(1)}, u32[]{:S(2)}, u32[]{:S(2)}) collective-permute-start(f32[224,128]{1,0:T(8,128)S(1)} %get-tuple-element.30), channel_id=1, source_target_pairs={{0,120},{1,121},{2,122},{3,123},{4,124},{5,125},{6,126},{7,127},{8... | collective-permute-start | bytes 344072 | tf_op jit(solution)/shard_map/ppermute | solution.py:747
  13.8 4.4 %collective-permute-start.3 = (f32[224,128]{1,0:T(8,128)S(1)}, f32[224,128]{1,0:T(8,128)S(1)}, u32[]{:S(2)}, u32[]{:S(2)}) collective-permute-start(f32[224,128]{1,0:T(8,128)S(1)} %get-tuple-element.31), channel_id=1, source_target_pairs={{0,8},{1,9},{2,10},{3,11},{4,12},{5,13},{6,14},{7,15},{8,0},{9,1},... | collective-permute-start | bytes 344072 | tf_op jit(solution)/shard_map/ppermute | solution.py:747
  21.4 23.6 %all-to-all-start = ((f32[128,1,128]{2,1,0:T(1,128)}), f32[128,1,128]{2,1,0:T(1,128)S(1)}, u32[]{:S(2)}, u32[]{:S(2)}) async-start(f32[128,1,128]{2,1,0:T(1,128)} %bitcast.6), calls=%async_computation | async-start | bytes 131072 | tf_op jit(solution)/shard_map/all_to_all | solution.py:789
  35.5 0.8 %copy-start.1 = (s32[64,128]{1,0:T(8,128)S(1)}, s32[64,128]{1,0:T(8,128)}, u32[]{:S(2)}) copy-start(s32[64,128]{1,0:T(8,128)} %lev.3) | copy-start | bytes 98308

commit v8 on v7

--- a/solution.py
+++ b/solution.py
@@ -212,10 +212,11 @@
 def widen_kernel(fields, cols, tracer_cols, diff, north, south, recv_b, recv_a, tall, strips, tracer_rows, send_a, send_b, east, west):
     lat_odd = odd("lat")
     lon_odd = odd("lon")
+    at_south = lax.axis_index("lat") == 0
     def received(start, count):
         here = pl.ds(start, count)
         got_a = recv_a[here, :]
-        got_b = recv_b[here, :]
+        got_b = jnp.where(at_south, 0.0, recv_b[here, :])
         return jnp.where(lat_odd, got_b, got_a), jnp.where(lat_odd, got_a, got_b)
 
     lanes = lane_ids(TALL)
@@ -735,6 +736,8 @@
                 lat_b.append((index(i, j), index(i, lon - 1 - j)))
             elif i > 0:
                 lat_b.append((index(i, j), index(i + 1 if i % 2 else i - 1, j)))
+            else:
+                lat_b.append((index(i, j), index(i, j ^ 1)))
             lon_a.append((index(i, j), index(i, j ^ 1)))
             lon_b.append((index(i, j), index(i, (j + 1 if j % 2 else j - 1) % lon)))
     return lat_a, lat_b, lon_a, lon_b

time: 46.5 us -> 44.7 us (0.961)
  starting transfers between devices: 26.2 us -> 24.4 us
    ppermute x4, starting transfers between devices: 12.1 us -> 10.2 us  [swap(): return lax.ppermute(x, BOTH, pairs)]
where the time goes in v8:
time: 44.7 us; the launch traced here: 44.4 us
  starting transfers between devices  24.4 us (55%)
  Pallas kernels  9.53 us (21%)
  waiting for transfers between devices  9.38 us (21%)
  between operations  0.7 us (2%)
  local copies, waits for them, and re-layouts  0.45 us (1%)
    all_to_all x1, starting transfers between devices, per_device(): gathered = lax.all_to_all(partial, BOTH, 0, 0, tiled=True)  14.2 us
    ppermute x4, starting transfers between devices, swap(): return lax.ppermute(x, BOTH, pairs)  10.2 us
    pallas_call x7, Pallas kernels, call(): pl.pallas_call(kernel, out_shape=out, in_specs=[pl.BlockSpec(memory_space...  9.53 us
    all_to_all x1, waiting for transfers between devices, per_device(): gathered = lax.all_to_all(partial, BOTH, 0, 0, tiled=True)  6.88 us
    ppermute x4, waiting for transfers between devices, swap(): return lax.ppermute(x, BOTH, pairs)  2.5 us
  transfers between devices with their start and end apart: 5, of which 3 were waited for; matrix products, arithmetic and copies ran while one was open for 0% of the time, Pallas kernels for 5%

profile of v8, /device:TPU:1, one launch (start us, length us, event | category | flops | bytes accessed | tf_op | source)
XLA Modules:
  0.0 44.4 jit_solution(16203371981045091735)
XLA Ops:
  0.6 0.0 copy-start
  0.6 2.5 %shard_map.94 = (f32[1280,128]{1,0:T(8,128)S(1)}, f32[128,128]{1,0:T(8,128)S(1)}, f32[192,128]{1,0:T(8,128)S(1)}, f32[64,128]{1,0:T(8,128)S(1)}, f32[72,128]{1,0...) custom-call(f32[1280,128]{1,0:T(8,128)} %bitcast.15, ...), custom_call_target="tpu_custom_call" | custom-call | flops 10000000 | bytes 2588672 | tf_op jit(solution)/shard_map/pallas_call | solution.py:717
  3.1 1.5 %collective-permute-start = (f32[152,128]{1,0:T(8,128)S(1)}, f32[152,128]{1,0:T(8,128)S(1)}, u32[]{:S(2)}, u32[]{:S(2)}) collective-permute-start(f32[152,128]{1,0:T(8,128)S(1)} %get-tuple-element.27), channel_id=1, source_target_pairs={{0,8},{1,2},{2,1},{3,4},{4,3},{5,6},{6,5},{7,127},{8,0},{9,10},{10... | collective-permute-start | bytes 233480 | tf_op jit(solution)/shard_map/ppermute | solution.py:750
  4.6 1.8 %collective-permute-start.1 = (f32[152,128]{1,0:T(8,128)S(1)}, f32[152,128]{1,0:T(8,128)S(1)}, u32[]{:S(2)}, u32[]{:S(2)}) collective-permute-start(f32[152,128]{1,0:T(8,128)S(1)} %get-tuple-element.28), channel_id=1, source_target_pairs={{0,1},{1,0},{2,3},{3,2},{4,5},{5,4},{6,7},{7,6},{8,9},{9,8},{10,11... | collective-permute-start | bytes 233480 | tf_op jit(solution)/shard_map/ppermute | solution.py:750
  6.4 0.0 copy-done
  6.4 0.0 copy-start.2
  6.4 0.2 shard_map.95.tracer_cols
  6.7 0.0 collective-permute-done.recv_b
  6.7 1.5 %collective-permute-done.1.recv_a = f32[152,128]{1,0:T(8,128)S(1)} collective-permute-done((f32[152,128]{1,0:T(8,128)S(1)}, f32[152,128]{1,0:T(8,128)S(1)}, u32[]{:S(2)}, u32[]{:S(2)}) %collective-permute-start.1) | collective-permute-done | bytes 77856 | tf_op jit(solution)/shard_map/ppermute | solution.py:750
  8.2 0.0 copy-done.2
  8.2 0.2 shard_map.96
  8.4 3.4 %collective-permute-start.2 = (f32[224,128]{1,0:T(8,128)S(1)}, f32[224,128]{1,0:T(8,128)S(1)}, u32[]{:S(2)}, u32[]{:S(2)}) collective-permute-start(f32[224,128]{1,0:T(8,128)S(1)} %get-tuple-element.30), channel_id=1, source_target_pairs={{0,120},{1,121},{2,122},{3,123},{4,124},{5,125},{6,126},{7,127},{8... | collective-permute-start | bytes 344072 | tf_op jit(solution)/shard_map/ppermute | solution.py:750
  11.9 3.4 %collective-permute-start.3 = (f32[224,128]{1,0:T(8,128)S(1)}, f32[224,128]{1,0:T(8,128)S(1)}, u32[]{:S(2)}, u32[]{:S(2)}) collective-permute-start(f32[224,128]{1,0:T(8,128)S(1)} %get-tuple-element.31), channel_id=1, source_target_pairs={{0,8},{1,9},{2,10},{3,11},{4,12},{5,13},{6,14},{7,15},{8,0},{9,1},... | collective-permute-start | bytes 344072 | tf_op jit(solution)/shard_map/ppermute | solution.py:750
  15.3 0.0 collective-permute-done.2.recv_b
  15.3 1.0 %collective-permute-done.3.recv_a = f32[224,128]{1,0:T(8,128)S(1)} collective-permute-done((f32[224,128]{1,0:T(8,128)S(1)}, f32[224,128]{1,0:T(8,128)S(1)}, u32[]{:S(2)}, u32[]{:S(2)}) %collective-permute-start.3) | collective-permute-done | bytes 114720 | tf_op jit(solution)/shard_map/ppermute | solution.py:750
  16.3 3.2 %shard_map.98 = (f32[4,2,80,128]{3,2,1,0:T(8,128)S(1)}, f32[128,128]{1,0:T(8,128)S(1)}, f32[128,128]{1,0:T(8,128)}, f32[64,128]{1,0:T(8,128)S(1)}, f32[96,128]{1,0:T(8,128)S(1)}) custom-call(f32[448,128]{1,0:T(8,128)S(1)} %get-tuple-element.32.tall, f32[192,128]{1,0:T(8,128)S(1)} %get-tuple-element.33.strips, f32[128,128]{1,0:T(8,128)S(1)} %get-tuple-element.34.mean, ...), custom_call_target="tpu_custom_call" | custom-call | flops 10000000 | bytes 1163264 | tf_op jit(solution)/shard_map/pallas_call | solution.py:717
  19.5 14.2 %all-to-all-start = ((f32[128,1,128]{2,1,0:T(1,128)}), f32[128,1,128]{2,1,0:T(1,128)S(1)}, u32[]{:S(2)}, u32[]{:S(2)}) async-start(f32[128,1,128]{2,1,0:T(1,128)} %bitcast.6), calls=%async_computation | async-start | bytes 131072 | tf_op jit(solution)/shard_map/all_to_all | solution.py:792
  33.7 0.0 copy-start.1
  33.7 0.3 shard_map.99.star
  34.0 0.4 copy-done.1
  34.4 1.9 %shard_map.97 = f32[1280,128]{1,0:T(8,128)} custom-call(f32[1280,128]{1,0:T(8,128)S(1)} %bitcast.12, s32[64,128]{1,0:T(8,128)S(1)} %copy-done.1, f32[64,128]{1,0:T(8,128)S(1)} %copy-done.2, f32[96,128]{1,0:T(8,128)S(1)} %get-tuple-element.29.tracer_rows, f32[224,128]{1,0:T(8,128)S(1)} %collective-permute-done.2.recv_b, ...), custom_call_target="tpu_custom_call" | custom-call | flops 1000000 | bytes 1654784 | tf_op jit(solution)/shard_map/pallas_call | solution.py:717
  36.3 6.9 %all-to-all-done = f32[128,1,128]{2,1,0:T(1,128)S(1)} async-done(((f32[128,1,128]{2,1,0:T(1,128)}), f32[128,1,128]{2,1,0:T(1,128)S(1)}, u32[]{:S(2)}, u32[]{:S(2)}) %all-to-all-start) | async-done | bytes 65568 | tf_op jit(solution)/shard_map/all_to_all | solution.py:792
  43.2 1.2 %shard_map.100 = (f32[1280,128]{1,0:T(8,128)}, f32[64,128]{1,0:T(8,128)}) custom-call(f32[128,128]{1,0:T(8,128)S(1)} %bitcast.13, f32[4,2,80,128]{3,2,1,0:T(8,128)S(1)} %get-tuple-element.36.basis, f32[128,128]{1,0:T(8,128)S(1)} %get-tuple-element.37.flow, f32[1280,128]{1,0:T(8,128)S(1)} %shard_map.99.star, s32[64,128]{1,0:T(8,128)S(1)} %copy-done.1), custom_call_target="tpu_custom_call" | custom-call | flops 1000000 | bytes 1835008 | tf_op jit(solution)/shard_map/pallas_call | solution.py:717
Async XLA Ops:
  0.6 5.8 %copy-start = (f32[2,10,64,128]{3,2,1,0:T(8,128)S(1)}, f32[2,10,64,128]{3,2,1,0:T(8,128)}, u32[]{:S(2)}) copy-start(f32[2,10,64,128]{3,2,1,0:T(8,128)} %param.7) | copy-start | bytes 1966084
  3.1 3.6 %collective-permute-start = (f32[152,128]{1,0:T(8,128)S(1)}, f32[152,128]{1,0:T(8,128)S(1)}, u32[]{:S(2)}, u32[]{:S(2)}) collective-permute-start(f32[152,128]{1,0:T(8,128)S(1)} %get-tuple-element.27), channel_id=1, source_target_pairs={{0,8},{1,2},{2,1},{3,4},{4,3},{5,6},{6,5},{7,127},{8,0},{9,10},{10... | collective-permute-start | bytes 233480 | tf_op jit(solution)/shard_map/ppermute | solution.py:750
  4.6 3.6 %collective-permute-start.1 = (f32[152,128]{1,0:T(8,128)S(1)}, f32[152,128]{1,0:T(8,128)S(1)}, u32[]{:S(2)}, u32[]{:S(2)}) collective-permute-start(f32[152,128]{1,0:T(8,128)S(1)} %get-tuple-element.28), channel_id=1, source_target_pairs={{0,1},{1,0},{2,3},{3,2},{4,5},{5,4},{6,7},{7,6},{8,9},{9,8},{10,11... | collective-permute-start | bytes 233480 | tf_op jit(solution)/shard_map/ppermute | solution.py:750
  6.4 1.8 %copy-start.2 = (f32[64,128]{1,0:T(8,128)S(1)}, f32[64,128]{1,0:T(8,128)}, u32[]{:S(2)}) copy-start(f32[64,128]{1,0:T(8,128)} %diff.3) | copy-start | bytes 98308
  8.4 6.9 %collective-permute-start.2 = (f32[224,128]{1,0:T(8,128)S(1)}, f32[224,128]{1,0:T(8,128)S(1)}, u32[]{:S(2)}, u32[]{:S(2)}) collective-permute-start(f32[224,128]{1,0:T(8,128)S(1)} %get-tuple-element.30), channel_id=1, source_target_pairs={{0,120},{1,121},{2,122},{3,123},{4,124},{5,125},{6,126},{7,127},{8... | collective-permute-start | bytes 344072 | tf_op jit(solution)/shard_map/ppermute | solution.py:750
  11.9 4.4 %collective-permute-start.3 = (f32[224,128]{1,0:T(8,128)S(1)}, f32[224,128]{1,0:T(8,128)S(1)}, u32[]{:S(2)}, u32[]{:S(2)}) collective-permute-start(f32[224,128]{1,0:T(8,128)S(1)} %get-tuple-element.31), channel_id=1, source_target_pairs={{0,8},{1,9},{2,10},{3,11},{4,12},{5,13},{6,14},{7,15},{8,0},{9,1},... | collective-permute-start | bytes 344072 | tf_op jit(solution)/shard_map/ppermute | solution.py:750
  19.5 23.7 %all-to-all-start = ((f32[128,1,128]{2,1,0:T(1,128)}), f32[128,1,128]{2,1,0:T(1,128)S(1)}, u32[]{:S(2)}, u32[]{:S(2)}) async-start(f32[128,1,128]{2,1,0:T(1,128)} %bitcast.6), calls=%async_computation | async-start | bytes 131072 | tf_op jit(solution)/shard_map/all_to_all | solution.py:792
  33.7 0.8 %copy-start.1 = (s32[64,128]{1,0:T(8,128)S(1)}, s32[64,128]{1,0:T(8,128)}, u32[]{:S(2)}) copy-start(s32[64,128]{1,0:T(8,128)} %lev.3) | copy-start | bytes 98308

commit v9 on v8

--- a/solution.py
+++ b/solution.py
@@ -28,7 +28,7 @@
 SENT = 20
 FULL = 22
 EDGE = 21
-NEAR, NEXT, LAST, COLS = 3 * SENT, 3 * SENT + FULL, 3 * SENT + 2 * FULL, 128
+NEAR, NEXT, COLS = 3 * SENT, 3 * SENT + FULL, 3 * SENT + 2 * FULL
 LAT_SEND = COLS + MARGIN
 LON_SEND = 2 * TALL
 WIDE = 21
@@ -78,7 +78,7 @@
 
 def block_kernel(
     vel_far, tra_far, lev_far, visc_far, diff_far, depth_far, wind_far,
-    star, mean, fields, cols, north, south, send_a, send_b,
+    star, mean, fields, cols, north, south, send_a, send_b, edge_a, edge_b,
     faces, face_levels, sums, turning, vel, tra_north, tra_south, visc, diff, depth, wind, levels_kept, laps, lev, done,
 ):
     pairs = (
@@ -178,11 +178,11 @@
 
     for f in range(3):
         put(f * SENT, fields[pl.ds((f + 1) * ROWS - SENT, SENT), :], fields[pl.ds(f * ROWS, SENT), :])
-    for start, first, count in ((NEAR, 0, FULL), (NEXT, STRIP, FULL), (LAST, 2 * STRIP, EDGE)):
+    edge_a[...] = jnp.where(lat_odd, south[2 * STRIP : RIMS, :], north[2 * STRIP : RIMS, :])
+    edge_b[...] = jnp.where(lat_odd, north[2 * STRIP : RIMS, :], south[2 * STRIP : RIMS, :])
+    for start, first, count in ((NEAR, 0, FULL), (NEXT, STRIP, FULL)):
         put(start, north[pl.ds(first, count), :], south[pl.ds(first, count), :])
     put(COLS, cols[ROWS - MARGIN : ROWS, :], cols[0:MARGIN, :])
-    for send in (send_a, send_b):
-        send[LAST + EDGE : COLS, :] = jnp.zeros((COLS - LAST - EDGE, LANES), F32)
 
     @pl.when(at_fold())
     def _():
@@ -193,7 +193,8 @@
         r = row_ids(RIMS)
         is_velocity = (r < PLANES) | ((r >= STRIP) & (r < STRIP + PLANES))
         turned = jnp.where(is_velocity, -turned, turned)
-        for start, first, count in ((NEAR, 0, FULL), (NEXT, STRIP, FULL), (LAST, 2 * STRIP, EDGE)):
+        edge_b[...] = turned[2 * STRIP : RIMS]
+        for start, first, count in ((NEAR, 0, FULL), (NEXT, STRIP, FULL)):
             send_b[pl.ds(start, count), :] = turned[first : first + count]
         turned = flip_rows(flip_lanes(cols[ROWS - MARGIN : ROWS, :], 3))
         send_b[pl.ds(COLS, MARGIN), :] = jnp.where(lane_ids(MARGIN) < 4 * PLANES, -turned, turned)
@@ -209,7 +210,7 @@
     out[...] = lax.fori_loop(0, PLANES, tracer_step, jnp.zeros((ROWS, LANES), F32), unroll=True)
 
 
-def widen_kernel(fields, cols, tracer_cols, diff, north, south, recv_b, recv_a, tall, strips, tracer_rows, send_a, send_b, east, west):
+def widen_kernel(fields, cols, tracer_cols, diff, north, south, recv_b, recv_a, tall, strips, level_rows, send_a, send_b, east, west):
     lat_odd = odd("lat")
     lon_odd = odd("lon")
     at_south = lax.axis_index("lat") == 0
@@ -241,7 +242,7 @@
     for out, acc, shift in ((east, acc_east, 64), (west, acc_west, 63)):
         out[...] = acc
         out[pl.ds(MARGIN, ROWS), :] = jnp.where(lane_ids(ROWS) == 63, turn(diff[...], shift), acc[MARGIN : MARGIN + ROWS])
-    near, next_to, last = received(NEAR, FULL), received(NEXT, FULL), received(LAST, EDGE)
+    near, next_to = received(NEAR, FULL), received(NEXT, FULL)
     unused = jnp.zeros((STRIP - FULL, LANES), F32)
     group = lane_ids(STRIP) >> 5
     for s, own in enumerate((north, south)):
@@ -257,8 +258,7 @@
             here = pl.ds(block * STRIP, STRIP)
             east[here, :] = jnp.where(group == 2 + g, turn(x, (96 + 32 * g) % LANES), east[here, :])
             west[here, :] = jnp.where(group == 2 + g, turn(x, 64 + 32 * g), west[here, :])
-        tracer_rows[pl.ds(2 * s * STRIP, EDGE), :] = last[s]
-        tracer_rows[pl.ds((2 * s + 1) * STRIP, STRIP), :] = pieces[1]
+        level_rows[pl.ds(8 * s, 8), :] = jnp.broadcast_to(near[s][20:21], (8, LANES))
     k = tall[pl.ds(3 * TALL, TALL), :]
     send_a[pl.ds(0, TALL), :] = k
     send_b[pl.ds(0, TALL), :] = k
@@ -268,8 +268,13 @@
     send_b[rest, :] = jnp.where(lon_odd, e, w)
 
 
-def tracer_kernel(tra, lev, diff, tracer_rows, recv_b, recv_a, out, swap, faces, face_levels):
+def tracer_kernel(tra, lev, diff, level_rows, edge_b, edge_a, recv_b, recv_a, out, swap, faces, face_levels, rim_rows):
     is_odd = odd("lon")
+    lat_odd = odd("lat")
+    from_a = edge_a[...]
+    from_b = jnp.where(lax.axis_index("lat") == 0, 0.0, edge_b[...])
+    rim_rows[0:STRIP, :] = jnp.where(lat_odd, from_b, from_a)
+    rim_rows[STRIP : 2 * STRIP, :] = jnp.where(lat_odd, from_a, from_b)
     lanes = lane_ids(ROWS)
     ids = row_ids(ROWS)
 
@@ -283,20 +288,20 @@
     east_rest, west_rest = received(TALL)
     swap[...] = jnp.where((lanes & 1) == 0, turn(east_cols, LANES - 1), turn(west_cols, 1))
 
-    def sides(x, halo, row):
+    def sides(x, halo, row, rows=rim_rows, apart=STRIP):
         east, west, north, south = shifted(x)
         return (
             jnp.where(lanes == LANES - 1, halo, east),
             jnp.where(lanes == 0, halo, west),
-            jnp.where(ids == ROWS - 1, tracer_rows[pl.ds(row, 1), :], north),
-            jnp.where(ids == 0, tracer_rows[pl.ds(row + 2 * STRIP, 1), :], south),
+            jnp.where(ids == ROWS - 1, rows[pl.ds(row, 1), :], north),
+            jnp.where(ids == 0, rows[pl.ds(row + apart, 1), :], south),
         )
 
     level = lev[...].astype(F32)
     level_halo = jnp.where(lanes == LANES - 1, turn(east_cols, 45), turn(west_cols, 47))
     d = diff[...]
     d_halo = jnp.where(lanes == LANES - 1, turn(east_rest, 64), turn(west_rest, 65))
-    for n, other in enumerate(sides(level, level_halo, STRIP + 20)):
+    for n, other in enumerate(sides(level, level_halo, 0, level_rows, 8)):
         face_levels[n] = jnp.minimum(level, other)
     for n, other in enumerate(sides(d, d_halo, 20)):
         faces[n] = 0.5 * (d + other)
@@ -754,9 +759,10 @@
     vel = velocity.reshape(PLANES * ROWS, LANES)
     wind = wind_forcing.reshape(2 * ROWS, LANES)
     rim = (RIMS, LANES)
-    star, mean, fields, cols, north, south, send_a, send_b = call(
+    star, mean, fields, cols, north, south, send_a, send_b, edge_a, edge_b = call(
         block_kernel,
-        [(PLANES * ROWS, LANES), (2 * ROWS, LANES), (3 * ROWS, LANES), block, rim, rim, (LAT_SEND, LANES), (LAT_SEND, LANES)],
+        [(PLANES * ROWS, LANES), (2 * ROWS, LANES), (3 * ROWS, LANES), block, rim, rim, (LAT_SEND, LANES), (LAT_SEND, LANES),
+         (STRIP, LANES), (STRIP, LANES)],
         [(4,) + block, (4,) + block, (2,) + block, block, (PLANES * ROWS + 16, LANES), (PLANES, 8, LANES), (PLANES, 8, LANES), block, block, block, wind.shape,
          block, (PLANES * ROWS + 16, LANES),
          pltpu.VMEM(block, jnp.int32), pltpu.SemaphoreType.DMA((8,))],
@@ -766,10 +772,12 @@
     )
     got_a = swap(send_a, lat_a)
     got_b = swap(send_b, lat_b)
+    edge_a = swap(edge_a, lat_a)
+    edge_b = swap(edge_b, lat_b)
     (tracer_cols,) = call(tracer_rim_kernel, [block], [], 10**5, tra)
-    tall, strips, tracer_rows, send_a, send_b = call(
+    tall, strips, level_rows, send_a, send_b = call(
         widen_kernel,
-        [(4 * TALL, LANES), (8 * STRIP, LANES), (4 * STRIP, LANES), (LON_SEND, LANES), (LON_SEND, LANES)],
+        [(4 * TALL, LANES), (8 * STRIP, LANES), (16, LANES), (LON_SEND, LANES), (LON_SEND, LANES)],
         [(TALL, LANES)] * 2,
         10**6,
         fields, cols, tracer_cols, diffusivity, north, south, got_b, got_a,
@@ -777,8 +785,8 @@
     got_a = swap(send_a, lon_a)
     got_b = swap(send_b, lon_b)
     (tracers_out,) = call(
-        tracer_kernel, [(PLANES * ROWS, LANES)], [block, (4,) + block, (4,) + block], 10**6,
-        tra, active_levels, diffusivity, tracer_rows, got_b, got_a,
+        tracer_kernel, [(PLANES * ROWS, LANES)], [block, (4,) + block, (4,) + block, (2 * STRIP, LANES)], 10**6,
+        tra, active_levels, diffusivity, level_rows, edge_b, edge_a, got_b, got_a,
     )
     padded = (2, TALL + 16, LANES)
     short = (2, ROWS + 16, LANES)

time: 44.7 us -> 44.3 us (level)
  starting transfers between devices: 24.4 us -> 26.9 us
  waiting for transfers between devices: 9.38 us -> 7.03 us
    all_to_all x1, waiting for transfers between devices: 6.88 us -> 3.61 us  [per_device(): gathered = lax.all_to_all(partial, BOTH, 0, 0, tiled=True)]
    ppermute x4 -> x6, starting transfers between devices: 10.2 us -> 12.8 us  [swap(): return lax.ppermute(x, BOTH, pairs)]
    ppermute x4 -> x6, waiting for transfers between devices: 2.5 us -> 3.43 us  [swap(): return lax.ppermute(x, BOTH, pairs)]
  transfers between devices with their start and end apart: 5 -> 7, of which waited for: 3 -> 4; matrix products, arithmetic and copies ran while one was open for 0% -> 0% of each run, Pallas kernels for 5% -> 5%
where the time goes in v9:
time: 44.3 us; the launch traced here: 44.2 us
  starting transfers between devices  26.9 us (61%)
  Pallas kernels  9.55 us (22%)
  waiting for transfers between devices  7.03 us (16%)
  between operations  0.7 us (2%)
    all_to_all x1, starting transfers between devices, per_device(): gathered = lax.all_to_all(partial, BOTH, 0, 0, tiled=True)  14 us
    ppermute x6, starting transfers between devices, swap(): return lax.ppermute(x, BOTH, pairs)  12.8 us
    pallas_call x7, Pallas kernels, call(): pl.pallas_call(kernel, out_shape=out, in_specs=[pl.BlockSpec(memory_space...  9.55 us
    all_to_all x1, waiting for transfers between devices, per_device(): gathered = lax.all_to_all(partial, BOTH, 0, 0, tiled=True)  3.61 us
    ppermute x6, waiting for transfers between devices, swap(): return lax.ppermute(x, BOTH, pairs)  3.43 us
  transfers between devices with their start and end apart: 7, of which 4 were waited for; matrix products, arithmetic and copies ran while one was open for 0% of the time, Pallas kernels for 5%

profile of v9, /device:TPU:1, one launch (start us, length us, event | category | flops | bytes accessed | tf_op | source)
XLA Modules:
  0.0 44.2 jit_solution(15223474108335630946)
XLA Ops:
  0.6 0.0 copy-start
  0.6 2.5 %shard_map.94 = (f32[1280,128]{1,0:T(8,128)S(1)}, f32[128,128]{1,0:T(8,128)S(1)}, f32[192,128]{1,0:T(8,128)S(1)}, f32[64,128]{1,0:T(8,128)S(1)}, f32[72,128]{1,0...) custom-call(f32[1280,128]{1,0:T(8,128)} %bitcast.15, ...), custom_call_target="tpu_custom_call" | custom-call | flops 10000000 | bytes 2588672 | tf_op jit(solution)/shard_map/pallas_call | solution.py:722
  3.1 1.5 %collective-permute-start = (f32[128,128]{1,0:T(8,128)S(1)}, f32[128,128]{1,0:T(8,128)S(1)}, u32[]{:S(2)}, u32[]{:S(2)}) collective-permute-start(f32[128,128]{1,0:T(8,128)S(1)} %get-tuple-element.29), channel_id=1, source_target_pairs={{0,8},{1,2},{2,1},{3,4},{4,3},{5,6},{6,5},{7,127},{8,0},{9,10},{10... | collective-permute-start | bytes 196616 | tf_op jit(solution)/shard_map/ppermute | solution.py:755
  4.6 1.8 %collective-permute-start.1 = (f32[128,128]{1,0:T(8,128)S(1)}, f32[128,128]{1,0:T(8,128)S(1)}, u32[]{:S(2)}, u32[]{:S(2)}) collective-permute-start(f32[128,128]{1,0:T(8,128)S(1)} %get-tuple-element.30), channel_id=1, source_target_pairs={{0,1},{1,0},{2,3},{3,2},{4,5},{5,4},{6,7},{7,6},{8,9},{9,8},{10,11... | collective-permute-start | bytes 196616 | tf_op jit(solution)/shard_map/ppermute | solution.py:755
  6.4 0.2 shard_map.95.tracer_cols
  6.7 0.0 collective-permute-done.recv_b
  6.7 1.4 %collective-permute-done.1.recv_a = f32[128,128]{1,0:T(8,128)S(1)} collective-permute-done((f32[128,128]{1,0:T(8,128)S(1)}, f32[128,128]{1,0:T(8,128)S(1)}, u32[]{:S(2)}, u32[]{:S(2)}) %collective-permute-start.1) | collective-permute-done | bytes 65568 | tf_op jit(solution)/shard_map/ppermute | solution.py:755
  8.1 0.0 copy-done.1
  8.1 0.2 shard_map.96
  8.3 3.4 %collective-permute-start.4 = (f32[224,128]{1,0:T(8,128)S(1)}, f32[224,128]{1,0:T(8,128)S(1)}, u32[]{:S(2)}, u32[]{:S(2)}) collective-permute-start(f32[224,128]{1,0:T(8,128)S(1)} %get-tuple-element.34), channel_id=1, source_target_pairs={{0,120},{1,121},{2,122},{3,123},{4,124},{5,125},{6,126},{7,127},{8... | collective-permute-start | bytes 344072 | tf_op jit(solution)/shard_map/ppermute | solution.py:755
  11.7 3.4 %collective-permute-start.5 = (f32[224,128]{1,0:T(8,128)S(1)}, f32[224,128]{1,0:T(8,128)S(1)}, u32[]{:S(2)}, u32[]{:S(2)}) collective-permute-start(f32[224,128]{1,0:T(8,128)S(1)} %get-tuple-element.35), channel_id=1, source_target_pairs={{0,8},{1,9},{2,10},{3,11},{4,12},{5,13},{6,14},{7,15},{8,0},{9,1},... | collective-permute-start | bytes 344072 | tf_op jit(solution)/shard_map/ppermute | solution.py:755
  15.2 0.0 collective-permute-done.4.recv_b
  15.2 1.0 %collective-permute-done.5.recv_a = f32[224,128]{1,0:T(8,128)S(1)} collective-permute-done((f32[224,128]{1,0:T(8,128)S(1)}, f32[224,128]{1,0:T(8,128)S(1)}, u32[]{:S(2)}, u32[]{:S(2)}) %collective-permute-start.5) | collective-permute-done | bytes 114720 | tf_op jit(solution)/shard_map/ppermute | solution.py:755
  16.1 3.2 %shard_map.98 = (f32[4,2,80,128]{3,2,1,0:T(8,128)S(1)}, f32[128,128]{1,0:T(8,128)S(1)}, f32[128,128]{1,0:T(8,128)}, f32[64,128]{1,0:T(8,128)S(1)}, f32[96,128]{1,0:T(8,128)S(1)}) custom-call(f32[448,128]{1,0:T(8,128)S(1)} %get-tuple-element.36.tall, f32[192,128]{1,0:T(8,128)S(1)} %get-tuple-element.37.strips, f32[128,128]{1,0:T(8,128)S(1)} %get-tuple-element.38.mean, ...), custom_call_target="tpu_custom_call" | custom-call | flops 10000000 | bytes 1163264 | tf_op jit(solution)/shard_map/pallas_call | solution.py:722
  19.4 14.0 %all-to-all-start = ((f32[128,1,128]{2,1,0:T(1,128)}), f32[128,1,128]{2,1,0:T(1,128)S(1)}, u32[]{:S(2)}, u32[]{:S(2)}) async-start(f32[128,1,128]{2,1,0:T(1,128)} %bitcast.6), calls=%async_computation | async-start | bytes 131072 | tf_op jit(solution)/shard_map/all_to_all | solution.py:800
  33.4 1.1 %collective-permute-start.2 = (f32[24,128]{1,0:T(8,128)S(1)}, f32[24,128]{1,0:T(8,128)S(1)}, u32[]{:S(2)}, u32[]{:S(2)}) collective-permute-start(f32[24,128]{1,0:T(8,128)S(1)} %get-tuple-element.32), channel_id=1, source_target_pairs={{0,8},{1,2},{2,1},{3,4},{4,3},{5,6},{6,5},{7,127},{8,0},{9,10},{10... | collective-permute-start | bytes 36872 | tf_op jit(solution)/shard_map/ppermute | solution.py:755
  34.6 1.5 %collective-permute-start.3 = (f32[24,128]{1,0:T(8,128)S(1)}, f32[24,128]{1,0:T(8,128)S(1)}, u32[]{:S(2)}, u32[]{:S(2)}) collective-permute-start(f32[24,128]{1,0:T(8,128)S(1)} %get-tuple-element.33), channel_id=1, source_target_pairs={{0,1},{1,0},{2,3},{3,2},{4,5},{5,4},{6,7},{7,6},{8,9},{9,8},{10,11... | collective-permute-start | bytes 36872 | tf_op jit(solution)/shard_map/ppermute | solution.py:755
  36.1 0.3 shard_map.99.star
  36.4 0.0 collective-permute-done.2.edge_b
  36.4 1.1 %collective-permute-done.3.edge_a = f32[24,128]{1,0:T(8,128)S(1)} collective-permute-done((f32[24,128]{1,0:T(8,128)S(1)}, f32[24,128]{1,0:T(8,128)S(1)}, u32[]{:S(2)}, u32[]{:S(2)}) %collective-permute-start.3) | collective-permute-done | bytes 12320 | tf_op jit(solution)/shard_map/ppermute | solution.py:755
  37.5 0.0 copy-done.2
  37.5 1.9 %shard_map.97 = f32[1280,128]{1,0:T(8,128)} custom-call(f32[1280,128]{1,0:T(8,128)S(1)} %bitcast.12, s32[64,128]{1,0:T(8,128)S(1)} %copy-done.2, f32[64,128]{1,0:T(8,128)S(1)} %copy-done.1, f32[16,128]{1,0:T(8,128)S(1)} %get-tuple-element.31.level_rows, f32[24,128]{1,0:T(8,128)S(1)} %collective-permute-done.2.edge_b, ...), custom_call_target="tpu_custom_call" | custom-call | flops 1000000 | bytes 1638400 | tf_op jit(solution)/shard_map/pallas_call | solution.py:722
  39.4 3.6 %all-to-all-done = f32[128,1,128]{2,1,0:T(1,128)S(1)} async-done(((f32[128,1,128]{2,1,0:T(1,128)}), f32[128,1,128]{2,1,0:T(1,128)S(1)}, u32[]{:S(2)}, u32[]{:S(2)}) %all-to-all-start) | async-done | bytes 65568 | tf_op jit(solution)/shard_map/all_to_all | solution.py:800
  43.0 1.2 %shard_map.100 = (f32[1280,128]{1,0:T(8,128)}, f32[64,128]{1,0:T(8,128)}) custom-call(f32[128,128]{1,0:T(8,128)S(1)} %bitcast.13, f32[4,2,80,128]{3,2,1,0:T(8,128)S(1)} %get-tuple-element.40.basis, f32[128,128]{1,0:T(8,128)S(1)} %get-tuple-element.41.flow, f32[1280,128]{1,0:T(8,128)S(1)} %shard_map.99.star, s32[64,128]{1,0:T(8,128)S(1)} %copy-done.2), custom_call_target="tpu_custom_call" | custom-call | flops 1000000 | bytes 1835008 | tf_op jit(solution)/shard_map/pallas_call | solution.py:722
  (3 shorter events, 0.0 us)
Async XLA Ops:
  0.6 5.8 %copy-start = (f32[2,10,64,128]{3,2,1,0:T(8,128)S(1)}, f32[2,10,64,128]{3,2,1,0:T(8,128)}, u32[]{:S(2)}) copy-start(f32[2,10,64,128]{3,2,1,0:T(8,128)} %param.7) | copy-start | bytes 1966084
  3.1 3.6 %collective-permute-start = (f32[128,128]{1,0:T(8,128)S(1)}, f32[128,128]{1,0:T(8,128)S(1)}, u32[]{:S(2)}, u32[]{:S(2)}) collective-permute-start(f32[128,128]{1,0:T(8,128)S(1)} %get-tuple-element.29), channel_id=1, source_target_pairs={{0,8},{1,2},{2,1},{3,4},{4,3},{5,6},{6,5},{7,127},{8,0},{9,10},{10... | collective-permute-start | bytes 196616 | tf_op jit(solution)/shard_map/ppermute | solution.py:755
  4.6 3.5 %collective-permute-start.1 = (f32[128,128]{1,0:T(8,128)S(1)}, f32[128,128]{1,0:T(8,128)S(1)}, u32[]{:S(2)}, u32[]{:S(2)}) collective-permute-start(f32[128,128]{1,0:T(8,128)S(1)} %get-tuple-element.30), channel_id=1, source_target_pairs={{0,1},{1,0},{2,3},{3,2},{4,5},{5,4},{6,7},{7,6},{8,9},{9,8},{10,11... | collective-permute-start | bytes 196616 | tf_op jit(solution)/shard_map/ppermute | solution.py:755
  6.4 1.7 %copy-start.1 = (f32[64,128]{1,0:T(8,128)S(1)}, f32[64,128]{1,0:T(8,128)}, u32[]{:S(2)}) copy-start(f32[64,128]{1,0:T(8,128)} %diff.3) | copy-start | bytes 98308
  8.3 6.9 %collective-permute-start.4 = (f32[224,128]{1,0:T(8,128)S(1)}, f32[224,128]{1,0:T(8,128)S(1)}, u32[]{:S(2)}, u32[]{:S(2)}) collective-permute-start(f32[224,128]{1,0:T(8,128)S(1)} %get-tuple-element.34), channel_id=1, source_target_pairs={{0,120},{1,121},{2,122},{3,123},{4,124},{5,125},{6,126},{7,127},{8... | collective-permute-start | bytes 344072 | tf_op jit(solution)/shard_map/ppermute | solution.py:755
  11.7 4.4 %collective-permute-start.5 = (f32[224,128]{1,0:T(8,128)S(1)}, f32[224,128]{1,0:T(8,128)S(1)}, u32[]{:S(2)}, u32[]{:S(2)}) collective-permute-start(f32[224,128]{1,0:T(8,128)S(1)} %get-tuple-element.35), channel_id=1, source_target_pairs={{0,8},{1,9},{2,10},{3,11},{4,12},{5,13},{6,14},{7,15},{8,0},{9,1},... | collective-permute-start | bytes 344072 | tf_op jit(solution)/shard_map/ppermute | solution.py:755
  19.4 23.6 %all-to-all-start = ((f32[128,1,128]{2,1,0:T(1,128)}), f32[128,1,128]{2,1,0:T(1,128)S(1)}, u32[]{:S(2)}, u32[]{:S(2)}) async-start(f32[128,1,128]{2,1,0:T(1,128)} %bitcast.6), calls=%async_computation | async-start | bytes 131072 | tf_op jit(solution)/shard_map/all_to_all | solution.py:800
  33.4 3.0 %collective-permute-start.2 = (f32[24,128]{1,0:T(8,128)S(1)}, f32[24,128]{1,0:T(8,128)S(1)}, u32[]{:S(2)}, u32[]{:S(2)}) collective-permute-start(f32[24,128]{1,0:T(8,128)S(1)} %get-tuple-element.32), channel_id=1, source_target_pairs={{0,8},{1,2},{2,1},{3,4},{4,3},{5,6},{6,5},{7,127},{8,0},{9,10},{10... | collective-permute-start | bytes 36872 | tf_op jit(solution)/shard_map/ppermute | solution.py:755
  34.6 2.9 %collective-permute-start.3 = (f32[24,128]{1,0:T(8,128)S(1)}, f32[24,128]{1,0:T(8,128)S(1)}, u32[]{:S(2)}, u32[]{:S(2)}) collective-permute-start(f32[24,128]{1,0:T(8,128)S(1)} %get-tuple-element.33), channel_id=1, source_target_pairs={{0,1},{1,0},{2,3},{3,2},{4,5},{5,4},{6,7},{7,6},{8,9},{9,8},{10,11... | collective-permute-start | bytes 36872 | tf_op jit(solution)/shard_map/ppermute | solution.py:755
  36.1 1.4 %copy-start.2 = (s32[64,128]{1,0:T(8,128)S(1)}, s32[64,128]{1,0:T(8,128)}, u32[]{:S(2)}) copy-start(s32[64,128]{1,0:T(8,128)} %lev.3) | copy-start | bytes 98308

commit v10 on v9

--- a/solution.py
+++ b/solution.py
@@ -43,7 +43,7 @@
 
 
 def turn(x, shift):
-    return pltpu.roll(x, shift, 1)
+    return x if isinstance(shift, int) and shift == 0 else pltpu.roll(x, shift, 1)
 
 
 def pick(x, index):
@@ -233,15 +233,16 @@
         tall[pl.ds(f * TALL + MARGIN + ROWS + SENT, MARGIN - SENT), :] = unused
         x = tall[pl.ds(f * TALL, TALL), :]
         here = (lanes >= f * WIDE) & (lanes < (f + 1) * WIDE)
-        acc_east = jnp.where(here, turn(x, (f + 1) * WIDE), acc_east)
+        before = (lanes >= LANES - WIDE) if f == 0 else (lanes >= (f - 1) * WIDE) & (lanes < f * WIDE)
+        acc_east = jnp.where(before, turn(x, f * WIDE), acc_east)
         acc_west = jnp.where(here, turn(x, f * WIDE), acc_west)
     from_north, from_south = received(COLS, MARGIN)
     tall[pl.ds(3 * TALL, MARGIN), :] = from_south
     tall[pl.ds(3 * TALL + MARGIN, ROWS), :] = jnp.where(lane_ids(ROWS) < 88, cols[...], tracer_cols[...])
     tall[pl.ds(3 * TALL + MARGIN + ROWS, MARGIN), :] = from_north
-    for out, acc, shift in ((east, acc_east, 64), (west, acc_west, 63)):
+    for out, acc, lane, shift in ((east, acc_east, 106, 107), (west, acc_west, 63, 63)):
         out[...] = acc
-        out[pl.ds(MARGIN, ROWS), :] = jnp.where(lane_ids(ROWS) == 63, turn(diff[...], shift), acc[MARGIN : MARGIN + ROWS])
+        out[pl.ds(MARGIN, ROWS), :] = jnp.where(lane_ids(ROWS) == lane, turn(diff[...], shift), acc[MARGIN : MARGIN + ROWS])
     near, next_to = received(NEAR, FULL), received(NEXT, FULL)
     unused = jnp.zeros((STRIP - FULL, LANES), F32)
     group = lane_ids(STRIP) >> 5
@@ -256,7 +257,9 @@
             strips[pl.ds((4 * s + r) * STRIP, STRIP), :] = x
             block, g = divmod(4 * s + r, 2)
             here = pl.ds(block * STRIP, STRIP)
-            east[here, :] = jnp.where(group == 2 + g, turn(x, (96 + 32 * g) % LANES), east[here, :])
+            first = 42 + 32 * g
+            mine = (lane_ids(STRIP) >= first) & (lane_ids(STRIP) < first + 32)
+            east[here, :] = jnp.where(mine, turn(x, first + 32), east[here, :])
             west[here, :] = jnp.where(group == 2 + g, turn(x, 64 + 32 * g), west[here, :])
         level_rows[pl.ds(8 * s, 8), :] = jnp.broadcast_to(near[s][20:21], (8, LANES))
     k = tall[pl.ds(3 * TALL, TALL), :]
@@ -300,7 +303,7 @@
     level = lev[...].astype(F32)
     level_halo = jnp.where(lanes == LANES - 1, turn(east_cols, 45), turn(west_cols, 47))
     d = diff[...]
-    d_halo = jnp.where(lanes == LANES - 1, turn(east_rest, 64), turn(west_rest, 65))
+    d_halo = jnp.where(lanes == LANES - 1, turn(east_rest, 64), turn(west_rest, 22))
     for n, other in enumerate(sides(level, level_halo, 0, level_rows, 8)):
         face_levels[n] = jnp.minimum(level, other)
     for n, other in enumerate(sides(d, d_halo, 20)):
@@ -370,15 +373,14 @@
         got_b = recv_b[here, :]
         return jnp.where(is_odd, got_b, got_a), jnp.where(is_odd, got_a, got_b)
 
-    def ghost(east, west, first, count):
-        return jnp.where(
-            lane_ids(east.shape[0]) < 64, turn(east, (LANES - first) % LANES), turn(west, LANES - first - count)
-        )
+    def ghost_strip(east, west, g):
+        return jnp.where(lane_ids(STRIP) < 64, turn(east, 64 - 32 * g), turn(west, 54 - 32 * g))
 
     from_east, from_west = received(TALL, TALL)
     for f in range(3):
         state[f, 0, rows, :] = tall[pl.ds(f * TALL, TALL), :]
-        state[f, 1, rows, :] = ghost(from_east, from_west, f * WIDE, WIDE)
+        here = (lanes >= f * WIDE) & (lanes < (f + 1) * WIDE)
+        state[f, 1, rows, :] = turn(jnp.where(here, from_east, from_west), (LANES - f * WIDE) % LANES)
     last = lanes == LANES - 1
     first = lanes == 0
 
@@ -427,7 +429,7 @@
         for r in range(4):
             centre = strips[pl.ds((4 * s + r) * STRIP, STRIP), :]
             block, g = divmod(4 * s + r, 2)
-            both = (centre, ghost(*received(TALL + block * STRIP, STRIP), 64 + 32 * g, 32))
+            both = (centre, ghost_strip(*received(TALL + block * STRIP, STRIP), g))
             deep.append([b[20:21] for b in both])
             v.append([jnp.broadcast_to(b[21:22], (STRIP, LANES)) for b in both])
             wet.append([jnp.where(is_plane & (level_of_row < b[20:21]), 1.0, 0.0) for b in both])

time: 44.3 us -> 44.2 us (level)
  transfers between devices with their start and end apart: 7 -> 7, of which waited for: 4 -> 4; matrix products, arithmetic and copies ran while one was open for 0% -> 0% of each run, Pallas kernels for 5% -> 6%
where the time goes in v10:
time: 44.2 us; the launch traced here: 44.1 us
  starting transfers between devices  26.9 us (61%)
  Pallas kernels  9.44 us (21%)
  waiting for transfers between devices  7.03 us (16%)
  between operations  0.7 us (2%)
    all_to_all x1, starting transfers between devices, per_device(): gathered = lax.all_to_all(partial, BOTH, 0, 0, tiled=True)  14 us
    ppermute x6, starting transfers between devices, swap(): return lax.ppermute(x, BOTH, pairs)  12.8 us
    pallas_call x7, Pallas kernels, call(): pl.pallas_call(kernel, out_shape=out, in_specs=[pl.BlockSpec(memory_space...  9.44 us
    all_to_all x1, waiting for transfers between devices, per_device(): gathered = lax.all_to_all(partial, BOTH, 0, 0, tiled=True)  3.61 us
    ppermute x6, waiting for transfers between devices, swap(): return lax.ppermute(x, BOTH, pairs)  3.43 us
  transfers between devices with their start and end apart: 7, of which 4 were waited for; matrix products, arithmetic and copies ran while one was open for 0% of the time, Pallas kernels for 6%

profile of v10, /device:TPU:1, one launch (start us, length us, event | category | flops | bytes accessed | tf_op | source)
XLA Modules:
  0.0 44.1 jit_solution(4890549336129115390)
XLA Ops:
  0.6 0.0 copy-start
  0.6 2.5 %shard_map.94 = (f32[1280,128]{1,0:T(8,128)S(1)}, f32[128,128]{1,0:T(8,128)S(1)}, f32[192,128]{1,0:T(8,128)S(1)}, f32[64,128]{1,0:T(8,128)S(1)}, f32[72,128]{1,0...) custom-call(f32[1280,128]{1,0:T(8,128)} %bitcast.15, ...), custom_call_target="tpu_custom_call" | custom-call | flops 10000000 | bytes 2588672 | tf_op jit(solution)/shard_map/pallas_call | solution.py:724
  3.1 1.5 %collective-permute-start = (f32[128,128]{1,0:T(8,128)S(1)}, f32[128,128]{1,0:T(8,128)S(1)}, u32[]{:S(2)}, u32[]{:S(2)}) collective-permute-start(f32[128,128]{1,0:T(8,128)S(1)} %get-tuple-element.29), channel_id=1, source_target_pairs={{0,8},{1,2},{2,1},{3,4},{4,3},{5,6},{6,5},{7,127},{8,0},{9,10},{10... | collective-permute-start | bytes 196616 | tf_op jit(solution)/shard_map/ppermute | solution.py:757
  4.6 1.8 %collective-permute-start.1 = (f32[128,128]{1,0:T(8,128)S(1)}, f32[128,128]{1,0:T(8,128)S(1)}, u32[]{:S(2)}, u32[]{:S(2)}) collective-permute-start(f32[128,128]{1,0:T(8,128)S(1)} %get-tuple-element.30), channel_id=1, source_target_pairs={{0,1},{1,0},{2,3},{3,2},{4,5},{5,4},{6,7},{7,6},{8,9},{9,8},{10,11... | collective-permute-start | bytes 196616 | tf_op jit(solution)/shard_map/ppermute | solution.py:757
  6.4 0.0 copy-done
  6.4 0.2 shard_map.95.tracer_cols
  6.7 0.0 collective-permute-done.recv_b
  6.7 1.4 %collective-permute-done.1.recv_a = f32[128,128]{1,0:T(8,128)S(1)} collective-permute-done((f32[128,128]{1,0:T(8,128)S(1)}, f32[128,128]{1,0:T(8,128)S(1)}, u32[]{:S(2)}, u32[]{:S(2)}) %collective-permute-start.1) | collective-permute-done | bytes 65568 | tf_op jit(solution)/shard_map/ppermute | solution.py:757
  8.1 0.0 copy-done.1
  8.1 0.2 shard_map.96
  8.3 3.4 %collective-permute-start.4 = (f32[224,128]{1,0:T(8,128)S(1)}, f32[224,128]{1,0:T(8,128)S(1)}, u32[]{:S(2)}, u32[]{:S(2)}) collective-permute-start(f32[224,128]{1,0:T(8,128)S(1)} %get-tuple-element.34), channel_id=1, source_target_pairs={{0,120},{1,121},{2,122},{3,123},{4,124},{5,125},{6,126},{7,127},{8... | collective-permute-start | bytes 344072 | tf_op jit(solution)/shard_map/ppermute | solution.py:757
  11.7 3.4 %collective-permute-start.5 = (f32[224,128]{1,0:T(8,128)S(1)}, f32[224,128]{1,0:T(8,128)S(1)}, u32[]{:S(2)}, u32[]{:S(2)}) collective-permute-start(f32[224,128]{1,0:T(8,128)S(1)} %get-tuple-element.35), channel_id=1, source_target_pairs={{0,8},{1,9},{2,10},{3,11},{4,12},{5,13},{6,14},{7,15},{8,0},{9,1},... | collective-permute-start | bytes 344072 | tf_op jit(solution)/shard_map/ppermute | solution.py:757
  15.1 0.0 collective-permute-done.4.recv_b
  15.1 1.0 %collective-permute-done.5.recv_a = f32[224,128]{1,0:T(8,128)S(1)} collective-permute-done((f32[224,128]{1,0:T(8,128)S(1)}, f32[224,128]{1,0:T(8,128)S(1)}, u32[]{:S(2)}, u32[]{:S(2)}) %collective-permute-start.5) | collective-permute-done | bytes 114720 | tf_op jit(solution)/shard_map/ppermute | solution.py:757
  16.1 3.2 %shard_map.98 = (f32[4,2,80,128]{3,2,1,0:T(8,128)S(1)}, f32[128,128]{1,0:T(8,128)S(1)}, f32[128,128]{1,0:T(8,128)}, f32[64,128]{1,0:T(8,128)S(1)}, f32[96,128]{1,0:T(8,128)S(1)}) custom-call(f32[448,128]{1,0:T(8,128)S(1)} %get-tuple-element.36.tall, f32[192,128]{1,0:T(8,128)S(1)} %get-tuple-element.37.strips, f32[128,128]{1,0:T(8,128)S(1)} %get-tuple-element.38.mean, ...), custom_call_target="tpu_custom_call" | custom-call | flops 10000000 | bytes 1163264 | tf_op jit(solution)/shard_map/pallas_call | solution.py:724
  19.3 14.0 %all-to-all-start = ((f32[128,1,128]{2,1,0:T(1,128)}), f32[128,1,128]{2,1,0:T(1,128)S(1)}, u32[]{:S(2)}, u32[]{:S(2)}) async-start(f32[128,1,128]{2,1,0:T(1,128)} %bitcast.6), calls=%async_computation | async-start | bytes 131072 | tf_op jit(solution)/shard_map/all_to_all | solution.py:802
  33.3 1.1 %collective-permute-start.2 = (f32[24,128]{1,0:T(8,128)S(1)}, f32[24,128]{1,0:T(8,128)S(1)}, u32[]{:S(2)}, u32[]{:S(2)}) collective-permute-start(f32[24,128]{1,0:T(8,128)S(1)} %get-tuple-element.32), channel_id=1, source_target_pairs={{0,8},{1,2},{2,1},{3,4},{4,3},{5,6},{6,5},{7,127},{8,0},{9,10},{10... | collective-permute-start | bytes 36872 | tf_op jit(solution)/shard_map/ppermute | solution.py:757
  34.5 1.5 %collective-permute-start.3 = (f32[24,128]{1,0:T(8,128)S(1)}, f32[24,128]{1,0:T(8,128)S(1)}, u32[]{:S(2)}, u32[]{:S(2)}) collective-permute-start(f32[24,128]{1,0:T(8,128)S(1)} %get-tuple-element.33), channel_id=1, source_target_pairs={{0,1},{1,0},{2,3},{3,2},{4,5},{5,4},{6,7},{7,6},{8,9},{9,8},{10,11... | collective-permute-start | bytes 36872 | tf_op jit(solution)/shard_map/ppermute | solution.py:757
  36.0 0.3 shard_map.99.star
  36.3 0.0 collective-permute-done.2.edge_b
  36.3 1.1 %collective-permute-done.3.edge_a = f32[24,128]{1,0:T(8,128)S(1)} collective-permute-done((f32[24,128]{1,0:T(8,128)S(1)}, f32[24,128]{1,0:T(8,128)S(1)}, u32[]{:S(2)}, u32[]{:S(2)}) %collective-permute-start.3) | collective-permute-done | bytes 12320 | tf_op jit(solution)/shard_map/ppermute | solution.py:757
  37.3 1.9 %shard_map.97 = f32[1280,128]{1,0:T(8,128)} custom-call(f32[1280,128]{1,0:T(8,128)S(1)} %bitcast.12, s32[64,128]{1,0:T(8,128)S(1)} %copy-done.2, f32[64,128]{1,0:T(8,128)S(1)} %copy-done.1, f32[16,128]{1,0:T(8,128)S(1)} %get-tuple-element.31.level_rows, f32[24,128]{1,0:T(8,128)S(1)} %collective-permute-done.2.edge_b, ...), custom_call_target="tpu_custom_call" | custom-call | flops 1000000 | bytes 1638400 | tf_op jit(solution)/shard_map/pallas_call | solution.py:724
  39.2 3.6 %all-to-all-done = f32[128,1,128]{2,1,0:T(1,128)S(1)} async-done(((f32[128,1,128]{2,1,0:T(1,128)}), f32[128,1,128]{2,1,0:T(1,128)S(1)}, u32[]{:S(2)}, u32[]{:S(2)}) %all-to-all-start) | async-done | bytes 65568 | tf_op jit(solution)/shard_map/all_to_all | solution.py:802
  42.8 1.2 %shard_map.100 = (f32[1280,128]{1,0:T(8,128)}, f32[64,128]{1,0:T(8,128)}) custom-call(f32[128,128]{1,0:T(8,128)S(1)} %bitcast.13, f32[4,2,80,128]{3,2,1,0:T(8,128)S(1)} %get-tuple-element.40.basis, f32[128,128]{1,0:T(8,128)S(1)} %get-tuple-element.41.flow, f32[1280,128]{1,0:T(8,128)S(1)} %shard_map.99.star, s32[64,128]{1,0:T(8,128)S(1)} %copy-done.2), custom_call_target="tpu_custom_call" | custom-call | flops 1000000 | bytes 1835008 | tf_op jit(solution)/shard_map/pallas_call | solution.py:724
  (3 shorter events, 0.0 us)
Async XLA Ops:
  0.6 5.8 %copy-start = (f32[2,10,64,128]{3,2,1,0:T(8,128)S(1)}, f32[2,10,64,128]{3,2,1,0:T(8,128)}, u32[]{:S(2)}) copy-start(f32[2,10,64,128]{3,2,1,0:T(8,128)} %param.7) | copy-start | bytes 1966084
  3.1 3.6 %collective-permute-start = (f32[128,128]{1,0:T(8,128)S(1)}, f32[128,128]{1,0:T(8,128)S(1)}, u32[]{:S(2)}, u32[]{:S(2)}) collective-permute-start(f32[128,128]{1,0:T(8,128)S(1)} %get-tuple-element.29), channel_id=1, source_target_pairs={{0,8},{1,2},{2,1},{3,4},{4,3},{5,6},{6,5},{7,127},{8,0},{9,10},{10... | collective-permute-start | bytes 196616 | tf_op jit(solution)/shard_map/ppermute | solution.py:757
  4.6 3.5 %collective-permute-start.1 = (f32[128,128]{1,0:T(8,128)S(1)}, f32[128,128]{1,0:T(8,128)S(1)}, u32[]{:S(2)}, u32[]{:S(2)}) collective-permute-start(f32[128,128]{1,0:T(8,128)S(1)} %get-tuple-element.30), channel_id=1, source_target_pairs={{0,1},{1,0},{2,3},{3,2},{4,5},{5,4},{6,7},{7,6},{8,9},{9,8},{10,11... | collective-permute-start | bytes 196616 | tf_op jit(solution)/shard_map/ppermute | solution.py:757
  6.4 1.7 %copy-start.1 = (f32[64,128]{1,0:T(8,128)S(1)}, f32[64,128]{1,0:T(8,128)}, u32[]{:S(2)}) copy-start(f32[64,128]{1,0:T(8,128)} %diff.3) | copy-start | bytes 98308
  8.3 6.9 %collective-permute-start.4 = (f32[224,128]{1,0:T(8,128)S(1)}, f32[224,128]{1,0:T(8,128)S(1)}, u32[]{:S(2)}, u32[]{:S(2)}) collective-permute-start(f32[224,128]{1,0:T(8,128)S(1)} %get-tuple-element.34), channel_id=1, source_target_pairs={{0,120},{1,121},{2,122},{3,123},{4,124},{5,125},{6,126},{7,127},{8... | collective-permute-start | bytes 344072 | tf_op jit(solution)/shard_map/ppermute | solution.py:757
  11.7 4.4 %collective-permute-start.5 = (f32[224,128]{1,0:T(8,128)S(1)}, f32[224,128]{1,0:T(8,128)S(1)}, u32[]{:S(2)}, u32[]{:S(2)}) collective-permute-start(f32[224,128]{1,0:T(8,128)S(1)} %get-tuple-element.35), channel_id=1, source_target_pairs={{0,8},{1,9},{2,10},{3,11},{4,12},{5,13},{6,14},{7,15},{8,0},{9,1},... | collective-permute-start | bytes 344072 | tf_op jit(solution)/shard_map/ppermute | solution.py:757
  19.3 23.6 %all-to-all-start = ((f32[128,1,128]{2,1,0:T(1,128)}), f32[128,1,128]{2,1,0:T(1,128)S(1)}, u32[]{:S(2)}, u32[]{:S(2)}) async-start(f32[128,1,128]{2,1,0:T(1,128)} %bitcast.6), calls=%async_computation | async-start | bytes 131072 | tf_op jit(solution)/shard_map/all_to_all | solution.py:802
  33.3 3.0 %collective-permute-start.2 = (f32[24,128]{1,0:T(8,128)S(1)}, f32[24,128]{1,0:T(8,128)S(1)}, u32[]{:S(2)}, u32[]{:S(2)}) collective-permute-start(f32[24,128]{1,0:T(8,128)S(1)} %get-tuple-element.32), channel_id=1, source_target_pairs={{0,8},{1,2},{2,1},{3,4},{4,3},{5,6},{6,5},{7,127},{8,0},{9,10},{10... | collective-permute-start | bytes 36872 | tf_op jit(solution)/shard_map/ppermute | solution.py:757
  34.5 2.9 %collective-permute-start.3 = (f32[24,128]{1,0:T(8,128)S(1)}, f32[24,128]{1,0:T(8,128)S(1)}, u32[]{:S(2)}, u32[]{:S(2)}) collective-permute-start(f32[24,128]{1,0:T(8,128)S(1)} %get-tuple-element.33), channel_id=1, source_target_pairs={{0,1},{1,0},{2,3},{3,2},{4,5},{5,4},{6,7},{7,6},{8,9},{9,8},{10,11... | collective-permute-start | bytes 36872 | tf_op jit(solution)/shard_map/ppermute | solution.py:757
  36.0 1.4 %copy-start.2 = (s32[64,128]{1,0:T(8,128)S(1)}, s32[64,128]{1,0:T(8,128)}, u32[]{:S(2)}) copy-start(s32[64,128]{1,0:T(8,128)} %lev.3) | copy-start | bytes 98308

commit v11 on v10

--- a/solution.py
+++ b/solution.py
@@ -342,9 +342,10 @@
     open_n = wet * pltpu.roll(wet, rows - 1, 0)
     flux_e = open_e * (turn(x, LANES - 1) - x)
     flux_n = open_n * (pltpu.roll(x, rows - 1, 0) - x)
-    lap = (flux_e - turn(flux_e, 1)) + (flux_n - pltpu.roll(flux_n, 1, 0))
+    flux_w = turn(flux_e, 1)
+    lap = (flux_e - flux_w) + (flux_n - pltpu.roll(flux_n, 1, 0))
     seam = jnp.where(phase == 1, flux_e, 0.0)
-    seam_west = turn(seam, 1)
+    seam_west = jnp.where(phase == 2, flux_w, 0.0)
     added = seam - seam_west
     step = jnp.where(phase == 1, turn(lap, LANES - 1) - lap, turn(seam, LANES - 1) + seam_west)
     flux_e = (v + turn(v, LANES - 1)) * open_e * step

time: 44.2 us -> 44.2 us (level)
  no operation moved by 1% of the time
where the time goes in v11:
time: 44.2 us; the launch traced here: 44 us
  starting transfers between devices  26.9 us (61%)
  Pallas kernels  9.38 us (21%)
  waiting for transfers between devices  7.03 us (16%)
  between operations  0.7 us (2%)
    all_to_all x1, starting transfers between devices, per_device(): gathered = lax.all_to_all(partial, BOTH, 0, 0, tiled=True)  14 us
    ppermute x6, starting transfers between devices, swap(): return lax.ppermute(x, BOTH, pairs)  12.8 us
    pallas_call x7, Pallas kernels, call(): pl.pallas_call(kernel, out_shape=out, in_specs=[pl.BlockSpec(memory_space...  9.38 us
    all_to_all x1, waiting for transfers between devices, per_device(): gathered = lax.all_to_all(partial, BOTH, 0, 0, tiled=True)  3.61 us
    ppermute x6, waiting for transfers between devices, swap(): return lax.ppermute(x, BOTH, pairs)  3.43 us
  transfers between devices with their start and end apart: 7, of which 4 were waited for; matrix products, arithmetic and copies ran while one was open for 0% of the time, Pallas kernels for 6%

profile of v11, /device:TPU:1, one launch (start us, length us, event | category | flops | bytes accessed | tf_op | source)
XLA Modules:
  0.0 44.0 jit_solution(14837528147997548384)
XLA Ops:
  0.6 0.0 copy-start
  0.6 2.5 %shard_map.94 = (f32[1280,128]{1,0:T(8,128)S(1)}, f32[128,128]{1,0:T(8,128)S(1)}, f32[192,128]{1,0:T(8,128)S(1)}, f32[64,128]{1,0:T(8,128)S(1)}, f32[72,128]{1,0...) custom-call(f32[1280,128]{1,0:T(8,128)} %bitcast.15, ...), custom_call_target="tpu_custom_call" | custom-call | flops 10000000 | bytes 2588672 | tf_op jit(solution)/shard_map/pallas_call | solution.py:725
  3.1 1.5 %collective-permute-start = (f32[128,128]{1,0:T(8,128)S(1)}, f32[128,128]{1,0:T(8,128)S(1)}, u32[]{:S(2)}, u32[]{:S(2)}) collective-permute-start(f32[128,128]{1,0:T(8,128)S(1)} %get-tuple-element.29), channel_id=1, source_target_pairs={{0,8},{1,2},{2,1},{3,4},{4,3},{5,6},{6,5},{7,127},{8,0},{9,10},{10... | collective-permute-start | bytes 196616 | tf_op jit(solution)/shard_map/ppermute | solution.py:758
  4.6 1.8 %collective-permute-start.1 = (f32[128,128]{1,0:T(8,128)S(1)}, f32[128,128]{1,0:T(8,128)S(1)}, u32[]{:S(2)}, u32[]{:S(2)}) collective-permute-start(f32[128,128]{1,0:T(8,128)S(1)} %get-tuple-element.30), channel_id=1, source_target_pairs={{0,1},{1,0},{2,3},{3,2},{4,5},{5,4},{6,7},{7,6},{8,9},{9,8},{10,11... | collective-permute-start | bytes 196616 | tf_op jit(solution)/shard_map/ppermute | solution.py:758
  6.4 0.0 copy-done
  6.4 0.2 shard_map.95.tracer_cols
  6.7 0.0 collective-permute-done.recv_b
  6.7 1.4 %collective-permute-done.1.recv_a = f32[128,128]{1,0:T(8,128)S(1)} collective-permute-done((f32[128,128]{1,0:T(8,128)S(1)}, f32[128,128]{1,0:T(8,128)S(1)}, u32[]{:S(2)}, u32[]{:S(2)}) %collective-permute-start.1) | collective-permute-done | bytes 65568 | tf_op jit(solution)/shard_map/ppermute | solution.py:758
  8.1 0.0 copy-done.1
  8.1 0.2 shard_map.96
  8.3 3.4 %collective-permute-start.4 = (f32[224,128]{1,0:T(8,128)S(1)}, f32[224,128]{1,0:T(8,128)S(1)}, u32[]{:S(2)}, u32[]{:S(2)}) collective-permute-start(f32[224,128]{1,0:T(8,128)S(1)} %get-tuple-element.34), channel_id=1, source_target_pairs={{0,120},{1,121},{2,122},{3,123},{4,124},{5,125},{6,126},{7,127},{8... | collective-permute-start | bytes 344072 | tf_op jit(solution)/shard_map/ppermute | solution.py:758
  11.7 3.4 %collective-permute-start.5 = (f32[224,128]{1,0:T(8,128)S(1)}, f32[224,128]{1,0:T(8,128)S(1)}, u32[]{:S(2)}, u32[]{:S(2)}) collective-permute-start(f32[224,128]{1,0:T(8,128)S(1)} %get-tuple-element.35), channel_id=1, source_target_pairs={{0,8},{1,9},{2,10},{3,11},{4,12},{5,13},{6,14},{7,15},{8,0},{9,1},... | collective-permute-start | bytes 344072 | tf_op jit(solution)/shard_map/ppermute | solution.py:758
  15.1 0.0 collective-permute-done.4.recv_b
  15.1 1.0 %collective-permute-done.5.recv_a = f32[224,128]{1,0:T(8,128)S(1)} collective-permute-done((f32[224,128]{1,0:T(8,128)S(1)}, f32[224,128]{1,0:T(8,128)S(1)}, u32[]{:S(2)}, u32[]{:S(2)}) %collective-permute-start.5) | collective-permute-done | bytes 114720 | tf_op jit(solution)/shard_map/ppermute | solution.py:758
  16.1 3.1 %shard_map.98 = (f32[4,2,80,128]{3,2,1,0:T(8,128)S(1)}, f32[128,128]{1,0:T(8,128)S(1)}, f32[128,128]{1,0:T(8,128)}, f32[64,128]{1,0:T(8,128)S(1)}, f32[96,128]{1,0:T(8,128)S(1)}) custom-call(f32[448,128]{1,0:T(8,128)S(1)} %get-tuple-element.36.tall, f32[192,128]{1,0:T(8,128)S(1)} %get-tuple-element.37.strips, f32[128,128]{1,0:T(8,128)S(1)} %get-tuple-element.38.mean, ...), custom_call_target="tpu_custom_call" | custom-call | flops 10000000 | bytes 1163264 | tf_op jit(solution)/shard_map/pallas_call | solution.py:725
  19.2 14.0 %all-to-all-start = ((f32[128,1,128]{2,1,0:T(1,128)}), f32[128,1,128]{2,1,0:T(1,128)S(1)}, u32[]{:S(2)}, u32[]{:S(2)}) async-start(f32[128,1,128]{2,1,0:T(1,128)} %bitcast.6), calls=%async_computation | async-start | bytes 131072 | tf_op jit(solution)/shard_map/all_to_all | solution.py:803
  33.3 1.1 %collective-permute-start.2 = (f32[24,128]{1,0:T(8,128)S(1)}, f32[24,128]{1,0:T(8,128)S(1)}, u32[]{:S(2)}, u32[]{:S(2)}) collective-permute-start(f32[24,128]{1,0:T(8,128)S(1)} %get-tuple-element.32), channel_id=1, source_target_pairs={{0,8},{1,2},{2,1},{3,4},{4,3},{5,6},{6,5},{7,127},{8,0},{9,10},{10... | collective-permute-start | bytes 36872 | tf_op jit(solution)/shard_map/ppermute | solution.py:758
  34.4 1.5 %collective-permute-start.3 = (f32[24,128]{1,0:T(8,128)S(1)}, f32[24,128]{1,0:T(8,128)S(1)}, u32[]{:S(2)}, u32[]{:S(2)}) collective-permute-start(f32[24,128]{1,0:T(8,128)S(1)} %get-tuple-element.33), channel_id=1, source_target_pairs={{0,1},{1,0},{2,3},{3,2},{4,5},{5,4},{6,7},{7,6},{8,9},{9,8},{10,11... | collective-permute-start | bytes 36872 | tf_op jit(solution)/shard_map/ppermute | solution.py:758
  35.9 0.3 shard_map.99.star
  36.2 0.0 collective-permute-done.2.edge_b
  36.2 1.1 %collective-permute-done.3.edge_a = f32[24,128]{1,0:T(8,128)S(1)} collective-permute-done((f32[24,128]{1,0:T(8,128)S(1)}, f32[24,128]{1,0:T(8,128)S(1)}, u32[]{:S(2)}, u32[]{:S(2)}) %collective-permute-start.3) | collective-permute-done | bytes 12320 | tf_op jit(solution)/shard_map/ppermute | solution.py:758
  37.3 1.9 %shard_map.97 = f32[1280,128]{1,0:T(8,128)} custom-call(f32[1280,128]{1,0:T(8,128)S(1)} %bitcast.12, s32[64,128]{1,0:T(8,128)S(1)} %copy-done.2, f32[64,128]{1,0:T(8,128)S(1)} %copy-done.1, f32[16,128]{1,0:T(8,128)S(1)} %get-tuple-element.31.level_rows, f32[24,128]{1,0:T(8,128)S(1)} %collective-permute-done.2.edge_b, ...), custom_call_target="tpu_custom_call" | custom-call | flops 1000000 | bytes 1638400 | tf_op jit(solution)/shard_map/pallas_call | solution.py:725
  39.2 3.6 %all-to-all-done = f32[128,1,128]{2,1,0:T(1,128)S(1)} async-done(((f32[128,1,128]{2,1,0:T(1,128)}), f32[128,1,128]{2,1,0:T(1,128)S(1)}, u32[]{:S(2)}, u32[]{:S(2)}) %all-to-all-start) | async-done | bytes 65568 | tf_op jit(solution)/shard_map/all_to_all | solution.py:803
  42.8 1.2 %shard_map.100 = (f32[1280,128]{1,0:T(8,128)}, f32[64,128]{1,0:T(8,128)}) custom-call(f32[128,128]{1,0:T(8,128)S(1)} %bitcast.13, f32[4,2,80,128]{3,2,1,0:T(8,128)S(1)} %get-tuple-element.40.basis, f32[128,128]{1,0:T(8,128)S(1)} %get-tuple-element.41.flow, f32[1280,128]{1,0:T(8,128)S(1)} %shard_map.99.star, s32[64,128]{1,0:T(8,128)S(1)} %copy-done.2), custom_call_target="tpu_custom_call" | custom-call | flops 1000000 | bytes 1835008 | tf_op jit(solution)/shard_map/pallas_call | solution.py:725
  (3 shorter events, 0.0 us)
Async XLA Ops:
  0.6 5.8 %copy-start = (f32[2,10,64,128]{3,2,1,0:T(8,128)S(1)}, f32[2,10,64,128]{3,2,1,0:T(8,128)}, u32[]{:S(2)}) copy-start(f32[2,10,64,128]{3,2,1,0:T(8,128)} %param.7) | copy-start | bytes 1966084
  3.1 3.6 %collective-permute-start = (f32[128,128]{1,0:T(8,128)S(1)}, f32[128,128]{1,0:T(8,128)S(1)}, u32[]{:S(2)}, u32[]{:S(2)}) collective-permute-start(f32[128,128]{1,0:T(8,128)S(1)} %get-tuple-element.29), channel_id=1, source_target_pairs={{0,8},{1,2},{2,1},{3,4},{4,3},{5,6},{6,5},{7,127},{8,0},{9,10},{10... | collective-permute-start | bytes 196616 | tf_op jit(solution)/shard_map/ppermute | solution.py:758
  4.6 3.5 %collective-permute-start.1 = (f32[128,128]{1,0:T(8,128)S(1)}, f32[128,128]{1,0:T(8,128)S(1)}, u32[]{:S(2)}, u32[]{:S(2)}) collective-permute-start(f32[128,128]{1,0:T(8,128)S(1)} %get-tuple-element.30), channel_id=1, source_target_pairs={{0,1},{1,0},{2,3},{3,2},{4,5},{5,4},{6,7},{7,6},{8,9},{9,8},{10,11... | collective-permute-start | bytes 196616 | tf_op jit(solution)/shard_map/ppermute | solution.py:758
  6.4 1.7 %copy-start.1 = (f32[64,128]{1,0:T(8,128)S(1)}, f32[64,128]{1,0:T(8,128)}, u32[]{:S(2)}) copy-start(f32[64,128]{1,0:T(8,128)} %diff.3) | copy-start | bytes 98308
  8.3 6.9 %collective-permute-start.4 = (f32[224,128]{1,0:T(8,128)S(1)}, f32[224,128]{1,0:T(8,128)S(1)}, u32[]{:S(2)}, u32[]{:S(2)}) collective-permute-start(f32[224,128]{1,0:T(8,128)S(1)} %get-tuple-element.34), channel_id=1, source_target_pairs={{0,120},{1,121},{2,122},{3,123},{4,124},{5,125},{6,126},{7,127},{8... | collective-permute-start | bytes 344072 | tf_op jit(solution)/shard_map/ppermute | solution.py:758
  11.7 4.4 %collective-permute-start.5 = (f32[224,128]{1,0:T(8,128)S(1)}, f32[224,128]{1,0:T(8,128)S(1)}, u32[]{:S(2)}, u32[]{:S(2)}) collective-permute-start(f32[224,128]{1,0:T(8,128)S(1)} %get-tuple-element.35), channel_id=1, source_target_pairs={{0,8},{1,9},{2,10},{3,11},{4,12},{5,13},{6,14},{7,15},{8,0},{9,1},... | collective-permute-start | bytes 344072 | tf_op jit(solution)/shard_map/ppermute | solution.py:758
  19.2 23.6 %all-to-all-start = ((f32[128,1,128]{2,1,0:T(1,128)}), f32[128,1,128]{2,1,0:T(1,128)S(1)}, u32[]{:S(2)}, u32[]{:S(2)}) async-start(f32[128,1,128]{2,1,0:T(1,128)} %bitcast.6), calls=%async_computation | async-start | bytes 131072 | tf_op jit(solution)/shard_map/all_to_all | solution.py:803
  33.3 3.0 %collective-permute-start.2 = (f32[24,128]{1,0:T(8,128)S(1)}, f32[24,128]{1,0:T(8,128)S(1)}, u32[]{:S(2)}, u32[]{:S(2)}) collective-permute-start(f32[24,128]{1,0:T(8,128)S(1)} %get-tuple-element.32), channel_id=1, source_target_pairs={{0,8},{1,2},{2,1},{3,4},{4,3},{5,6},{6,5},{7,127},{8,0},{9,10},{10... | collective-permute-start | bytes 36872 | tf_op jit(solution)/shard_map/ppermute | solution.py:758
  34.4 2.9 %collective-permute-start.3 = (f32[24,128]{1,0:T(8,128)S(1)}, f32[24,128]{1,0:T(8,128)S(1)}, u32[]{:S(2)}, u32[]{:S(2)}) collective-permute-start(f32[24,128]{1,0:T(8,128)S(1)} %get-tuple-element.33), channel_id=1, source_target_pairs={{0,1},{1,0},{2,3},{3,2},{4,5},{5,4},{6,7},{7,6},{8,9},{9,8},{10,11... | collective-permute-start | bytes 36872 | tf_op jit(solution)/shard_map/ppermute | solution.py:758
  35.9 1.4 %copy-start.2 = (s32[64,128]{1,0:T(8,128)S(1)}, s32[64,128]{1,0:T(8,128)}, u32[]{:S(2)}) copy-start(s32[64,128]{1,0:T(8,128)} %lev.3) | copy-start | bytes 98308
